TPU v7x, 512 devices: a whole 4x4x16 slice. The times are simulated.
512 devices in a mesh: seq: 64 (over x, z), track: 8 (over y, core).
Axes of the slice: x: 4, y: 4, z: 16, core: 2. Of those that a mesh axis runs over, the one named last changes fastest.
Arguments:
- embeddings: bfloat16 [768, 131072], P('track', 'seq'), may hold values from -1000 to 1000, as said below
- taps: bfloat16 [5, 768], P(None, 'track'), may hold values from -3 to 3
- head_weight: bfloat16 [768, 768], P('track'), may hold values from -0.21875 to 0.21875
- targets: float32 [768, 131072], P('track', 'seq'), may hold values from 0.04 to 15, as said below
Outputs:
- embed_grad: bfloat16 [768, 131072], P('track', 'seq')
- weight_grad: float32 [768, 768], P('track')
- taps_grad: float32 [5, 768], P(None, 'track')
Inputs may be any that keep to these rules, and one draw needn't show every extreme that they name: embeddings are real-valued. targets are positive counts.
All inputs are finite; a program needn't handle non-finite values.
Results may differ from a plain program's by a relative error of at most 0.02.
Values may be sent and summed in bfloat16 or wider, within the bound.
No kernel may reach another device: no remote copies, remote signals or barrier semaphores. Data moves between devices by JAX's collectives and lax.ppermute only.
A program may use at most 64 MiB of HBM per device.

v0:
```python
import jax
import jax.numpy as jnp
from jax import lax
from jax.sharding import PartitionSpec as P


def with_halo(cells, sides, width):
    for axis, dim in sides:
        count = lax.axis_size(axis)
        ends = count - 1
        head = lax.slice_in_dim(cells, 0, width, axis=dim)
        tail = lax.slice_in_dim(cells, cells.shape[dim] - width, cells.shape[dim], axis=dim)
        cells = jnp.concatenate(
            [
                lax.ppermute(tail, axis, [(i, (i + 1) % count) for i in range(ends)]),
                cells,
                lax.ppermute(head, axis, [((i + 1) % count, i) for i in range(ends)]),
            ],
            axis=dim,
        )
    return cells


def convolve(padded, tap_rows, count):
    result = jnp.zeros((padded.shape[0], count), jnp.float32)
    for k in range(tap_rows.shape[0]):
        result = result + tap_rows[k].astype(jnp.float32)[:, None] * padded[
            :, k : k + count
        ].astype(jnp.float32)
    return result


def shards(embeddings, taps, head_weight, targets):
    local_width = embeddings.shape[0]
    count = embeddings.shape[1]
    ntaps = taps.shape[0]
    width = ntaps // 2
    padded = with_halo(embeddings, (("seq", 1),), width)
    conv = convolve(padded, taps, count)
    hidden = lax.all_gather(jax.nn.silu(conv).astype(jnp.bfloat16), "track", axis=0, tiled=True)
    logits = jnp.dot(head_weight, hidden, preferred_element_type=jnp.float32)
    local_counts = jnp.sum(targets, axis=1)
    peak = lax.pmax(jnp.max(logits, axis=1), "seq")
    expo = jnp.exp(logits - peak[:, None])
    total, counts = lax.psum((jnp.sum(expo, axis=1), local_counts), "seq")
    logit_grad = (counts[:, None] * expo / total[:, None] - targets).astype(jnp.bfloat16)
    local_weight = lax.dot_general(
        logit_grad, hidden, (((1,), (1,)), ((), ())), preferred_element_type=jnp.float32
    )
    partial_grad = lax.dot_general(
        head_weight, logit_grad, (((0,), (0,)), ((), ())), preferred_element_type=jnp.float32
    )
    hidden_grad = lax.psum_scatter(
        partial_grad.astype(jnp.bfloat16), "track", scatter_dimension=0, tiled=True
    ).astype(jnp.float32)
    weight_grad = lax.psum(local_weight, "seq")
    sig = jax.nn.sigmoid(conv)
    conv_grad = (hidden_grad * sig * (1.0 + conv * (1.0 - sig))).astype(jnp.bfloat16)
    grad_pad = with_halo(conv_grad, (("seq", 1),), width)
    embed_grad = jnp.zeros((local_width, count), jnp.float32)
    for k in range(ntaps):
        embed_grad = embed_grad + taps[k].astype(jnp.float32)[:, None] * grad_pad[
            :, 2 * width - k : 2 * width - k + count
        ].astype(jnp.float32)
    grad_float = conv_grad.astype(jnp.float32)
    local_taps = jnp.stack(
        [
            jnp.sum(padded[:, k : k + count].astype(jnp.float32) * grad_float, axis=1)
            for k in range(ntaps)
        ]
    )
    taps_grad = lax.psum(local_taps, "seq")
    return (embed_grad.astype(jnp.bfloat16), weight_grad, taps_grad)


def solution(mesh):
    return jax.shard_map(
        shards,
        mesh=mesh,
        in_specs=(P("track", "seq"), P(None, "track"), P("track", None), P("track", "seq")),
        out_specs=(P("track", "seq"), P("track", None), P(None, "track")),
        check_vma=False,
    )
```

profile of v0, /device:TPU:6, one launch (start us, length us, event | category | flops | bytes accessed | tf_op | source)
XLA Modules:
  0.0 656.5 jit_solution(9263471499076404739)
XLA Ops:
  7.2 0.9 fusion.21
  8.1 3.8 collective-permute-start
  12.0 9.8 %collective-permute-start.1 = (bf16[96,2]{1,0:T(8,128)(2,1)S(1)}, bf16[96,2]{1,0:T(8,128)(2,1)S(1)}, u32[]{:S(2)}, u32[]{:S(2)}) collective-permute-start(bf16[96,2]{1,0:T(8,128)(2,1)S(1)} %get-tuple-element.22), channel_id=1, source_target_pairs={{8,0},{16,8},{24,16},{32,24},{40,32},{48,40},{56,48},{64,56},{72,6... | collective-permute-start | bytes 1160 | tf_op jit(solution)/shard_map/ppermute | solution.py:17
  21.7 1.0 constant_dynamic-update-slice_fusion.1
  22.8 0.9 bitcast_convert_fusion.4
  23.7 0.8 copy-done.2
  24.4 3.4 multiply_convert_fusion.1
  28.1 33.7 %all-gather.2.cloned.1.call-done = bf16[768,2048]{1,0:T(8,128)(2,1)} async-done(((bf16[96,2048]{1,0:T(8,128)(2,1)}), bf16[768,2048]{1,0:T(8,128)(2,1)}) %all-gather.2.cloned.1.call-update) | async-done | bytes 3145744 | tf_op jit(solution)/shard_map/all_gather | solution.py:40
  61.8 2.6 fusion.22
  64.4 122.9 %pmax.7 = f32[96]{0:T(128)S(1)} all-reduce(f32[96]{0:T(128)S(1)} %get-tuple-element.28), channel_id=1, replica_groups=mesh['seq'=64,'track'=8] {'seq'}, use_global_device_ids=true, to_apply=%region_3.4 | all-reduce | flops 96 | bytes 768 | tf_op jit(solution)/shard_map/pmax | solution.py:43
  187.6 134.8 %all-reduce = (f32[96]{0:T(128)S(1)}, f32[96]{0:T(128)S(1)}) all-reduce(f32[96]{0:T(128)S(1)} %fusion.15, f32[96]{0:T(128)S(1)} %reduce_sum.63), channel_id=1, replica_groups=mesh['seq'=64,'track'=8] {'seq'}, use_global_device_ids=true, to_apply=%region_5.6 | all-reduce | flops 192 | bytes 1536 | tf_op jit(solution)/shard_map/psum | solution.py:45
  322.7 0.7 copy-done.3
  323.4 1.0 fusion
  324.5 3.0 copy.14
  327.6 1.8 copy-done.1
  329.4 2.8 fusion.23
  332.2 52.0 %reduce-scatter.4.cloned.1.call-done = bf16[96,2048]{1,0:T(8,128)(2,1)} async-done(((bf16[768,2048]{1,0:T(8,128)(2,1)}), bf16[96,2048]{1,0:T(8,128)(2,1)}) %reduce-scatter.4.cloned.1.call-update) | async-done | bytes 393232 | tf_op jit(solution)/shard_map/reduce_scatter | solution.py:53
  384.2 3.5 fusion.13
  387.8 6.2 collective-permute-start.2
  394.0 1.9 collective-permute-start.3
  396.0 123.3 %psum.31 = f32[5,96]{1,0:T(8,128)} all-reduce(f32[5,96]{1,0:T(8,128)S(1)} %stack.23), channel_id=1, replica_groups=mesh['seq'=64,'track'=8] {'seq'}, use_global_device_ids=true, to_apply=%region_13.14 | all-reduce | flops 480 | bytes 3840 | tf_op jit(solution)/shard_map/psum | solution.py:72
  519.3 1.5 fusion.8
  520.9 127.4 %all-reduce.3.cloned.1.call-done = f32[96,768]{1,0:T(8,128)} async-done(((f32[96,768]{1,0:T(8,128)}), f32[96,768]{1,0:T(8,128)}) %all-reduce.3.cloned.1.call-update) | async-done | bytes 294928 | tf_op jit(solution)/shard_map/psum | solution.py:56
  648.3 1.7 copy.18
  (23 shorter events, 1.0 us)
Async XLA Ops:
  7.2 54.6 %copy-start = (bf16[96,768]{1,0:T(8,128)(2,1)S(1)}, bf16[96,768]{1,0:T(8,128)(2,1)}, u32[]{:S(2)}) copy-start(bf16[96,768]{1,0:T(8,128)(2,1)} %param.6) | copy-start | bytes 442372
  7.2 20.8 %copy-start.4 = (f32[96,2048]{1,0:T(8,128)S(1)}, f32[96,2048]{1,0:T(8,128)}, u32[]{:S(2)}) copy-start(f32[96,2048]{1,0:T(8,128)} %param.7) | copy-start | bytes 2359300
  7.2 54.6 %all-gather.2.cloned.1.call-start = ((), (), s32[]{:S(2)}) async-start(), calls=%async_computation.1 | async-start | bytes 3538944 | tf_op jit(solution)/shard_map/all_gather | solution.py:40
  8.1 15.5 %collective-permute-start = (bf16[96,2]{1,0:T(8,128)(2,1)S(1)}, bf16[96,2]{1,0:T(8,128)(2,1)S(1)}, u32[]{:S(2)}, u32[]{:S(2)}) collective-permute-start(bf16[96,2]{1,0:T(8,128)(2,1)S(1)} %get-tuple-element.21), channel_id=1, source_target_pairs={{0,8},{8,16},{16,24},{24,32},{32,40},{40,48},{48,56},{56,64},{64,7... | collective-permute-start | bytes 1160 | tf_op jit(solution)/shard_map/ppermute | solution.py:15
  12.0 11.7 %collective-permute-start.1 = (bf16[96,2]{1,0:T(8,128)(2,1)S(1)}, bf16[96,2]{1,0:T(8,128)(2,1)S(1)}, u32[]{:S(2)}, u32[]{:S(2)}) collective-permute-start(bf16[96,2]{1,0:T(8,128)(2,1)S(1)} %get-tuple-element.22), channel_id=1, source_target_pairs={{8,0},{16,8},{24,16},{32,24},{40,32},{48,40},{56,48},{64,56},{72,6... | collective-permute-start | bytes 1160 | tf_op jit(solution)/shard_map/ppermute | solution.py:17
  23.7 0.8 copy-start.2
  27.9 356.3 %reduce-scatter.4.cloned.1.call-start = ((), (), s32[]{:S(2)}) async-start(), calls=%async_computation.3 | async-start | bytes 3538944 | tf_op jit(solution)/shard_map/reduce_scatter | solution.py:53
  322.7 0.7 copy-start.3
  327.5 1.9 copy-start.1
  327.5 320.8 %all-reduce.3.cloned.1.call-start = ((), (), s32[]{:S(2)}) async-start(), calls=%async_computation.2 | async-start | bytes 589824 | tf_op jit(solution)/shard_map/psum | solution.py:56
  387.8 131.5 %collective-permute-start.2 = (bf16[96,2]{1,0:T(8,128)(2,1)S(1)}, bf16[96,2]{1,0:T(8,128)(2,1)S(1)}, u32[]{:S(2)}, u32[]{:S(2)}) collective-permute-start(bf16[96,2]{1,0:T(8,128)(2,1)S(1)} %get-tuple-element.19), channel_id=1, source_target_pairs={{8,0},{16,8},{24,16},{32,24},{40,32},{48,40},{56,48},{64,56},{72,6... | collective-permute-start | bytes 1160 | tf_op jit(solution)/shard_map/ppermute | solution.py:17
  394.0 125.3 %collective-permute-start.3 = (bf16[96,2]{1,0:T(8,128)(2,1)S(1)}, bf16[96,2]{1,0:T(8,128)(2,1)S(1)}, u32[]{:S(2)}, u32[]{:S(2)}) collective-permute-start(bf16[96,2]{1,0:T(8,128)(2,1)S(1)} %get-tuple-element.20), channel_id=1, source_target_pairs={{0,8},{8,16},{16,24},{24,32},{32,40},{40,48},{48,56},{56,64},{64,7... | collective-permute-start | bytes 1160 | tf_op jit(solution)/shard_map/ppermute | solution.py:15
Sparse Core Ops, SparseCore 0:
  28.0 33.7 all-gather.1
  327.6 56.5 reduce-scatter.3
  388.2 259.9 all-reduce.2
where the time goes:
time: 659 us; the launch traced here: 657 us
  blocking collectives  381 us (58%)
  waiting for transfers between devices  213 us (32%)
  starting transfers between devices  21.8 us (3%)
  between operations  13.9 us (2%)
  local copies, waits for them, and re-layouts  10.1 us (2%)
  other arithmetic  10.1 us (2%)
    psum x1, blocking collectives, shards(): total, counts = lax.psum((jnp.sum(expo, axis=1), local_counts), 'seq')  135 us
    psum x1, waiting for transfers between devices, shards(): weight_grad = lax.psum(local_weight, 'seq')  127 us
    psum x1, blocking collectives, shards(): taps_grad = lax.psum(local_taps, 'seq')  123 us
    pmax x1, blocking collectives, shards(): peak = lax.pmax(jnp.max(logits, axis=1), 'seq')  123 us
    reduce_scatter x1, waiting for transfers between devices, shards(): lax.psum_scatter(partial_grad.astype(jnp.bfloat16), 'track', scatter_dime...  52 us
    all_gather x1, waiting for transfers between devices, shards(): lax.all_gather(jax.nn.silu(conv).astype(jnp.bfloat16), 'track', axis=0, t...  33.7 us
    ppermute x2, starting transfers between devices, with_halo(): lax.ppermute(head, axis, [((i + 1) % count, i) for i in range(ends)])  16 us
  transfers between devices with their start and end apart: 7, of which 3 were waited for; matrix products, arithmetic and copies ran while one was open for 2% of the time, Pallas kernels for 0%

commit v1 on v0

v1 whole, which is shorter than its diff:
```python
import jax
import jax.numpy as jnp
import numpy as np
from jax import lax
from jax.sharding import Mesh
from jax.sharding import PartitionSpec as P

F32 = jnp.float32
BF16 = jnp.bfloat16
SEQ = ("x", "z")


def ring(count, shift):
    return [(i, (i + shift) % count) for i in range(count)]


def along_y(value, shift):
    return lax.ppermute(value, "y", ring(lax.axis_size("y"), shift))


def other_core(value):
    return lax.ppermute(value, "c", [(0, 1), (1, 0)])


def halo(cells, width):
    count = lax.axis_size(SEQ)
    head = cells[:, :width]
    tail = cells[:, -width:]
    left = lax.ppermute(tail, SEQ, [(i, i + 1) for i in range(count - 1)])
    right = lax.ppermute(head, SEQ, [(i + 1, i) for i in range(count - 1)])
    return jnp.concatenate([left, cells, right], axis=1)


def exchange(value, axes):
    count = lax.axis_size(axes)
    copies = jnp.broadcast_to(value[None], (count,) + value.shape)
    return lax.all_to_all(copies, axes, 0, 0, tiled=True)


def gather_track(block):
    half = block.shape[0] // 2
    above = along_y(block, -1)
    below = along_y(block, 1)
    far_low = along_y(below[:half], 1)
    far_high = along_y(above[half:], -1)
    mine = jnp.concatenate([block, above, far_low, far_high, below], axis=0)
    theirs = [other_core(part) for part in (block, above, below)]
    far = other_core(jnp.concatenate([far_low, far_high], axis=0))
    return jnp.concatenate([mine, theirs[0], theirs[1], far, theirs[2]], axis=0)


def scatter_track(kept, sent):
    width = kept.shape[0] // 4
    half = width // 2
    both = (kept.astype(F32) + other_core(sent).astype(F32)).reshape(4, width, -1)
    narrow = both.astype(BF16)
    low = along_y(narrow[2, :half], 1)
    high = along_y(narrow[2, half:], -1)
    up = jnp.concatenate(
        [(both[1, :half] + low.astype(F32)).astype(BF16), narrow[1, half:]], axis=0
    )
    down = jnp.concatenate(
        [narrow[3, :half], (both[3, half:] + high.astype(F32)).astype(BF16)], axis=0
    )
    from_below = along_y(up, 1)
    from_above = along_y(down, -1)
    return both[0] + from_below.astype(F32) + from_above.astype(F32)


def shards(embeddings, taps, head_weight, targets):
    width = embeddings.shape[0]
    count = embeddings.shape[1]
    tracks = head_weight.shape[0]
    ntaps = taps.shape[0]
    reach = ntaps // 2
    y = lax.axis_index("y")
    c = lax.axis_index("c")
    ny = lax.axis_size("y")
    tap = taps.astype(F32)

    blocks = head_weight.reshape(tracks, ny, 2, width)
    twice = jnp.concatenate([blocks, blocks], axis=1)
    turned = lax.dynamic_slice_in_dim(twice, y, ny, axis=1)
    first = jnp.where(c == 0, turned[:, :, 0], turned[:, :, 1]).reshape(tracks, ny * width)
    second = jnp.where(c == 0, turned[:, :, 1], turned[:, :, 0]).reshape(tracks, ny * width)

    padded = halo(embeddings, reach).astype(F32)
    conv = jnp.zeros((width, count), F32)
    for k in range(ntaps):
        conv = conv + tap[k][:, None] * padded[:, k : k + count]
    hidden = gather_track(jax.nn.silu(conv).astype(BF16))

    logits = jnp.dot(
        jnp.concatenate([first, second], axis=1), hidden, preferred_element_type=F32
    )
    top = jnp.max(logits, axis=1)
    expo = jnp.exp(logits - top[:, None])
    stats = jnp.stack([top, jnp.sum(expo, axis=1), jnp.sum(targets, axis=1)])
    every = exchange(stats, SEQ)
    peak = jnp.max(every[:, 0], axis=0)
    total = jnp.sum(every[:, 1] * jnp.exp(every[:, 0] - peak[None]), axis=0)
    counts = jnp.sum(every[:, 2], axis=0)
    scale = counts * jnp.exp(top - peak) / total
    logit_grad = (scale[:, None] * expo - targets).astype(BF16)

    turn = (((0,), (0,)), ((), ()))
    sent = lax.dot_general(second, logit_grad, turn, preferred_element_type=F32).astype(BF16)
    kept = lax.dot_general(first, logit_grad, turn, preferred_element_type=F32).astype(BF16)
    hidden_grad = scatter_track(kept, sent)

    local = lax.dot_general(
        hidden, logit_grad, (((1,), (1,)), ((), ())), preferred_element_type=F32
    ).reshape(2, ny, width, tracks)
    local = jnp.where(c == 0, local, local[::-1])
    local = lax.dynamic_slice_in_dim(
        jnp.concatenate([local, local], axis=1), (ny - y) % ny, ny, axis=1
    )
    local = local.transpose(1, 0, 2, 3).reshape(2 * ny * width, tracks)
    nx, nz = lax.axis_size("x"), lax.axis_size("z")
    part = local.reshape(nx, -1, tracks)
    part = jnp.sum(lax.all_to_all(part, "x", 0, 0, tiled=True), axis=0)
    part = part.reshape(nz, -1, tracks)
    part = jnp.sum(lax.all_to_all(part, "z", 0, 0, tiled=True), axis=0)

    sig = jax.nn.sigmoid(conv)
    conv_grad = (hidden_grad * sig * (1.0 + conv * (1.0 - sig))).astype(BF16)
    grad_float = conv_grad.astype(F32)
    local_taps = jnp.stack(
        [jnp.sum(padded[:, k : k + count] * grad_float, axis=1) for k in range(ntaps)]
    )
    slab = exchange(jnp.concatenate([part, local_taps], axis=0), "z")
    rows = part.shape[0]
    taps_z = jnp.sum(slab[:, rows:], axis=0)
    slab = exchange(
        jnp.concatenate([slab[:, :rows].reshape(-1, tracks), taps_z], axis=0), "x"
    )
    rows = rows * nz
    weight_grad = slab[:, :rows].reshape(-1, tracks).T
    taps_grad = jnp.sum(slab[:, rows:], axis=0)

    grad_pad = halo(conv_grad, reach).astype(F32)
    embed_grad = jnp.zeros((width, count), F32)
    for k in range(ntaps):
        start = 2 * reach - k
        embed_grad = embed_grad + tap[k][:, None] * grad_pad[:, start : start + count]
    return embed_grad.astype(BF16), weight_grad, taps_grad


def solution(mesh):
    fine = Mesh(np.asarray(mesh.devices).reshape(4, 16, 4, 2), ("x", "z", "y", "c"))
    track = ("y", "c")
    return jax.shard_map(
        shards,
        mesh=fine,
        in_specs=(P(track, SEQ), P(None, track), P(track, None), P(track, SEQ)),
        out_specs=(P(track, SEQ), P(track, None), P(None, track)),
        check_vma=False,
    )
```

time: 659 us -> 172 us (0.26)
  blocking collectives: 381 us -> 45.9 us
  waiting for transfers between devices: 213 us -> 14.9 us
  starting transfers between devices: 21.8 us -> 73 us
  between operations: 13.9 us -> 1.16 us
    psum x2 -> x0, blocking collectives: 258 us -> none  [the longest x1 135 us: shards(): total, counts = lax.psum((jnp.sum(expo, axis=1), local_counts), 'seq')]
    psum x1 -> x0, waiting for transfers between devices: 127 us -> none  [shards(): weight_grad = lax.psum(local_weight, 'seq')]
    pmax x1 -> x0, blocking collectives: 123 us -> none  [shards(): peak = lax.pmax(jnp.max(logits, axis=1), 'seq')]
    reduce_scatter x1 -> x0, waiting for transfers between devices: 52 us -> none  [shards(): lax.psum_scatter(partial_grad.astype(jnp.bfloat16), 'track', scatter_dime...]
    all_to_all x0 -> x2, blocking collectives: none -> 45.9 us  [the longest x1 28.4 us: exchange(): return lax.all_to_all(copies, axes, 0, 0, tiled=True)]
    ppermute x4 -> x17, starting transfers between devices: 21.7 us -> 59.9 us  [the longest x8 28.3 us: along_y(): return lax.ppermute(value, 'y', ring(lax.axis_size('y'), shift))]
    all_gather x1 -> x0, waiting for transfers between devices: 33.7 us -> none  [shards(): lax.all_gather(jax.nn.silu(conv).astype(jnp.bfloat16), 'track', axis=0, t...]
    all_to_all x0 -> x3, starting transfers between devices: none -> 13.1 us  [the longest x2 8.39 us: exchange(): return lax.all_to_all(copies, axes, 0, 0, tiled=True)]
  transfers between devices with their start and end apart: 7 -> 20, of which waited for: 3 -> 6; matrix products, arithmetic and copies ran while one was open for 2% -> 9% of each run, Pallas kernels for 0% -> 0%
where the time goes in v1:
time: 172 us; the launch traced here: 171 us
  starting transfers between devices  73 us (42%)
  blocking collectives  45.9 us (27%)
  waiting for transfers between devices  14.9 us (9%)
  local copies, waits for them, and re-layouts  14.8 us (9%)
  other arithmetic  11.4 us (7%)
  matrix products  9.36 us (5%)
    all_to_all x1, blocking collectives, exchange(): return lax.all_to_all(copies, axes, 0, 0, tiled=True)  28.4 us
    ppermute x8, starting transfers between devices, along_y(): return lax.ppermute(value, 'y', ring(lax.axis_size('y'), shift))  28.3 us
    all_to_all x1, blocking collectives, shards(): part = jnp.sum(lax.all_to_all(part, 'z', 0, 0, tiled=True), axis=0)  17.5 us
    ppermute x2, starting transfers between devices, halo(): right = lax.ppermute(head, SEQ, [(i + 1, i) for i in range(count - 1)])  13.9 us
    ppermute x5, starting transfers between devices, other_core(): return lax.ppermute(value, 'c', [(0, 1), (1, 0)])  10.1 us
    all_to_all x2, waiting for transfers between devices, exchange(): return lax.all_to_all(copies, axes, 0, 0, tiled=True)  8.96 us
    all_to_all x2, starting transfers between devices, exchange(): return lax.all_to_all(copies, axes, 0, 0, tiled=True)  8.39 us
    ppermute x2, starting transfers between devices, halo(): left = lax.ppermute(tail, SEQ, [(i, i + 1) for i in range(count - 1)])  7.64 us
  transfers between devices with their start and end apart: 20, of which 6 were waited for; matrix products, arithmetic and copies ran while one was open for 9% of the time, Pallas kernels for 0%

profile of v1, /device:TPU:6, one launch (start us, length us, event | category | flops | bytes accessed | tf_op | source)
XLA Modules:
  0.0 170.5 jit_solution(9734152679699527068)
XLA Ops:
  1.5 3.8 %collective-permute-start = (bf16[96,2]{1,0:T(8,128)(2,1)S(1)}, bf16[96,2]{1,0:T(8,128)(2,1)S(1)}, u32[]{:S(2)}, u32[]{:S(2)}) collective-permute-start(bf16[96,2]{1,0:T(8,128)(2,1)S(1)} %get-tuple-element.33), channel_id=1, source_target_pairs={{0,8},{8,16},{16,24},{24,32},{32,40},{40,48},{48,56},{56,64},{64,7... | collective-permute-start | bytes 1160 | tf_op jit(solution)/shard_map/ppermute | solution.py:29
  5.3 9.8 %collective-permute-start.1 = (bf16[96,2]{1,0:T(8,128)(2,1)S(1)}, bf16[96,2]{1,0:T(8,128)(2,1)S(1)}, u32[]{:S(2)}, u32[]{:S(2)}) collective-permute-start(bf16[96,2]{1,0:T(8,128)(2,1)S(1)} %get-tuple-element.32), channel_id=1, source_target_pairs={{8,0},{16,8},{24,16},{32,24},{40,32},{48,40},{56,48},{64,56},{72,6... | collective-permute-start | bytes 1160 | tf_op jit(solution)/shard_map/ppermute | solution.py:30
  18.0 2.0 %constant_dynamic-update-slice_fusion.8 = (bf16[768,2048]{1,0:T(8,128)(2,1)}, bf16[96,2048]{1,0:T(8,128)(2,1)S(1)}, f32[96,2048]{1,0:T(8,128)}) fusion(f32[96,2052]{1,0:T(8,128)S(1)} %convert_element_type.58, f32[96]{0:T(128)S(1)} %get-tuple-element.40, f32[96]{0:T(128)S(1)} %get-tuple-element.41, f32[96]{0:T(128)S(1)} %get-tuple-element.42, ...), kind=kLoop, calls=%fused_computation.72 | loop fusion | flops 2752511 | bytes 5506944
  20.0 3.5 %collective-permute-start.3 = (bf16[96,2048]{1,0:T(8,128)(2,1)S(1)}, bf16[96,2048]{1,0:T(8,128)(2,1)S(1)}, u32[]{:S(2)}, u32[]{:S(2)}) collective-permute-start(bf16[96,2048]{1,0:T(8,128)(2,1)S(1)} %get-tuple-element.22), channel_id=1, source_target_pairs={{0,2},{2,4},{4,6},{6,0},{1,3},{3,5},{5,7},{7,1},{8,10},{10,12},{12... | collective-permute-start | bytes 1179656 | tf_op jit(solution)/shard_map/ppermute | solution.py:18
  23.5 3.6 %collective-permute-start.2 = (bf16[96,2048]{1,0:T(8,128)(2,1)S(1)}, bf16[96,2048]{1,0:T(8,128)(2,1)S(1)}, u32[]{:S(2)}, u32[]{:S(2)}) collective-permute-start(bf16[96,2048]{1,0:T(8,128)(2,1)S(1)} %get-tuple-element.22), channel_id=1, source_target_pairs={{0,6},{2,0},{4,2},{6,4},{1,7},{3,1},{5,3},{7,5},{8,14},{10,8},{12,... | collective-permute-start | bytes 1179656 | tf_op jit(solution)/shard_map/ppermute | solution.py:18
  30.2 2.9 %collective-permute-done.3 = bf16[96,2048]{1,0:T(8,128)(2,1)S(1)} collective-permute-done((bf16[96,2048]{1,0:T(8,128)(2,1)S(1)}, bf16[96,2048]{1,0:T(8,128)(2,1)S(1)}, u32[]{:S(2)}, u32[]{:S(2)}) %collective-permute-start.3) | collective-permute-done | bytes 393248 | tf_op jit(solution)/shard_map/ppermute | solution.py:18
  33.2 2.2 %collective-permute-start.4 = (bf16[48,2048]{1,0:T(8,128)(2,1)S(1)}, bf16[48,2048]{1,0:T(8,128)(2,1)S(1)}, u32[]{:S(2)}, u32[]{:S(2)}) collective-permute-start(bf16[48,2048]{1,0:T(8,128)(2,1)S(1)} %slice.169), channel_id=1, source_target_pairs={{0,2},{2,4},{4,6},{6,0},{1,3},{3,5},{5,7},{7,1},{8,10},{10,12},{12... | collective-permute-start | bytes 589832 | tf_op jit(solution)/shard_map/ppermute | solution.py:18
  35.4 4.8 %collective-permute-start.5 = (bf16[48,2048]{1,0:T(8,128)(2,1)S(1)}, bf16[48,2048]{1,0:T(8,128)(2,1)S(1)}, u32[]{:S(2)}, u32[]{:S(2)}) collective-permute-start(bf16[48,2048]{1,0:T(8,128)(2,1)S(1)} %slice.170), channel_id=1, source_target_pairs={{0,6},{2,0},{4,2},{6,4},{1,7},{3,1},{5,3},{7,5},{8,14},{10,8},{12,... | collective-permute-start | bytes 589832 | tf_op jit(solution)/shard_map/ppermute | solution.py:18
  42.2 2.4 %collective-permute-start.9 = (bf16[96,2048]{1,0:T(8,128)(2,1)S(1)}, bf16[96,2048]{1,0:T(8,128)(2,1)S(1)}, u32[]{:S(2)}, u32[]{:S(2)}) collective-permute-start(bf16[96,2048]{1,0:T(8,128)(2,1)S(1)} %collective-permute-done.3), channel_id=1, source_target_pairs={{0,1},{1,0},{2,3},{3,2},{4,5},{5,4},{6,7},{7,6},{8,9},{9,8},{10,11... | collective-permute-start | bytes 1179656 | tf_op jit(solution)/shard_map/ppermute | solution.py:22
  52.7 2.6 %fusion.30 = (f32[96]{0:T(128)S(1)}, f32[96,2048]{1,0:T(8,128)S(1)}) fusion(bf16[768,2048]{1,0:T(8,128)(2,1)} %constant_dynamic-update-slice_fusion, bf16[96,384]{1,0:T(8,128)(2,1)S(1)} %select_n.46, bf16[96,384]{1,0:T(8,128)(2,1)S(1)} %select_n.44), kind=kOutput, calls=%fused_computation.84 | convolution fusion | flops 302481312 | bytes 4080000 | tf_op jit(solution)/shard_map/dot_general | solution.py:93
  55.6 28.4 %all_to_all.25 = f32[64,3,96]{2,1,0:T(4,128)S(1)} all-to-all(f32[64,3,96]{2,1,0:T(4,128)S(1)} %broadcast_in_dim.6), channel_id=1, replica_groups=mesh['x'=4,'z'=16,'y'=4,'c'=2] {'x','z'}, dimensions={0} | all-to-all | bytes 147456 | tf_op jit(solution)/shard_map/all_to_all | solution.py:37
  88.2 3.0 %fusion.31 = f32[768,96]{0,1:T(8,128)S(1)} fusion(bf16[768,2048]{1,0:T(8,128)(2,1)} %constant_dynamic-update-slice_fusion, bf16[96,2048]{1,0:T(8,128)(2,1)S(1)} %subtract_convert_fusion), kind=kOutput, calls=%fused_computation.85 | convolution fusion | flops 301989888 | bytes 3833856 | tf_op jit(solution)/shard_map/dot_general | solution.py:111
  91.9 2.0 %convert_add_fusion = f32[384,2048]{1,0:T(8,128)S(1)} fusion(bf16[384,2048]{1,0:T(8,128)(2,1)} %collective-permute-done.10, bf16[96,384]{1,0:T(8,128)(2,1)S(1)} %select_n.44, bf16[96,2048]{1,0:T(8,128)(2,1)S(1)} %subtract_convert_fusion), kind=kOutput, calls=%fused_computation | convolution fusion | flops 154140672 | bytes 5185536 | tf_op jit(solution)/shard_map/dot_general | solution.py:108
  97.5 5.3 %collective-permute-start.13 = (bf16[48,2048]{1,0:T(8,128)(2,1)S(1)}, bf16[48,2048]{1,0:T(8,128)(2,1)}, u32[]{:S(2)}, u32[]{:S(2)}) collective-permute-start(bf16[48,2048]{1,0:T(8,128)(2,1)S(1)} %get-tuple-element.27), channel_id=1, source_target_pairs={{0,6},{2,0},{4,2},{6,4},{1,7},{3,1},{5,3},{7,5},{8,14},{10,8},{12,... | collective-permute-start | bytes 589832 | tf_op jit(solution)/shard_map/ppermute | solution.py:18
  103.6 4.7 %all-to-all-start.1 = ((f32[4,192,96]{2,1,0:T(8,128)}), f32[4,192,96]{2,1,0:T(8,128)S(1)}, u32[]{:S(2)}, u32[]{:S(2)}) async-start(f32[4,192,96]{2,1,0:T(8,128)} %bitcast.19), calls=%async_computation.1 | async-start | bytes 786432 | tf_op jit(solution)/shard_map/all_to_all | solution.py:121
  112.3 5.1 %collective-permute-start.14 = (bf16[96,2048]{1,0:T(8,128)(2,1)}, bf16[96,2048]{1,0:T(8,128)(2,1)S(1)}, u32[]{:S(2)}, u32[]{:S(2)}) collective-permute-start(bf16[96,2048]{1,0:T(8,128)(2,1)} %pad_maximum_fusion.2), channel_id=1, source_target_pairs={{0,6},{2,0},{4,2},{6,4},{1,7},{3,1},{5,3},{7,5},{8,14},{10,8},{12,... | collective-permute-start | bytes 1179656 | tf_op jit(solution)/shard_map/ppermute | solution.py:18
  117.5 17.5 %all_to_all.26 = f32[16,12,96]{2,1,0:T(8,128)S(1)} all-to-all(f32[16,12,96]{2,1,0:T(8,128)S(1)} %reshape.61), channel_id=1, replica_groups=mesh['x'=4,'z'=16,'y'=4,'c'=2] {'z'}, dimensions={0} | all-to-all | bytes 147456 | tf_op jit(solution)/shard_map/all_to_all | solution.py:123
  135.0 2.2 %fusion.4 = (f32[96]{0:T(128)S(1)}, f32[96]{0:T(128)S(1)}, f32[96]{0:T(128)S(1)}, f32[96]{0:T(128)S(1)}, f32[96]{0:T(128)S(1)}, /*index=5*/bf16[96,2048]{1,0:T(8,128)(2,1)S(1)}) fusion(f32[96,2052]{1,0:T(8,128)S(1)} %convert_element_type.58, f32[96,2048]{1,0:T(8,128)S(1)} %copy-done.2, bf16[96,2048]{1,0:T(8,128)(2,1)S(1)} %collective-permute-done.14, ...), kind=kLoop, calls=%fused_computation.12 | loop fusion | flops 4718112 | bytes 6686592 | tf_op jit(solution)/shard_map/reduce_sum | solution.py:129
  138.0 3.6 %all-to-all-start.3 = ((f32[16,17,96]{2,1,0:T(8,128)}), f32[16,17,96]{2,1,0:T(8,128)S(1)}, u32[]{:S(2)}, u32[]{:S(2)}) async-start(f32[16,17,96]{2,1,0:T(8,128)} %broadcast_in_dim.7), calls=%async_computation.3 | async-start | bytes 393216 | tf_op jit(solution)/shard_map/all_to_all | solution.py:37
  141.7 3.8 %collective-permute-start.15 = (bf16[96,2]{1,0:T(8,128)(2,1)S(1)}, bf16[96,2]{1,0:T(8,128)(2,1)S(1)}, u32[]{:S(2)}, u32[]{:S(2)}) collective-permute-start(bf16[96,2]{1,0:T(8,128)(2,1)S(1)} %get-tuple-element.31), channel_id=1, source_target_pairs={{0,8},{8,16},{16,24},{24,32},{32,40},{40,48},{48,56},{56,64},{64,7... | collective-permute-start | bytes 1160 | tf_op jit(solution)/shard_map/ppermute | solution.py:29
  145.5 4.1 %collective-permute-start.16 = (bf16[96,2]{1,0:T(8,128)(2,1)S(1)}, bf16[96,2]{1,0:T(8,128)(2,1)S(1)}, u32[]{:S(2)}, u32[]{:S(2)}) collective-permute-start(bf16[96,2]{1,0:T(8,128)(2,1)S(1)} %get-tuple-element.30), channel_id=1, source_target_pairs={{8,0},{16,8},{24,16},{32,24},{40,32},{48,40},{56,48},{64,56},{72,6... | collective-permute-start | bytes 1160 | tf_op jit(solution)/shard_map/ppermute | solution.py:30
  152.1 5.4 %all-to-all-done.3 = f32[16,17,96]{2,1,0:T(8,128)S(1)} async-done(((f32[16,17,96]{2,1,0:T(8,128)}), f32[16,17,96]{2,1,0:T(8,128)S(1)}, u32[]{:S(2)}, u32[]{:S(2)}) %all-to-all-start.3) | async-done | bytes 104480 | tf_op jit(solution)/shard_map/all_to_all | solution.py:37
  158.4 4.8 %all-to-all-start.4 = ((f32[4,197,96]{1,2,0:T(8,128)}), f32[4,197,96]{1,2,0:T(8,128)S(1)}, u32[]{:S(2)}, u32[]{:S(2)}) async-start(f32[4,197,96]{1,2,0:T(8,128)} %broadcast_in_dim.8), calls=%async_computation.4 | async-start | bytes 786432 | tf_op jit(solution)/shard_map/all_to_all | solution.py:37
  164.9 3.6 %all-to-all-done.4 = f32[4,197,96]{1,2,0:T(8,128)S(1)} async-done(((f32[4,197,96]{1,2,0:T(8,128)}), f32[4,197,96]{1,2,0:T(8,128)S(1)}, u32[]{:S(2)}, u32[]{:S(2)}) %all-to-all-start.4) | async-done | bytes 302624 | tf_op jit(solution)/shard_map/all_to_all | solution.py:37
  (92 shorter events, 38.2 us)
Async XLA Ops:
  1.5 14.3 %collective-permute-start = (bf16[96,2]{1,0:T(8,128)(2,1)S(1)}, bf16[96,2]{1,0:T(8,128)(2,1)S(1)}, u32[]{:S(2)}, u32[]{:S(2)}) collective-permute-start(bf16[96,2]{1,0:T(8,128)(2,1)S(1)} %get-tuple-element.33), channel_id=1, source_target_pairs={{0,8},{8,16},{16,24},{24,32},{32,40},{40,48},{48,56},{56,64},{64,7... | collective-permute-start | bytes 1160 | tf_op jit(solution)/shard_map/ppermute | solution.py:29
  5.3 11.3 %collective-permute-start.1 = (bf16[96,2]{1,0:T(8,128)(2,1)S(1)}, bf16[96,2]{1,0:T(8,128)(2,1)S(1)}, u32[]{:S(2)}, u32[]{:S(2)}) collective-permute-start(bf16[96,2]{1,0:T(8,128)(2,1)S(1)} %get-tuple-element.32), channel_id=1, source_target_pairs={{8,0},{16,8},{24,16},{32,24},{40,32},{48,40},{56,48},{64,56},{72,6... | collective-permute-start | bytes 1160 | tf_op jit(solution)/shard_map/ppermute | solution.py:30
  17.9 9.1 %copy-start.3 = (bf16[96,768]{1,0:T(8,128)(2,1)S(1)}, bf16[96,768]{1,0:T(8,128)(2,1)}, u32[]{:S(2)}) copy-start(bf16[96,768]{1,0:T(8,128)(2,1)} %param.6) | copy-start | bytes 442372
  18.0 10.2 %copy-start.1 = (f32[96,2048]{1,0:T(8,128)S(1)}, f32[96,2048]{1,0:T(8,128)}, u32[]{:S(2)}) copy-start(f32[96,2048]{1,0:T(8,128)} %param.7) | copy-start | bytes 2359300
  20.0 13.2 %collective-permute-start.3 = (bf16[96,2048]{1,0:T(8,128)(2,1)S(1)}, bf16[96,2048]{1,0:T(8,128)(2,1)S(1)}, u32[]{:S(2)}, u32[]{:S(2)}) collective-permute-start(bf16[96,2048]{1,0:T(8,128)(2,1)S(1)} %get-tuple-element.22), channel_id=1, source_target_pairs={{0,2},{2,4},{4,6},{6,0},{1,3},{3,5},{5,7},{7,1},{8,10},{10,12},{12... | collective-permute-start | bytes 1179656 | tf_op jit(solution)/shard_map/ppermute | solution.py:18
  23.5 11.9 %collective-permute-start.2 = (bf16[96,2048]{1,0:T(8,128)(2,1)S(1)}, bf16[96,2048]{1,0:T(8,128)(2,1)S(1)}, u32[]{:S(2)}, u32[]{:S(2)}) collective-permute-start(bf16[96,2048]{1,0:T(8,128)(2,1)S(1)} %get-tuple-element.22), channel_id=1, source_target_pairs={{0,6},{2,0},{4,2},{6,4},{1,7},{3,1},{5,3},{7,5},{8,14},{10,8},{12,... | collective-permute-start | bytes 1179656 | tf_op jit(solution)/shard_map/ppermute | solution.py:18
  28.3 21.2 %collective-permute-start.6 = (bf16[96,2048]{1,0:T(8,128)(2,1)S(1)}, bf16[96,2048]{1,0:T(8,128)(2,1)S(1)}, u32[]{:S(2)}, u32[]{:S(2)}) collective-permute-start(bf16[96,2048]{1,0:T(8,128)(2,1)S(1)} %get-tuple-element.22), channel_id=1, source_target_pairs={{0,1},{1,0},{2,3},{3,2},{4,5},{5,4},{6,7},{7,6},{8,9},{9,8},{10,11... | collective-permute-start | bytes 1179656 | tf_op jit(solution)/shard_map/ppermute | solution.py:22
  33.2 12.2 %collective-permute-start.4 = (bf16[48,2048]{1,0:T(8,128)(2,1)S(1)}, bf16[48,2048]{1,0:T(8,128)(2,1)S(1)}, u32[]{:S(2)}, u32[]{:S(2)}) collective-permute-start(bf16[48,2048]{1,0:T(8,128)(2,1)S(1)} %slice.169), channel_id=1, source_target_pairs={{0,2},{2,4},{4,6},{6,0},{1,3},{3,5},{5,7},{7,1},{8,10},{10,12},{12... | collective-permute-start | bytes 589832 | tf_op jit(solution)/shard_map/ppermute | solution.py:18
  35.4 10.0 %collective-permute-start.5 = (bf16[48,2048]{1,0:T(8,128)(2,1)S(1)}, bf16[48,2048]{1,0:T(8,128)(2,1)S(1)}, u32[]{:S(2)}, u32[]{:S(2)}) collective-permute-start(bf16[48,2048]{1,0:T(8,128)(2,1)S(1)} %slice.170), channel_id=1, source_target_pairs={{0,6},{2,0},{4,2},{6,4},{1,7},{3,1},{5,3},{7,5},{8,14},{10,8},{12,... | collective-permute-start | bytes 589832 | tf_op jit(solution)/shard_map/ppermute | solution.py:18
  40.3 10.0 %collective-permute-start.7 = (bf16[96,2048]{1,0:T(8,128)(2,1)S(1)}, bf16[96,2048]{1,0:T(8,128)(2,1)S(1)}, u32[]{:S(2)}, u32[]{:S(2)}) collective-permute-start(bf16[96,2048]{1,0:T(8,128)(2,1)S(1)} %collective-permute-done.2), channel_id=1, source_target_pairs={{0,1},{1,0},{2,3},{3,2},{4,5},{5,4},{6,7},{7,6},{8,9},{9,8},{10,11... | collective-permute-start | bytes 1179656 | tf_op jit(solution)/shard_map/ppermute | solution.py:22
  42.2 9.7 %collective-permute-start.9 = (bf16[96,2048]{1,0:T(8,128)(2,1)S(1)}, bf16[96,2048]{1,0:T(8,128)(2,1)S(1)}, u32[]{:S(2)}, u32[]{:S(2)}) collective-permute-start(bf16[96,2048]{1,0:T(8,128)(2,1)S(1)} %collective-permute-done.3), channel_id=1, source_target_pairs={{0,1},{1,0},{2,3},{3,2},{4,5},{5,4},{6,7},{7,6},{8,9},{9,8},{10,11... | collective-permute-start | bytes 1179656 | tf_op jit(solution)/shard_map/ppermute | solution.py:22
  45.4 5.7 %collective-permute-start.8 = (bf16[96,2048]{1,0:T(8,128)(2,1)S(1)}, bf16[96,2048]{1,0:T(8,128)(2,1)S(1)}, u32[]{:S(2)}, u32[]{:S(2)}) collective-permute-start(bf16[96,2048]{1,0:T(8,128)(2,1)S(1)} %pad_maximum_fusion), channel_id=1, source_target_pairs={{0,1},{1,0},{2,3},{3,2},{4,5},{5,4},{6,7},{7,6},{8,9},{9,8},{10,11... | collective-permute-start | bytes 1179656 | tf_op jit(solution)/shard_map/ppermute | solution.py:22
  86.2 5.6 %collective-permute-start.10 = (bf16[384,2048]{1,0:T(8,128)(2,1)}, bf16[384,2048]{1,0:T(8,128)(2,1)}, u32[]{:S(2)}, u32[]{:S(2)}) collective-permute-start(bf16[384,2048]{1,0:T(8,128)(2,1)} %convolution_convert_fusion), channel_id=1, source_target_pairs={{0,1},{1,0},{2,3},{3,2},{4,5},{5,4},{6,7},{7,6},{8,9},{9,8},{10,11... | collective-permute-start | bytes 4718600 | tf_op jit(solution)/shard_map/ppermute | solution.py:22
  93.9 1.7 copy-start
  95.6 12.8 %collective-permute-start.11 = (bf16[48,2048]{1,0:T(8,128)(2,1)S(1)}, bf16[48,2048]{1,0:T(8,128)(2,1)S(1)}, u32[]{:S(2)}, u32[]{:S(2)}) collective-permute-start(bf16[48,2048]{1,0:T(8,128)(2,1)S(1)} %get-tuple-element.26), channel_id=1, source_target_pairs={{0,2},{2,4},{4,6},{6,0},{1,3},{3,5},{5,7},{7,1},{8,10},{10,12},{12... | collective-permute-start | bytes 589832 | tf_op jit(solution)/shard_map/ppermute | solution.py:18
  97.5 37.6 %copy-start.2 = (f32[96,2048]{1,0:T(8,128)S(1)}, f32[96,2048]{1,0:T(8,128)}, u32[]{:S(2)}) copy-start(f32[96,2048]{1,0:T(8,128)} %get-tuple-element.23) | copy-start | bytes 2359300
  97.5 10.8 %collective-permute-start.13 = (bf16[48,2048]{1,0:T(8,128)(2,1)S(1)}, bf16[48,2048]{1,0:T(8,128)(2,1)}, u32[]{:S(2)}, u32[]{:S(2)}) collective-permute-start(bf16[48,2048]{1,0:T(8,128)(2,1)S(1)} %get-tuple-element.27), channel_id=1, source_target_pairs={{0,6},{2,0},{4,2},{6,4},{1,7},{3,1},{5,3},{7,5},{8,14},{10,8},{12,... | collective-permute-start | bytes 589832 | tf_op jit(solution)/shard_map/ppermute | solution.py:18
  103.6 13.8 %all-to-all-start.1 = ((f32[4,192,96]{2,1,0:T(8,128)}), f32[4,192,96]{2,1,0:T(8,128)S(1)}, u32[]{:S(2)}, u32[]{:S(2)}) async-start(f32[4,192,96]{2,1,0:T(8,128)} %bitcast.19), calls=%async_computation.1 | async-start | bytes 786432 | tf_op jit(solution)/shard_map/all_to_all | solution.py:121
  109.6 25.4 %collective-permute-start.12 = (bf16[96,2048]{1,0:T(8,128)(2,1)S(1)}, bf16[96,2048]{1,0:T(8,128)(2,1)S(1)}, u32[]{:S(2)}, u32[]{:S(2)}) collective-permute-start(bf16[96,2048]{1,0:T(8,128)(2,1)S(1)} %pad_maximum_fusion.1), channel_id=1, source_target_pairs={{0,2},{2,4},{4,6},{6,0},{1,3},{3,5},{5,7},{7,1},{8,10},{10,12},{12... | collective-permute-start | bytes 1179656 | tf_op jit(solution)/shard_map/ppermute | solution.py:18
  112.3 22.7 %collective-permute-start.14 = (bf16[96,2048]{1,0:T(8,128)(2,1)}, bf16[96,2048]{1,0:T(8,128)(2,1)S(1)}, u32[]{:S(2)}, u32[]{:S(2)}) collective-permute-start(bf16[96,2048]{1,0:T(8,128)(2,1)} %pad_maximum_fusion.2), channel_id=1, source_target_pairs={{0,6},{2,0},{4,2},{6,4},{1,7},{3,1},{5,3},{7,5},{8,14},{10,8},{12,... | collective-permute-start | bytes 1179656 | tf_op jit(solution)/shard_map/ppermute | solution.py:18
  138.0 19.4 %all-to-all-start.3 = ((f32[16,17,96]{2,1,0:T(8,128)}), f32[16,17,96]{2,1,0:T(8,128)S(1)}, u32[]{:S(2)}, u32[]{:S(2)}) async-start(f32[16,17,96]{2,1,0:T(8,128)} %broadcast_in_dim.7), calls=%async_computation.3 | async-start | bytes 393216 | tf_op jit(solution)/shard_map/all_to_all | solution.py:37
  141.7 9.9 %collective-permute-start.15 = (bf16[96,2]{1,0:T(8,128)(2,1)S(1)}, bf16[96,2]{1,0:T(8,128)(2,1)S(1)}, u32[]{:S(2)}, u32[]{:S(2)}) collective-permute-start(bf16[96,2]{1,0:T(8,128)(2,1)S(1)} %get-tuple-element.31), channel_id=1, source_target_pairs={{0,8},{8,16},{16,24},{24,32},{32,40},{40,48},{48,56},{56,64},{64,7... | collective-permute-start | bytes 1160 | tf_op jit(solution)/shard_map/ppermute | solution.py:29
  145.5 6.1 %collective-permute-start.16 = (bf16[96,2]{1,0:T(8,128)(2,1)S(1)}, bf16[96,2]{1,0:T(8,128)(2,1)S(1)}, u32[]{:S(2)}, u32[]{:S(2)}) collective-permute-start(bf16[96,2]{1,0:T(8,128)(2,1)S(1)} %get-tuple-element.30), channel_id=1, source_target_pairs={{8,0},{16,8},{24,16},{32,24},{40,32},{48,40},{56,48},{64,56},{72,6... | collective-permute-start | bytes 1160 | tf_op jit(solution)/shard_map/ppermute | solution.py:30
  158.4 10.1 %all-to-all-start.4 = ((f32[4,197,96]{1,2,0:T(8,128)}), f32[4,197,96]{1,2,0:T(8,128)S(1)}, u32[]{:S(2)}, u32[]{:S(2)}) async-start(f32[4,197,96]{1,2,0:T(8,128)} %broadcast_in_dim.8), calls=%async_computation.4 | async-start | bytes 786432 | tf_op jit(solution)/shard_map/all_to_all | solution.py:37

commit v2 on v1

v2 whole, which is shorter than its diff:
```python
import jax
import jax.numpy as jnp
import numpy as np
from jax import lax
from jax.sharding import Mesh
from jax.sharding import PartitionSpec as P

F32 = jnp.float32
BF16 = jnp.bfloat16
SEQ = ("x", "z")


def ring(count, shift):
    return [(i, (i + shift) % count) for i in range(count)]


def along_y(value, shift):
    return lax.ppermute(value, "y", ring(lax.axis_size("y"), shift))


def other_core(value):
    return lax.ppermute(value, "c", [(0, 1), (1, 0)])


def halo(cells, width):
    count = lax.axis_size(SEQ)
    head = cells[:, :width]
    tail = cells[:, -width:]
    left = lax.ppermute(tail, SEQ, [(i, i + 1) for i in range(count - 1)])
    right = lax.ppermute(head, SEQ, [(i + 1, i) for i in range(count - 1)])
    return jnp.concatenate([left, cells, right], axis=1)


def share(value, axes):
    count = lax.axis_size(axes)
    copies = jnp.broadcast_to(value.reshape(1, 1, -1), (count, 1, value.size))
    return lax.all_to_all(copies, axes, 0, 0, tiled=True)[:, 0]


def scatter_track(kept, sent):
    width = kept.shape[0] // 4
    half = width // 2
    both = (kept.astype(F32) + other_core(sent).astype(F32)).reshape(4, width, -1)
    narrow = both.astype(BF16)
    low = along_y(narrow[2, :half], 1)
    high = along_y(narrow[2, half:], -1)
    up = jnp.concatenate(
        [(both[1, :half] + low.astype(F32)).astype(BF16), narrow[1, half:]], axis=0
    )
    down = jnp.concatenate(
        [narrow[3, :half], (both[3, half:] + high.astype(F32)).astype(BF16)], axis=0
    )
    from_below = along_y(up, 1)
    from_above = along_y(down, -1)
    return both[0] + from_below.astype(F32) + from_above.astype(F32)


def convolve(cells, tap, offsets, count):
    result = jnp.zeros((cells.shape[0], count), F32)
    for k, start in enumerate(offsets):
        result = result + tap[k][:, None] * cells[:, start : start + count]
    return result


def shards(embeddings, taps, head_weight, targets):
    width = embeddings.shape[0]
    count = embeddings.shape[1]
    tracks = head_weight.shape[0]
    ntaps = taps.shape[0]
    reach = ntaps // 2
    y = lax.axis_index("y")
    c = lax.axis_index("c")
    ny = lax.axis_size("y")
    nseq = lax.axis_size(SEQ)
    me = lax.axis_index(SEQ)
    features = ny * 2 * width
    tap = taps.astype(F32)
    steps = list(range(ntaps))

    bare = jnp.pad(embeddings, ((0, 0), (reach, reach))).astype(F32)
    early = jax.nn.silu(convolve(bare, tap, steps, count)).astype(BF16)
    gathered = lax.all_gather(early, ("y", "c"), axis=0, tiled=True)

    padded = halo(embeddings, reach).astype(F32)
    conv = convolve(padded, tap, steps, count)
    sig = jax.nn.sigmoid(conv)
    slope = sig * (1.0 + conv * (1.0 - sig))
    lanes = 128
    late = conv * sig
    rim = jnp.concatenate([late[:, : lanes // 2], late[:, -lanes // 2 :]], axis=1).astype(BF16)
    rims = lax.all_to_all(
        jnp.broadcast_to(rim[None], (2 * ny, width, lanes)), ("y", "c"), 0, 0, tiled=True
    ).reshape(features, lanes)
    place = jnp.arange(lanes)[None, :]
    hidden = jnp.concatenate(
        [
            jnp.where(place < reach, rims, gathered[:, :lanes]),
            gathered[:, lanes:-lanes],
            jnp.where(place >= lanes - reach, rims, gathered[:, -lanes:]),
        ],
        axis=1,
    )

    blocks = head_weight.reshape(tracks, ny, 2, width)
    twice = jnp.concatenate([blocks, blocks], axis=1)
    turned = lax.dynamic_slice_in_dim(twice, y, ny, axis=1)
    first = jnp.where(c == 0, turned[:, :, 0], turned[:, :, 1]).reshape(tracks, ny * width)
    second = jnp.where(c == 0, turned[:, :, 1], turned[:, :, 0]).reshape(tracks, ny * width)

    logits = jnp.dot(head_weight, hidden, preferred_element_type=F32)
    top = jnp.max(logits, axis=1)
    expo = jnp.exp(logits - top[:, None])
    stats = jnp.concatenate([top, jnp.sum(expo, axis=1), jnp.sum(targets, axis=1)])
    every = share(stats, SEQ)
    tops = every[:, :tracks]
    peak = jnp.max(tops, axis=0)
    total = jnp.sum(every[:, tracks : 2 * tracks] * jnp.exp(tops - peak[None]), axis=0)
    counts = jnp.sum(every[:, 2 * tracks :], axis=0)
    scale = counts * jnp.exp(top - peak) / total
    logit_grad = (scale[:, None] * expo - targets).astype(BF16)

    turn = (((0,), (0,)), ((), ()))
    sent = lax.dot_general(second, logit_grad, turn, preferred_element_type=F32).astype(BF16)
    kept = lax.dot_general(first, logit_grad, turn, preferred_element_type=F32).astype(BF16)
    hidden_grad = scatter_track(kept, sent)

    local = lax.dot_general(
        logit_grad, hidden, (((1,), (1,)), ((), ())), preferred_element_type=F32
    ).reshape(nseq, 1, -1)
    part = jnp.sum(lax.all_to_all(local, SEQ, 0, 0, tiled=True), axis=0).reshape(-1)

    conv_grad = (hidden_grad * slope).astype(BF16)
    grad_float = conv_grad.astype(F32)
    local_taps = jnp.concatenate(
        [jnp.sum(padded[:, k : k + count] * grad_float, axis=1) for k in range(ntaps)]
    )
    row = jnp.arange(nseq)[:, None]
    head = grad_float[:, :reach].T.reshape(1, -1)
    tail = grad_float[:, -reach:].T.reshape(1, -1)
    edge = jnp.where(row == me + 1, tail, jnp.where(row == me - 1, head, 0.0))
    same = jnp.concatenate([part, local_taps])
    message = jnp.concatenate(
        [jnp.broadcast_to(same[None], (nseq, same.size)), edge], axis=1
    )
    slab = lax.all_to_all(message[:, None], SEQ, 0, 0, tiled=True)[:, 0]
    weight_grad = slab[:, : part.size].reshape(tracks, features)
    taps_grad = jnp.sum(slab[:, part.size : same.size], axis=0).reshape(ntaps, width)
    edges = slab[:, same.size :]
    left = jnp.sum(jnp.where(row == me - 1, edges, 0.0), axis=0).reshape(reach, width).T
    right = jnp.sum(jnp.where(row == me + 1, edges, 0.0), axis=0).reshape(reach, width).T

    grad_pad = jnp.concatenate([left, grad_float, right], axis=1)
    embed_grad = convolve(grad_pad, tap, [2 * reach - k for k in steps], count)
    return embed_grad.astype(BF16), weight_grad, taps_grad


def solution(mesh):
    fine = Mesh(np.asarray(mesh.devices).reshape(4, 16, 4, 2), ("x", "z", "y", "c"))
    track = ("y", "c")
    return jax.shard_map(
        shards,
        mesh=fine,
        in_specs=(P(track, SEQ), P(None, track), P(track, None), P(track, SEQ)),
        out_specs=(P(track, SEQ), P(track, None), P(None, track)),
        check_vma=False,
    )
```

time: 172 us -> 202 us (1.17)
  waiting for transfers between devices: 14.9 us -> 58.3 us
  starting transfers between devices: 73 us -> 56.4 us
  between operations: 1.16 us -> 14.5 us
  blocking collectives: 45.9 us -> 37.6 us
  matrix products: 9.36 us -> 6.33 us
  other arithmetic: 11.4 us -> 14.2 us
    all_gather x0 -> x1, waiting for transfers between devices: none -> 28.1 us  [shards(): gathered = lax.all_gather(early, ('y', 'c'), axis=0, tiled=True)]
    all_to_all x3, waiting for transfers between devices: 8.96 us -> 26.8 us  [the longest x1 14 us: share(): return lax.all_to_all(copies, axes, 0, 0, tiled=True)[:, 0]]
    ppermute x8 -> x4, starting transfers between devices: 28.3 us -> 14.2 us  [along_y(): return lax.ppermute(value, 'y', ring(lax.axis_size('y'), shift))]
    all_to_all x3, starting transfers between devices: 13.1 us -> 26.6 us  [the longest x1 15.9 us: share(): return lax.all_to_all(copies, axes, 0, 0, tiled=True)[:, 0]]
    all_to_all x2 -> x1, blocking collectives: 45.9 us -> 37.6 us  [shards(): slab = lax.all_to_all(message[:, None], SEQ, 0, 0, tiled=True)[:, 0]]
    ppermute x5 -> x1, starting transfers between devices: 10.1 us -> 1.92 us  [other_core(): return lax.ppermute(value, 'c', [(0, 1), (1, 0)])]
    unnamed x16 -> x20, local copies, waits for them, and re-layouts: 7.34 us -> 1.42 us
    ppermute x2 -> x1, starting transfers between devices: 13.9 us -> 9.76 us  [halo(): right = lax.ppermute(head, SEQ, [(i + 1, i) for i in range(count - 1)])]
  transfers between devices with their start and end apart: 20 -> 11, of which waited for: 6 -> 4; matrix products, arithmetic and copies ran while one was open for 9% -> 6% of each run, Pallas kernels for 0% -> 0%
where the time goes in v2:
time: 202 us; the launch traced here: 200 us
  waiting for transfers between devices  58.3 us (29%)
  starting transfers between devices  56.4 us (28%)
  blocking collectives  37.6 us (19%)
  between operations  14.5 us (7%)
  other arithmetic  14.2 us (7%)
  local copies, waits for them, and re-layouts  12.9 us (6%)
  matrix products  6.33 us (3%)
    all_to_all x1, blocking collectives, shards(): slab = lax.all_to_all(message[:, None], SEQ, 0, 0, tiled=True)[:, 0]  37.6 us
    all_gather x1, waiting for transfers between devices, shards(): gathered = lax.all_gather(early, ('y', 'c'), axis=0, tiled=True)  28.1 us
    all_to_all x1, starting transfers between devices, share(): return lax.all_to_all(copies, axes, 0, 0, tiled=True)[:, 0]  15.9 us
    ppermute x4, starting transfers between devices, along_y(): return lax.ppermute(value, 'y', ring(lax.axis_size('y'), shift))  14.2 us
    all_to_all x1, waiting for transfers between devices, share(): return lax.all_to_all(copies, axes, 0, 0, tiled=True)[:, 0]  14 us
    all_to_all x1, waiting for transfers between devices, shards(): lax.all_to_all(local, SEQ, 0, 0, tiled=True)  12.8 us
    ppermute x1, starting transfers between devices, halo(): right = lax.ppermute(head, SEQ, [(i + 1, i) for i in range(count - 1)])  9.76 us
    all_to_all x1, starting transfers between devices, shards(): lax.all_to_all(local, SEQ, 0, 0, tiled=True)  6.23 us
  transfers between devices with their start and end apart: 11, of which 4 were waited for; matrix products, arithmetic and copies ran while one was open for 6% of the time, Pallas kernels for 0%

profile of v2, /device:TPU:6, one launch (start us, length us, event | category | flops | bytes accessed | tf_op | source)
XLA Modules:
  0.0 200.2 jit_solution(4246611985438826048)
XLA Ops:
  8.0 3.8 %collective-permute-start = (bf16[96,2]{1,0:T(8,128)(2,1)S(1)}, bf16[96,2]{1,0:T(8,128)(2,1)S(1)}, u32[]{:S(2)}, u32[]{:S(2)}) collective-permute-start(bf16[96,2]{1,0:T(8,128)(2,1)S(1)} %get-tuple-element.28), channel_id=1, source_target_pairs={{0,8},{8,16},{16,24},{24,32},{32,40},{40,48},{48,56},{56,64},{64,7... | collective-permute-start | bytes 1160 | tf_op jit(solution)/shard_map/ppermute | solution.py:29
  11.9 9.8 %collective-permute-start.1 = (bf16[96,2]{1,0:T(8,128)(2,1)S(1)}, bf16[96,2]{1,0:T(8,128)(2,1)S(1)}, u32[]{:S(2)}, u32[]{:S(2)}) collective-permute-start(bf16[96,2]{1,0:T(8,128)(2,1)S(1)} %get-tuple-element.27), channel_id=1, source_target_pairs={{8,0},{16,8},{24,16},{32,24},{40,32},{48,40},{56,48},{64,56},{72,6... | collective-permute-start | bytes 1160 | tf_op jit(solution)/shard_map/ppermute | solution.py:30
  23.5 1.4 concatenate.42
  25.0 2.8 %multiply_convert_fusion.1 = (bf16[96,2048]{1,0:T(8,128)(2,1)S(1)}, f32[96,2048]{1,0:T(8,128)}, bf16[96,2048]{1,0:T(8,128)(2,1)}) fusion(f32[96,2052]{1,0:T(8,128)S(1)} %convert_element_type.65, f32[96]{0:T(128)S(1)} %get-tuple-element.32, f32[96]{0:T(128)S(1)} %get-tuple-element.33, f32[96]{0:T(128)S(1)} %get-tuple-element.34, f32[96]{0:T(128)S(1)} %get-tuple-element.35, ...), kind=kLoop, calls=%fused_computation.51 | loop fusion | flops 5505024 | bytes 9439104 | tf_op jit(solution)/shard_map/convert.3
  28.7 4.5 %all-to-all-start = ((bf16[8,96,128]{2,1,0:T(8,128)(2,1)}), bf16[8,96,128]{2,1,0:T(8,128)(2,1)S(1)}, u32[]{:S(2)}, u32[]{:S(2)}) async-start(bf16[8,96,128]{2,1,0:T(8,128)(2,1)} %broadcast_in_dim.91), calls=%async_computation | async-start | bytes 393216 | tf_op jit(solution)/shard_map/all_to_all | solution.py:91
  33.6 28.1 %all-gather.2.cloned.1.call-done = bf16[768,2048]{1,0:T(8,128)(2,1)} async-done(((bf16[96,2048]{1,0:T(8,128)(2,1)}), bf16[768,2048]{1,0:T(8,128)(2,1)}) %all-gather.2.cloned.1.call-update) | async-done | bytes 3145744 | tf_op jit(solution)/shard_map/all_gather | solution.py:82
  61.7 3.5 %slice.211 = bf16[768,1792]{1,0:T(8,128)(2,1)} slice(bf16[768,2048]{1,0:T(8,128)(2,1)} %all-gather.2.cloned.1.call-done), slice={[0:768], [128:1920]} | slice | bytes 5505024 | tf_op jit(solution)/shard_map/slice | solution.py:98
  66.3 2.7 %fusion.38 = (f32[96]{0:T(128)S(1)}, f32[2048,96]{0,1:T(8,128)S(1)}) fusion(bf16[96,768]{1,0:T(8,128)(2,1)S(1)} %copy-done.8, bf16[768,128]{1,0:T(8,128)(2,1)S(1)} %get-tuple-element.16, bf16[768,1792]{1,0:T(8,128)(2,1)} %slice.211, bf16[768,128]{1,0:T(8,128)(2,1)S(1)} %get-tuple-element.15), kind=kOutput, calls=%fused_computation.104 | convolution fusion | flops 311623584 | bytes 4080000 | tf_op jit(solution)/shard_map/dot_general | solution.py:110
  70.1 15.9 %all-to-all-start.1 = ((f32[64,1,288]{2,1,0:T(1,128)}), f32[64,1,288]{2,1,0:T(1,128)S(1)}, u32[]{:S(2)}, u32[]{:S(2)}) async-start(f32[64,1,288]{2,1,0:T(1,128)} %broadcast_in_dim.93), calls=%async_computation.1 | async-start | bytes 196608 | tf_op jit(solution)/shard_map/all_to_all | solution.py:37
  86.7 14.0 %all-to-all-done.1 = f32[64,1,288]{2,1,0:T(1,128)S(1)} async-done(((f32[64,1,288]{2,1,0:T(1,128)}), f32[64,1,288]{2,1,0:T(1,128)S(1)}, u32[]{:S(2)}, u32[]{:S(2)}) %all-to-all-start.1) | async-done | bytes 73760 | tf_op jit(solution)/shard_map/all_to_all | solution.py:37
  101.7 1.9 collective-permute-start.2
  103.7 3.4 %collective-permute-done.2 = bf16[384,2048]{1,0:T(8,128)(2,1)} collective-permute-done((bf16[384,2048]{1,0:T(8,128)(2,1)S(1)}, bf16[384,2048]{1,0:T(8,128)(2,1)}, u32[]{:S(2)}, u32[]{:S(2)}) %collective-permute-start.2) | collective-permute-done | bytes 1572896 | tf_op jit(solution)/shard_map/ppermute | solution.py:22
  107.1 2.0 convert_add_fusion
  109.5 1.3 copy-done
  110.8 2.5 %collective-permute-start.3 = (bf16[48,2048]{1,0:T(8,128)(2,1)S(1)}, bf16[48,2048]{1,0:T(8,128)(2,1)S(1)}, u32[]{:S(2)}, u32[]{:S(2)}) collective-permute-start(bf16[48,2048]{1,0:T(8,128)(2,1)S(1)} %get-tuple-element.19), channel_id=1, source_target_pairs={{0,2},{2,4},{4,6},{6,0},{1,3},{3,5},{5,7},{7,1},{8,10},{10,12},{12... | collective-permute-start | bytes 589832 | tf_op jit(solution)/shard_map/ppermute | solution.py:18
  113.3 4.7 %collective-permute-start.5 = (bf16[48,2048]{1,0:T(8,128)(2,1)S(1)}, bf16[48,2048]{1,0:T(8,128)(2,1)}, u32[]{:S(2)}, u32[]{:S(2)}) collective-permute-start(bf16[48,2048]{1,0:T(8,128)(2,1)S(1)} %get-tuple-element.20), channel_id=1, source_target_pairs={{0,6},{2,0},{4,2},{6,4},{1,7},{3,1},{5,3},{7,5},{8,14},{10,8},{12,... | collective-permute-start | bytes 589832 | tf_op jit(solution)/shard_map/ppermute | solution.py:18
  120.1 6.2 %all-to-all-start.2 = ((f32[64,1,1152]{2,1,0:T(1,128)}), f32[64,1,1152]{2,1,0:T(1,128)S(1)}, u32[]{:S(2)}, u32[]{:S(2)}) async-start(f32[64,1,1152]{2,1,0:T(1,128)} %reshape.116), calls=%async_computation.2 | async-start | bytes 589824 | tf_op jit(solution)/shard_map/all_to_all | solution.py:130
  126.4 1.2 fusion.30
  127.7 1.9 collective-permute-start.4
  130.4 5.1 %collective-permute-start.6 = (bf16[96,2048]{1,0:T(8,128)(2,1)}, bf16[96,2048]{1,0:T(8,128)(2,1)S(1)}, u32[]{:S(2)}, u32[]{:S(2)}) collective-permute-start(bf16[96,2048]{1,0:T(8,128)(2,1)} %pad_maximum_fusion.7), channel_id=1, source_target_pairs={{0,6},{2,0},{4,2},{6,4},{1,7},{3,1},{5,3},{7,5},{8,14},{10,8},{12,... | collective-permute-start | bytes 1179656 | tf_op jit(solution)/shard_map/ppermute | solution.py:18
  135.5 12.8 %all-to-all-done.2 = f32[64,1,1152]{2,1,0:T(1,128)S(1)} async-done(((f32[64,1,1152]{2,1,0:T(1,128)}), f32[64,1,1152]{2,1,0:T(1,128)S(1)}, u32[]{:S(2)}, u32[]{:S(2)}) %all-to-all-start.2) | async-done | bytes 294944 | tf_op jit(solution)/shard_map/all_to_all | solution.py:130
  148.5 2.2 %fusion.15 = (f32[96]{0:T(128)S(1)}, f32[96]{0:T(128)S(1)}, f32[96]{0:T(128)S(1)}, f32[96]{0:T(128)S(1)}, f32[96]{0:T(128)S(1)}, /*index=5*/bf16[96,2048]{1,0:T(8,128)(2,1)S(1)}) fusion(f32[96,2052]{1,0:T(8,128)S(1)} %convert_element_type.65, f32[96,2048]{1,0:T(8,128)S(1)} %copy-done.2, bf16[96,2048]{1,0:T(8,128)(2,1)S(1)} %collective-permute-done.6, ...), kind=kLoop, calls=%fused_computation.29 | loop fusion | flops 4718112 | bytes 6686592 | tf_op jit(solution)/shard_map/reduce_sum | solution.py:135
  151.9 37.6 %all_to_all.20 = f32[64,1,1824]{2,1,0:T(1,128)S(1)} all-to-all(f32[64,1,1824]{2,1,0:T(1,128)S(1)} %broadcast_in_dim.102), channel_id=1, replica_groups=mesh['x'=4,'z'=16,'y'=4,'c'=2] {'x','z'}, dimensions={0} | all-to-all | bytes 933888 | tf_op jit(solution)/shard_map/all_to_all | solution.py:145
  191.5 1.8 fusion.6
  (81 shorter events, 14.5 us)
Async XLA Ops:
  7.2 54.6 %all-gather.2.cloned.1.call-start = ((), (), s32[]{:S(2)}) async-start(), calls=%async_computation.4 | async-start | bytes 3538944 | tf_op jit(solution)/shard_map/all_gather | solution.py:82
  8.0 15.5 %collective-permute-start = (bf16[96,2]{1,0:T(8,128)(2,1)S(1)}, bf16[96,2]{1,0:T(8,128)(2,1)S(1)}, u32[]{:S(2)}, u32[]{:S(2)}) collective-permute-start(bf16[96,2]{1,0:T(8,128)(2,1)S(1)} %get-tuple-element.28), channel_id=1, source_target_pairs={{0,8},{8,16},{16,24},{24,32},{32,40},{40,48},{48,56},{56,64},{64,7... | collective-permute-start | bytes 1160 | tf_op jit(solution)/shard_map/ppermute | solution.py:29
  11.9 11.6 %collective-permute-start.1 = (bf16[96,2]{1,0:T(8,128)(2,1)S(1)}, bf16[96,2]{1,0:T(8,128)(2,1)S(1)}, u32[]{:S(2)}, u32[]{:S(2)}) collective-permute-start(bf16[96,2]{1,0:T(8,128)(2,1)S(1)} %get-tuple-element.27), channel_id=1, source_target_pairs={{8,0},{16,8},{24,16},{32,24},{40,32},{48,40},{56,48},{64,56},{72,6... | collective-permute-start | bytes 1160 | tf_op jit(solution)/shard_map/ppermute | solution.py:30
  25.0 8.2 %copy-start.8 = (bf16[96,768]{1,0:T(8,128)(2,1)S(1)}, bf16[96,768]{1,0:T(8,128)(2,1)}, u32[]{:S(2)}) copy-start(bf16[96,768]{1,0:T(8,128)(2,1)} %param.6) | copy-start | bytes 442372
  25.0 8.5 %copy-start.1 = (f32[96,2048]{1,0:T(8,128)S(1)}, f32[96,2048]{1,0:T(8,128)}, u32[]{:S(2)}) copy-start(f32[96,2048]{1,0:T(8,128)} %param.7) | copy-start | bytes 2359300
  28.7 36.6 %all-to-all-start = ((bf16[8,96,128]{2,1,0:T(8,128)(2,1)}), bf16[8,96,128]{2,1,0:T(8,128)(2,1)S(1)}, u32[]{:S(2)}, u32[]{:S(2)}) async-start(bf16[8,96,128]{2,1,0:T(8,128)(2,1)} %broadcast_in_dim.91), calls=%async_computation | async-start | bytes 393216 | tf_op jit(solution)/shard_map/all_to_all | solution.py:91
  66.3 2.7 %copy-start.4 = (bf16[768,128]{1,0:T(8,128)(2,1)}, bf16[768,128]{1,0:T(8,128)(2,1)S(1)}, u32[]{:S(2)}) copy-start(bf16[768,128]{1,0:T(8,128)(2,1)S(1)} %get-tuple-element.15) | copy-start | bytes 589828
  66.3 2.7 %copy-start.6 = (bf16[768,128]{1,0:T(8,128)(2,1)}, bf16[768,128]{1,0:T(8,128)(2,1)S(1)}, u32[]{:S(2)}) copy-start(bf16[768,128]{1,0:T(8,128)(2,1)S(1)} %get-tuple-element.16) | copy-start | bytes 589828
  70.1 30.6 %all-to-all-start.1 = ((f32[64,1,288]{2,1,0:T(1,128)}), f32[64,1,288]{2,1,0:T(1,128)S(1)}, u32[]{:S(2)}, u32[]{:S(2)}) async-start(f32[64,1,288]{2,1,0:T(1,128)} %broadcast_in_dim.93), calls=%async_computation.1 | async-start | bytes 196608 | tf_op jit(solution)/shard_map/all_to_all | solution.py:37
  101.7 5.4 %collective-permute-start.2 = (bf16[384,2048]{1,0:T(8,128)(2,1)S(1)}, bf16[384,2048]{1,0:T(8,128)(2,1)}, u32[]{:S(2)}, u32[]{:S(2)}) collective-permute-start(bf16[384,2048]{1,0:T(8,128)(2,1)S(1)} %convolution_convert_fusion), channel_id=1, source_target_pairs={{0,1},{1,0},{2,3},{3,2},{4,5},{5,4},{6,7},{7,6},{8,9},{9,8},{10,11... | collective-permute-start | bytes 4718600 | tf_op jit(solution)/shard_map/ppermute | solution.py:22
  109.1 1.7 copy-start
  109.1 8.8 %copy-start.3 = (bf16[768,1792]{1,0:T(8,128)(2,1)S(1)}, bf16[768,1792]{1,0:T(8,128)(2,1)}, u32[]{:S(2)}) copy-start(bf16[768,1792]{1,0:T(8,128)(2,1)} %slice.211) | copy-start | bytes 8257540
  109.1 8.8 %copy-start.5 = (bf16[768,128]{1,0:T(8,128)(2,1)S(1)}, bf16[768,128]{1,0:T(8,128)(2,1)}, u32[]{:S(2)}) copy-start(bf16[768,128]{1,0:T(8,128)(2,1)} %copy-done.4) | copy-start | bytes 589828
  109.2 8.8 %copy-start.7 = (bf16[768,128]{1,0:T(8,128)(2,1)S(1)}, bf16[768,128]{1,0:T(8,128)(2,1)}, u32[]{:S(2)}) copy-start(bf16[768,128]{1,0:T(8,128)(2,1)} %copy-done.6) | copy-start | bytes 589828
  110.8 15.6 %collective-permute-start.3 = (bf16[48,2048]{1,0:T(8,128)(2,1)S(1)}, bf16[48,2048]{1,0:T(8,128)(2,1)S(1)}, u32[]{:S(2)}, u32[]{:S(2)}) collective-permute-start(bf16[48,2048]{1,0:T(8,128)(2,1)S(1)} %get-tuple-element.19), channel_id=1, source_target_pairs={{0,2},{2,4},{4,6},{6,0},{1,3},{3,5},{5,7},{7,1},{8,10},{10,12},{12... | collective-permute-start | bytes 589832 | tf_op jit(solution)/shard_map/ppermute | solution.py:18
  113.3 13.1 %collective-permute-start.5 = (bf16[48,2048]{1,0:T(8,128)(2,1)S(1)}, bf16[48,2048]{1,0:T(8,128)(2,1)}, u32[]{:S(2)}, u32[]{:S(2)}) collective-permute-start(bf16[48,2048]{1,0:T(8,128)(2,1)S(1)} %get-tuple-element.20), channel_id=1, source_target_pairs={{0,6},{2,0},{4,2},{6,4},{1,7},{3,1},{5,3},{7,5},{8,14},{10,8},{12,... | collective-permute-start | bytes 589832 | tf_op jit(solution)/shard_map/ppermute | solution.py:18
  119.1 29.4 %copy-start.2 = (f32[96,2048]{1,0:T(8,128)S(1)}, f32[96,2048]{1,0:T(8,128)}, u32[]{:S(2)}) copy-start(f32[96,2048]{1,0:T(8,128)} %get-tuple-element.14) | copy-start | bytes 2359300
  120.1 28.2 %all-to-all-start.2 = ((f32[64,1,1152]{2,1,0:T(1,128)}), f32[64,1,1152]{2,1,0:T(1,128)S(1)}, u32[]{:S(2)}, u32[]{:S(2)}) async-start(f32[64,1,1152]{2,1,0:T(1,128)} %reshape.116), calls=%async_computation.2 | async-start | bytes 589824 | tf_op jit(solution)/shard_map/all_to_all | solution.py:130
  127.7 20.8 %collective-permute-start.4 = (bf16[96,2048]{1,0:T(8,128)(2,1)S(1)}, bf16[96,2048]{1,0:T(8,128)(2,1)S(1)}, u32[]{:S(2)}, u32[]{:S(2)}) collective-permute-start(bf16[96,2048]{1,0:T(8,128)(2,1)S(1)} %pad_maximum_fusion.6), channel_id=1, source_target_pairs={{0,2},{2,4},{4,6},{6,0},{1,3},{3,5},{5,7},{7,1},{8,10},{10,12},{12... | collective-permute-start | bytes 1179656 | tf_op jit(solution)/shard_map/ppermute | solution.py:18
  130.4 18.1 %collective-permute-start.6 = (bf16[96,2048]{1,0:T(8,128)(2,1)}, bf16[96,2048]{1,0:T(8,128)(2,1)S(1)}, u32[]{:S(2)}, u32[]{:S(2)}) collective-permute-start(bf16[96,2048]{1,0:T(8,128)(2,1)} %pad_maximum_fusion.7), channel_id=1, source_target_pairs={{0,6},{2,0},{4,2},{6,4},{1,7},{3,1},{5,3},{7,5},{8,14},{10,8},{12,... | collective-permute-start | bytes 1179656 | tf_op jit(solution)/shard_map/ppermute | solution.py:18
Sparse Core Ops, SparseCore 0:
  27.9 33.7 all-gather.1

commit v3 on v2

v3 whole, which is shorter than its diff:
```python
import functools

import jax
import jax.numpy as jnp
import numpy as np
from jax import lax
from jax.experimental import pallas as pl
from jax.experimental.pallas import tpu as pltpu
from jax.sharding import Mesh
from jax.sharding import PartitionSpec as P

F32 = jnp.float32
BF16 = jnp.bfloat16
SEQ = ("x", "z")
LANES = 128


def ring(count, shift):
    return [(i, (i + shift) % count) for i in range(count)]


def along_y(value, shift):
    return lax.ppermute(value, "y", ring(lax.axis_size("y"), shift))


def other_core(value):
    return lax.ppermute(value, "c", [(0, 1), (1, 0)])


def outer_columns(cells, width):
    count = lax.axis_size(SEQ)
    left = lax.ppermute(cells[:, -width:], SEQ, [(i, i + 1) for i in range(count - 1)])
    right = lax.ppermute(cells[:, :width], SEQ, [(i + 1, i) for i in range(count - 1)])
    return left, right


def share(value, axes):
    count = lax.axis_size(axes)
    copies = jnp.broadcast_to(value.reshape(1, 1, -1), (count, 1, value.size))
    return lax.all_to_all(copies, axes, 0, 0, tiled=True)[:, 0]


ORDER = ((0, 0), (0, 1), (1, 0), (3, 0), (1, 1), (3, 1), (2, 0), (2, 1))


def gather_track(block):
    half = block.shape[0] // 2
    above = along_y(block, -1)
    below = along_y(block, 1)
    beside = other_core(block)
    far_low = along_y(below[:half], 1)
    far_high = along_y(above[half:], -1)
    above_beside = other_core(above)
    below_beside = other_core(below)
    far = jnp.concatenate([far_low, far_high], axis=0)
    far_beside = other_core(far)
    return jnp.concatenate(
        [block, beside, above, below, above_beside, below_beside, far, far_beside], axis=0
    )


def scatter_sends(kept, sent):
    width = kept.shape[0] // 4
    half = width // 2
    both = (kept.astype(F32) + other_core(sent).astype(F32)).reshape(4, width, -1)
    narrow = both.astype(BF16)
    low = along_y(narrow[2, :half], 1)
    high = along_y(narrow[2, half:], -1)
    up = jnp.concatenate(
        [(both[1, :half] + low.astype(F32)).astype(BF16), narrow[1, half:]], axis=0
    )
    down = jnp.concatenate(
        [narrow[3, :half], (both[3, half:] + high.astype(F32)).astype(BF16)], axis=0
    )
    return both[0], up, down, narrow


def forward_kernel(cells, left, right, tap, hidden, slope, line):
    reach = left.shape[1]
    count = cells.shape[1]
    line[:, :LANES] = jnp.zeros((cells.shape[0], LANES), F32)
    line[:, LANES + count :] = jnp.zeros((cells.shape[0], LANES), F32)
    line[:, LANES - reach : LANES] = left[...].astype(F32)
    line[:, LANES + count : LANES + count + reach] = right[...].astype(F32)
    line[:, LANES : LANES + count] = cells[...].astype(F32)
    rows = 8

    @pl.loop(0, cells.shape[0] // 16)
    def _(block):
        both_hidden = []
        for part in range(2):
            at = pl.ds(pl.multiple_of(block * 16 + part * rows, rows), rows)
            whole = line[at, :]
            taps = tap[at, :]
            conv = jnp.zeros((rows, count), F32)
            for k in range(2 * reach + 1):
                shift = (reach - k) % whole.shape[1]
                moved = pltpu.roll(whole, shift, 1) if shift else whole
                conv = conv + taps[:, k : k + 1] * moved[:, LANES : LANES + count]
            sig = jax.nn.sigmoid(conv)
            both_hidden.append((conv * sig).astype(BF16))
            slope[at, :] = sig * (1.0 + conv * (1.0 - sig))
        out = pl.ds(pl.multiple_of(block * 16, 16), 16)
        hidden[out, :] = jnp.concatenate(both_hidden, axis=0)


def forward(cells, left, right, tap):
    rows, count = cells.shape
    return pl.pallas_call(
        forward_kernel,
        out_shape=(
            jax.ShapeDtypeStruct((rows, count), BF16),
            jax.ShapeDtypeStruct((rows, count), F32),
        ),
        scratch_shapes=[pltpu.VMEM((rows, count + 2 * LANES), F32)],
        compiler_params=pltpu.CompilerParams(vmem_limit_bytes=16 * 2**20),
        cost_estimate=pl.CostEstimate(
            flops=20 * rows * count, bytes_accessed=8 * rows * count, transcendentals=rows * count
        ),
        name="conv_silu",
    )(cells, left, right, tap)


def shards(embeddings, taps, head_weight, targets):
    width = embeddings.shape[0]
    count = embeddings.shape[1]
    tracks = head_weight.shape[0]
    ntaps = taps.shape[0]
    reach = ntaps // 2
    y = lax.axis_index("y")
    c = lax.axis_index("c")
    ny = lax.axis_size("y")
    nseq = lax.axis_size(SEQ)
    me = lax.axis_index(SEQ)
    features = ny * 2 * width
    tap = taps.astype(F32)

    left, right = outer_columns(embeddings, reach)
    block, slope = forward(embeddings, left, right, jnp.pad(tap, ((0, 8 - ntaps), (0, 0))).T)
    hidden = gather_track(block)

    blocks = head_weight.reshape(tracks, ny, 2, width)
    twice = jnp.concatenate([blocks, blocks], axis=1)
    turned = lax.dynamic_slice_in_dim(twice, y, ny, axis=1)
    turned = (
        jnp.where(c == 0, turned[:, :, 0], turned[:, :, 1]),
        jnp.where(c == 0, turned[:, :, 1], turned[:, :, 0]),
    )
    first = turned[0].reshape(tracks, ny * width)
    second = turned[1].reshape(tracks, ny * width)
    ordered = jnp.concatenate([turned[core][:, dy] for dy, core in ORDER], axis=1)

    logits = jnp.dot(ordered, hidden, preferred_element_type=F32)
    top = jnp.max(logits, axis=1)
    expo = jnp.exp(logits - top[:, None])
    stats = jnp.concatenate([top, jnp.sum(expo, axis=1), jnp.sum(targets, axis=1)])
    every = share(stats, SEQ)
    tops = every[:, :tracks]
    peak = jnp.max(tops, axis=0)
    total = jnp.sum(every[:, tracks : 2 * tracks] * jnp.exp(tops - peak[None]), axis=0)
    counts = jnp.sum(every[:, 2 * tracks :], axis=0)
    scale = counts * jnp.exp(top - peak) / total
    logit_grad = (scale[:, None] * expo - targets).astype(BF16)

    turn = (((0,), (0,)), ((), ()))
    sent = lax.dot_general(second, logit_grad, turn, preferred_element_type=F32).astype(BF16)
    kept = lax.dot_general(first, logit_grad, turn, preferred_element_type=F32).astype(BF16)
    mine, up, down, narrow = scatter_sends(kept, sent)

    late_grad, _ = lax.optimization_barrier((logit_grad, narrow))
    local = lax.dot_general(
        hidden, late_grad, (((1,), (1,)), ((), ())), preferred_element_type=F32
    ).reshape(2 * ny, width, tracks)
    sorted_blocks = [
        [local[ORDER.index((dy, core))] for dy in range(ny)] for core in range(2)
    ]
    by_core = jnp.stack([jnp.stack(sorted_blocks[0]), jnp.stack(sorted_blocks[1])], axis=1)
    by_core = jnp.where(c == 0, by_core, by_core[:, ::-1])
    by_core = lax.dynamic_slice_in_dim(
        jnp.concatenate([by_core, by_core], axis=0), (ny - y) % ny, ny, axis=0
    )
    local = by_core.reshape(features, tracks).T.reshape(nseq, 1, -1)
    local, up, down = lax.optimization_barrier((local, up, down))
    from_below = along_y(up, 1)
    from_above = along_y(down, -1)
    part = jnp.sum(lax.all_to_all(local, SEQ, 0, 0, tiled=True), axis=0).reshape(-1)

    hidden_grad = mine + from_below.astype(F32) + from_above.astype(F32)
    conv_grad = (hidden_grad * slope).astype(BF16)
    grad_float = conv_grad.astype(F32)
    padded = jnp.concatenate([left, embeddings, right], axis=1).astype(F32)
    local_taps = jnp.concatenate(
        [jnp.sum(padded[:, k : k + count] * grad_float, axis=1) for k in range(ntaps)]
    )
    high = lax.reduce_precision(local_taps, 8, 7)
    low = local_taps - high
    row = jnp.arange(nseq)[:, None]
    head = conv_grad[:, :reach].T.reshape(1, -1)
    tail = conv_grad[:, -reach:].T.reshape(1, -1)
    zero = jnp.zeros((), BF16)
    edge = jnp.where(row == me + 1, tail, jnp.where(row == me - 1, head, zero))
    same = jnp.concatenate([part, high, low]).astype(BF16)
    message = jnp.concatenate(
        [jnp.broadcast_to(same[None], (nseq, same.size)), edge], axis=1
    )
    slab = lax.all_to_all(message[:, None], SEQ, 0, 0, tiled=True)[:, 0]
    weight_grad = slab[:, : part.size].reshape(tracks, features).astype(F32)
    sums = jnp.sum(slab[:, part.size : same.size].astype(F32), axis=0).reshape(2, ntaps, width)
    taps_grad = sums[0] + sums[1]
    edges = slab[:, same.size :]
    before = jnp.sum(jnp.where(row == me - 1, edges, zero).astype(F32), axis=0)
    after = jnp.sum(jnp.where(row == me + 1, edges, zero).astype(F32), axis=0)

    grad_pad = jnp.concatenate(
        [before.reshape(reach, width).T, grad_float, after.reshape(reach, width).T], axis=1
    )
    embed_grad = jnp.zeros((width, count), F32)
    for k in range(ntaps):
        start = 2 * reach - k
        embed_grad = embed_grad + tap[k][:, None] * grad_pad[:, start : start + count]
    return embed_grad.astype(BF16), weight_grad, taps_grad


def solution(mesh):
    fine = Mesh(np.asarray(mesh.devices).reshape(4, 16, 4, 2), ("x", "z", "y", "c"))
    track = ("y", "c")
    return jax.shard_map(
        shards,
        mesh=fine,
        in_specs=(P(track, SEQ), P(None, track), P(track, None), P(track, SEQ)),
        out_specs=(P(track, SEQ), P(track, None), P(None, track)),
        check_vma=False,
    )
```

time: 202 us -> 191 us (0.946)
  blocking collectives: 37.6 us -> 0 us
  starting transfers between devices: 56.4 us -> 74.4 us
  waiting for transfers between devices: 58.3 us -> 74 us
  between operations: 14.5 us -> 1.28 us
  local copies, waits for them, and re-layouts: 12.9 us -> 19.2 us
    all_to_all x1 -> x0, blocking collectives: 37.6 us -> none  [shards(): slab = lax.all_to_all(message[:, None], SEQ, 0, 0, tiled=True)[:, 0]]
    all_gather x1 -> x0, waiting for transfers between devices: 28.1 us -> none  [shards(): gathered = lax.all_gather(early, ('y', 'c'), axis=0, tiled=True)]
    all_to_all x1, waiting for transfers between devices: 0.01 us -> 20.3 us  [shards(): slab = lax.all_to_all(message[:, None], SEQ, 0, 0, tiled=True)[:, 0]]
    ppermute x4 -> x8, waiting for transfers between devices: 0.01 us -> 19 us  [along_y(): return lax.ppermute(value, 'y', ring(lax.axis_size('y'), shift))]
    ppermute x4 -> x8, starting transfers between devices: 14.2 us -> 25.6 us  [along_y(): return lax.ppermute(value, 'y', ring(lax.axis_size('y'), shift))]
    ppermute x1 -> x5, starting transfers between devices: 1.92 us -> 10.1 us  [other_core(): return lax.ppermute(value, 'c', [(0, 1), (1, 0)])]
    unnamed x20 -> x25, local copies, waits for them, and re-layouts: 1.42 us -> 6.9 us
    all_to_all x1, starting transfers between devices: 15.9 us -> 12.3 us  [share(): return lax.all_to_all(copies, axes, 0, 0, tiled=True)[:, 0]]
  transfers between devices with their start and end apart: 11 -> 18, of which waited for: 4 -> 9; matrix products, arithmetic and copies ran while one was open for 6% -> 8% of each run, Pallas kernels for 0% -> 0%
where the time goes in v3:
time: 191 us; the launch traced here: 190 us
  starting transfers between devices  74.4 us (39%)
  waiting for transfers between devices  74 us (39%)
  local copies, waits for them, and re-layouts  19.2 us (10%)
  other arithmetic  12.9 us (7%)
  matrix products  6.46 us (3%)
    ppermute x8, starting transfers between devices, along_y(): return lax.ppermute(value, 'y', ring(lax.axis_size('y'), shift))  25.6 us
    all_to_all x1, waiting for transfers between devices, shards(): slab = lax.all_to_all(message[:, None], SEQ, 0, 0, tiled=True)[:, 0]  20.3 us
    ppermute x8, waiting for transfers between devices, along_y(): return lax.ppermute(value, 'y', ring(lax.axis_size('y'), shift))  19 us
    all_to_all x1, waiting for transfers between devices, shards(): lax.all_to_all(local, SEQ, 0, 0, tiled=True)  15.8 us
    all_to_all x1, waiting for transfers between devices, share(): return lax.all_to_all(copies, axes, 0, 0, tiled=True)[:, 0]  13.8 us
    all_to_all x1, starting transfers between devices, share(): return lax.all_to_all(copies, axes, 0, 0, tiled=True)[:, 0]  12.3 us
    ppermute x5, starting transfers between devices, other_core(): return lax.ppermute(value, 'c', [(0, 1), (1, 0)])  10.1 us
    ppermute x1, starting transfers between devices, outer_columns(): lax.ppermute(cells[:, :width], SEQ, [(i + 1, i) for i in range(count - 1)])  9.76 us
  transfers between devices with their start and end apart: 18, of which 9 were waited for; matrix products, arithmetic and copies ran while one was open for 8% of the time, Pallas kernels for 0%

profile of v3, /device:TPU:6, one launch (start us, length us, event | category | flops | bytes accessed | tf_op | source)
XLA Modules:
  0.0 189.9 jit_solution(1649075427595561791)
XLA Ops:
  1.6 3.8 %collective-permute-start = (bf16[96,2]{1,0:T(8,128)(2,1)S(1)}, bf16[96,2]{1,0:T(8,128)(2,1)S(1)}, u32[]{:S(2)}, u32[]{:S(2)}) collective-permute-start(bf16[96,2]{1,0:T(8,128)(2,1)S(1)} %get-tuple-element.44), channel_id=1, source_target_pairs={{0,8},{8,16},{16,24},{24,32},{32,40},{40,48},{48,56},{56,64},{64,7... | collective-permute-start | bytes 1160 | tf_op jit(solution)/shard_map/ppermute | solution.py:32
  5.4 9.8 %collective-permute-start.1 = (bf16[96,2]{1,0:T(8,128)(2,1)S(1)}, bf16[96,2]{1,0:T(8,128)(2,1)S(1)}, u32[]{:S(2)}, u32[]{:S(2)}) collective-permute-start(bf16[96,2]{1,0:T(8,128)(2,1)S(1)} %get-tuple-element.43), channel_id=1, source_target_pairs={{8,0},{16,8},{24,16},{32,24},{40,32},{48,40},{56,48},{64,56},{72,6... | collective-permute-start | bytes 1160 | tf_op jit(solution)/shard_map/ppermute | solution.py:33
  17.8 2.1 %fusion.31 = (bf16[96,4,96]{2,1,0:T(4,128)(2,1)}, bf16[96,4,1,96]{3,2,1,0:T(2,128)(2,1)S(1)}, bf16[96,4,96]{2,1,0:T(4,128)(2,1)S(1)}, bf16[96,4,1,96]{3,2,1,0:T(2,128)(2,1)S(1)}) fusion(bf16[96,4,2,96]{3,2,1,0:T(2,128)(2,1)S(1)} %fusion.25, pred[]{:T(512)S(6)} %eq.33), kind=kLoop, calls=%fused_computation.120 | loop fusion | flops 73728 | bytes 442369 | tf_op jit(solution)/shard_map/jit(_where)/select_n | solution.py:147
  22.4 1.9 %collective-permute-start.2 = (bf16[96,2048]{1,0:T(8,128)(2,1)S(1)}, bf16[96,2048]{1,0:T(8,128)(2,1)}, u32[]{:S(2)}, u32[]{:S(2)}) collective-permute-start(bf16[96,2048]{1,0:T(8,128)(2,1)S(1)} %get-tuple-element.9), channel_id=1, source_target_pairs={{0,1},{1,0},{2,3},{3,2},{4,5},{5,4},{6,7},{7,6},{8,9},{9,8},{10,11... | collective-permute-start | bytes 1179656 | tf_op jit(solution)/shard_map/ppermute | solution.py:27
  24.4 4.9 %collective-permute-start.3 = (bf16[96,2048]{1,0:T(8,128)(2,1)S(1)}, bf16[96,2048]{1,0:T(8,128)(2,1)S(1)}, u32[]{:S(2)}, u32[]{:S(2)}) collective-permute-start(bf16[96,2048]{1,0:T(8,128)(2,1)S(1)} %get-tuple-element.9), channel_id=1, source_target_pairs={{0,6},{2,0},{4,2},{6,4},{1,7},{3,1},{5,3},{7,5},{8,14},{10,8},{12,... | collective-permute-start | bytes 1179656 | tf_op jit(solution)/shard_map/ppermute | solution.py:23
  29.3 1.9 %collective-permute-start.4 = (bf16[96,2048]{1,0:T(8,128)(2,1)S(1)}, bf16[96,2048]{1,0:T(8,128)(2,1)S(1)}, u32[]{:S(2)}, u32[]{:S(2)}) collective-permute-start(bf16[96,2048]{1,0:T(8,128)(2,1)S(1)} %get-tuple-element.9), channel_id=1, source_target_pairs={{0,2},{2,4},{4,6},{6,0},{1,3},{3,5},{5,7},{7,1},{8,10},{10,12},{12... | collective-permute-start | bytes 1179656 | tf_op jit(solution)/shard_map/ppermute | solution.py:23
  32.9 10.8 %collective-permute-done.4 = bf16[96,2048]{1,0:T(8,128)(2,1)S(1)} collective-permute-done((bf16[96,2048]{1,0:T(8,128)(2,1)S(1)}, bf16[96,2048]{1,0:T(8,128)(2,1)S(1)}, u32[]{:S(2)}, u32[]{:S(2)}) %collective-permute-start.4) | collective-permute-done | bytes 393248 | tf_op jit(solution)/shard_map/ppermute | solution.py:23
  43.7 1.9 %collective-permute-start.7 = (bf16[48,2048]{1,0:T(8,128)(2,1)S(1)}, bf16[48,2048]{1,0:T(8,128)(2,1)S(1)}, u32[]{:S(2)}, u32[]{:S(2)}) collective-permute-start(bf16[48,2048]{1,0:T(8,128)(2,1)S(1)} %slice.280), channel_id=1, source_target_pairs={{0,2},{2,4},{4,6},{6,0},{1,3},{3,5},{5,7},{7,1},{8,10},{10,12},{12... | collective-permute-start | bytes 589832 | tf_op jit(solution)/shard_map/ppermute | solution.py:23
  45.6 5.1 %collective-permute-start.8 = (bf16[48,2048]{1,0:T(8,128)(2,1)S(1)}, bf16[48,2048]{1,0:T(8,128)(2,1)S(1)}, u32[]{:S(2)}, u32[]{:S(2)}) collective-permute-start(bf16[48,2048]{1,0:T(8,128)(2,1)S(1)} %slice.281), channel_id=1, source_target_pairs={{0,6},{2,0},{4,2},{6,4},{1,7},{3,1},{5,3},{7,5},{8,14},{10,8},{12,... | collective-permute-start | bytes 589832 | tf_op jit(solution)/shard_map/ppermute | solution.py:23
  52.7 2.4 %collective-permute-start.6 = (bf16[96,2048]{1,0:T(8,128)(2,1)S(1)}, bf16[96,2048]{1,0:T(8,128)(2,1)S(1)}, u32[]{:S(2)}, u32[]{:S(2)}) collective-permute-start(bf16[96,2048]{1,0:T(8,128)(2,1)S(1)} %collective-permute-done.4), channel_id=1, source_target_pairs={{0,1},{1,0},{2,3},{3,2},{4,5},{5,4},{6,7},{7,6},{8,9},{9,8},{10,11... | collective-permute-start | bytes 1179656 | tf_op jit(solution)/shard_map/ppermute | solution.py:27
  63.4 12.3 %all-to-all-start = ((f32[64,1,288]{2,1,0:T(1,128)}), f32[64,1,288]{2,1,0:T(1,128)S(1)}, u32[]{:S(2)}, u32[]{:S(2)}) async-start(f32[64,1,288]{2,1,0:T(1,128)} %broadcast_in_dim.70), calls=%async_computation | async-start | bytes 196608 | tf_op jit(solution)/shard_map/all_to_all | solution.py:40
  76.4 13.8 %all-to-all-done = f32[64,1,288]{2,1,0:T(1,128)S(1)} async-done(((f32[64,1,288]{2,1,0:T(1,128)}), f32[64,1,288]{2,1,0:T(1,128)S(1)}, u32[]{:S(2)}, u32[]{:S(2)}) %all-to-all-start) | async-done | bytes 73760 | tf_op jit(solution)/shard_map/all_to_all | solution.py:40
  90.7 2.6 %convolution_convert_fusion = bf16[384,2048]{1,0:T(8,128)(2,1)} fusion(bf16[96,384]{1,0:T(8,128)(2,1)} %select_n.69, bf16[96,2048]{1,0:T(8,128)(2,1)S(1)} %subtract_convert_fusion), kind=kOutput, calls=%fused_computation.1 | convolution fusion | flops 151781376 | bytes 2039808 | tf_op jit(solution)/shard_map/dot_general | solution.py:166
  95.4 3.6 %collective-permute-done.10 = bf16[384,2048]{1,0:T(8,128)(2,1)} collective-permute-done((bf16[384,2048]{1,0:T(8,128)(2,1)}, bf16[384,2048]{1,0:T(8,128)(2,1)}, u32[]{:S(2)}, u32[]{:S(2)}) %collective-permute-start.10) | collective-permute-done | bytes 1572896 | tf_op jit(solution)/shard_map/ppermute | solution.py:27
  99.0 2.0 %convert_add_fusion = f32[384,2048]{1,0:T(8,128)S(1)} fusion(bf16[384,2048]{1,0:T(8,128)(2,1)} %collective-permute-done.10, bf16[96,384]{1,0:T(8,128)(2,1)S(1)} %select_n.65, bf16[96,2048]{1,0:T(8,128)(2,1)S(1)} %subtract_convert_fusion), kind=kOutput, calls=%fused_computation | convolution fusion | flops 154140672 | bytes 5185536 | tf_op jit(solution)/shard_map/dot_general | solution.py:167
  105.3 3.5 %collective-permute-start.12 = (bf16[48,2048]{1,0:T(8,128)(2,1)}, bf16[48,2048]{1,0:T(8,128)(2,1)}, u32[]{:S(2)}, u32[]{:S(2)}) collective-permute-start(bf16[48,2048]{1,0:T(8,128)(2,1)} %get-tuple-element.38), channel_id=1, source_target_pairs={{0,6},{2,0},{4,2},{6,4},{1,7},{3,1},{5,3},{7,5},{8,14},{10,8},{12,... | collective-permute-start | bytes 589832 | tf_op jit(solution)/shard_map/ppermute | solution.py:23
  108.9 2.3 %collective-permute-start.11 = (bf16[48,2048]{1,0:T(8,128)(2,1)S(1)}, bf16[48,2048]{1,0:T(8,128)(2,1)}, u32[]{:S(2)}, u32[]{:S(2)}) collective-permute-start(bf16[48,2048]{1,0:T(8,128)(2,1)S(1)} %get-tuple-element.40), channel_id=1, source_target_pairs={{0,2},{2,4},{4,6},{6,0},{1,3},{3,5},{5,7},{7,1},{8,10},{10,12},{12... | collective-permute-start | bytes 589832 | tf_op jit(solution)/shard_map/ppermute | solution.py:23
  112.2 2.2 %collective-permute-done.12 = bf16[48,2048]{1,0:T(8,128)(2,1)} collective-permute-done((bf16[48,2048]{1,0:T(8,128)(2,1)}, bf16[48,2048]{1,0:T(8,128)(2,1)}, u32[]{:S(2)}, u32[]{:S(2)}) %collective-permute-start.12) | collective-permute-done | bytes 196640 | tf_op jit(solution)/shard_map/ppermute | solution.py:23
  114.5 4.3 %collective-permute-done.11 = bf16[48,2048]{1,0:T(8,128)(2,1)} collective-permute-done((bf16[48,2048]{1,0:T(8,128)(2,1)S(1)}, bf16[48,2048]{1,0:T(8,128)(2,1)}, u32[]{:S(2)}, u32[]{:S(2)}) %collective-permute-start.11) | collective-permute-done | bytes 196640 | tf_op jit(solution)/shard_map/ppermute | solution.py:23
  123.5 3.9 %collective-permute-start.13 = (bf16[96,2048]{1,0:T(8,128)(2,1)}, bf16[96,2048]{1,0:T(8,128)(2,1)}, u32[]{:S(2)}, u32[]{:S(2)}) collective-permute-start(bf16[96,2048]{1,0:T(8,128)(2,1)} %pad_maximum_fusion.4), channel_id=1, source_target_pairs={{0,2},{2,4},{4,6},{6,0},{1,3},{3,5},{5,7},{7,1},{8,10},{10,12},{12... | collective-permute-start | bytes 1179656 | tf_op jit(solution)/shard_map/ppermute | solution.py:23
  128.9 6.3 %all-to-all-start.1 = ((f32[64,1,1152]{2,1,0:T(1,128)}), f32[64,1,1152]{2,1,0:T(1,128)S(1)}, u32[]{:S(2)}, u32[]{:S(2)}) async-start(f32[64,1,1152]{2,1,0:T(1,128)} %copy.74), calls=%async_computation.1 | async-start | bytes 589824 | tf_op jit(solution)/shard_map/all_to_all | solution.py:186
  140.2 15.8 %all-to-all-done.1 = f32[64,1,1152]{2,1,0:T(1,128)S(1)} async-done(((f32[64,1,1152]{2,1,0:T(1,128)}), f32[64,1,1152]{2,1,0:T(1,128)S(1)}, u32[]{:S(2)}, u32[]{:S(2)}) %all-to-all-start.1) | async-done | bytes 294944 | tf_op jit(solution)/shard_map/all_to_all | solution.py:186
  158.5 6.6 %all-to-all-start.2 = ((bf16[64,2,1152]{2,1,0:T(2,128)(2,1)}), bf16[64,2,1152]{2,1,0:T(2,128)(2,1)S(1)}, u32[]{:S(2)}, u32[]{:S(2)}) async-start(bf16[64,2,1152]{2,1,0:T(2,128)(2,1)} %reshape.178), calls=%async_computation.2 | async-start | bytes 589824 | tf_op jit(solution)/shard_map/all_to_all | solution.py:206
  165.4 20.3 %all-to-all-done.2 = bf16[64,2,1152]{2,1,0:T(2,128)(2,1)S(1)} async-done(((bf16[64,2,1152]{2,1,0:T(2,128)(2,1)}), bf16[64,2,1152]{2,1,0:T(2,128)(2,1)S(1)}, u32[]{:S(2)}, u32[]{:S(2)}) %all-to-all-start.2) | async-done | bytes 294944 | tf_op jit(solution)/shard_map/all_to_all | solution.py:206
  (112 shorter events, 44.4 us)
Async XLA Ops:
  0.6 20.1 %copy-start = (bf16[96,2048]{1,0:T(8,128)(2,1)S(1)}, bf16[96,2048]{1,0:T(8,128)(2,1)}, u32[]{:S(2)}) copy-start(bf16[96,2048]{1,0:T(8,128)(2,1)} %cells.1) | copy-start | bytes 1179652
  0.6 19.9 %copy-start.4 = (f32[96,2048]{1,0:T(8,128)S(1)}, f32[96,2048]{1,0:T(8,128)}, u32[]{:S(2)}) copy-start(f32[96,2048]{1,0:T(8,128)} %param.7) | copy-start | bytes 2359300
  1.6 19.1 %collective-permute-start = (bf16[96,2]{1,0:T(8,128)(2,1)S(1)}, bf16[96,2]{1,0:T(8,128)(2,1)S(1)}, u32[]{:S(2)}, u32[]{:S(2)}) collective-permute-start(bf16[96,2]{1,0:T(8,128)(2,1)S(1)} %get-tuple-element.44), channel_id=1, source_target_pairs={{0,8},{8,16},{16,24},{24,32},{32,40},{40,48},{48,56},{56,64},{64,7... | collective-permute-start | bytes 1160 | tf_op jit(solution)/shard_map/ppermute | solution.py:32
  5.4 15.3 %collective-permute-start.1 = (bf16[96,2]{1,0:T(8,128)(2,1)S(1)}, bf16[96,2]{1,0:T(8,128)(2,1)S(1)}, u32[]{:S(2)}, u32[]{:S(2)}) collective-permute-start(bf16[96,2]{1,0:T(8,128)(2,1)S(1)} %get-tuple-element.43), channel_id=1, source_target_pairs={{8,0},{16,8},{24,16},{32,24},{40,32},{48,40},{56,48},{64,56},{72,6... | collective-permute-start | bytes 1160 | tf_op jit(solution)/shard_map/ppermute | solution.py:33
  22.4 32.7 %collective-permute-start.2 = (bf16[96,2048]{1,0:T(8,128)(2,1)S(1)}, bf16[96,2048]{1,0:T(8,128)(2,1)}, u32[]{:S(2)}, u32[]{:S(2)}) collective-permute-start(bf16[96,2048]{1,0:T(8,128)(2,1)S(1)} %get-tuple-element.9), channel_id=1, source_target_pairs={{0,1},{1,0},{2,3},{3,2},{4,5},{5,4},{6,7},{7,6},{8,9},{9,8},{10,11... | collective-permute-start | bytes 1179656 | tf_op jit(solution)/shard_map/ppermute | solution.py:27
  24.4 21.2 %collective-permute-start.3 = (bf16[96,2048]{1,0:T(8,128)(2,1)S(1)}, bf16[96,2048]{1,0:T(8,128)(2,1)S(1)}, u32[]{:S(2)}, u32[]{:S(2)}) collective-permute-start(bf16[96,2048]{1,0:T(8,128)(2,1)S(1)} %get-tuple-element.9), channel_id=1, source_target_pairs={{0,6},{2,0},{4,2},{6,4},{1,7},{3,1},{5,3},{7,5},{8,14},{10,8},{12,... | collective-permute-start | bytes 1179656 | tf_op jit(solution)/shard_map/ppermute | solution.py:23
  29.3 14.3 %collective-permute-start.4 = (bf16[96,2048]{1,0:T(8,128)(2,1)S(1)}, bf16[96,2048]{1,0:T(8,128)(2,1)S(1)}, u32[]{:S(2)}, u32[]{:S(2)}) collective-permute-start(bf16[96,2048]{1,0:T(8,128)(2,1)S(1)} %get-tuple-element.9), channel_id=1, source_target_pairs={{0,2},{2,4},{4,6},{6,0},{1,3},{3,5},{5,7},{7,1},{8,10},{10,12},{12... | collective-permute-start | bytes 1179656 | tf_op jit(solution)/shard_map/ppermute | solution.py:23
  43.7 12.6 %collective-permute-start.7 = (bf16[48,2048]{1,0:T(8,128)(2,1)S(1)}, bf16[48,2048]{1,0:T(8,128)(2,1)S(1)}, u32[]{:S(2)}, u32[]{:S(2)}) collective-permute-start(bf16[48,2048]{1,0:T(8,128)(2,1)S(1)} %slice.280), channel_id=1, source_target_pairs={{0,2},{2,4},{4,6},{6,0},{1,3},{3,5},{5,7},{7,1},{8,10},{10,12},{12... | collective-permute-start | bytes 589832 | tf_op jit(solution)/shard_map/ppermute | solution.py:23
  45.6 10.6 %collective-permute-start.8 = (bf16[48,2048]{1,0:T(8,128)(2,1)S(1)}, bf16[48,2048]{1,0:T(8,128)(2,1)S(1)}, u32[]{:S(2)}, u32[]{:S(2)}) collective-permute-start(bf16[48,2048]{1,0:T(8,128)(2,1)S(1)} %slice.281), channel_id=1, source_target_pairs={{0,6},{2,0},{4,2},{6,4},{1,7},{3,1},{5,3},{7,5},{8,14},{10,8},{12,... | collective-permute-start | bytes 589832 | tf_op jit(solution)/shard_map/ppermute | solution.py:23
  50.8 7.4 %collective-permute-start.5 = (bf16[96,2048]{1,0:T(8,128)(2,1)S(1)}, bf16[96,2048]{1,0:T(8,128)(2,1)S(1)}, u32[]{:S(2)}, u32[]{:S(2)}) collective-permute-start(bf16[96,2048]{1,0:T(8,128)(2,1)S(1)} %collective-permute-done.3), channel_id=1, source_target_pairs={{0,1},{1,0},{2,3},{3,2},{4,5},{5,4},{6,7},{7,6},{8,9},{9,8},{10,11... | collective-permute-start | bytes 1179656 | tf_op jit(solution)/shard_map/ppermute | solution.py:27
  52.7 5.6 %collective-permute-start.6 = (bf16[96,2048]{1,0:T(8,128)(2,1)S(1)}, bf16[96,2048]{1,0:T(8,128)(2,1)S(1)}, u32[]{:S(2)}, u32[]{:S(2)}) collective-permute-start(bf16[96,2048]{1,0:T(8,128)(2,1)S(1)} %collective-permute-done.4), channel_id=1, source_target_pairs={{0,1},{1,0},{2,3},{3,2},{4,5},{5,4},{6,7},{7,6},{8,9},{9,8},{10,11... | collective-permute-start | bytes 1179656 | tf_op jit(solution)/shard_map/ppermute | solution.py:27
  56.3 3.6 %collective-permute-start.9 = (bf16[96,2048]{1,0:T(8,128)(2,1)S(1)}, bf16[96,2048]{1,0:T(8,128)(2,1)S(1)}, u32[]{:S(2)}, u32[]{:S(2)}) collective-permute-start(bf16[96,2048]{1,0:T(8,128)(2,1)S(1)} %pad_maximum_fusion.2), channel_id=1, source_target_pairs={{0,1},{1,0},{2,3},{3,2},{4,5},{5,4},{6,7},{7,6},{8,9},{9,8},{10,11... | collective-permute-start | bytes 1179656 | tf_op jit(solution)/shard_map/ppermute | solution.py:27
  58.3 17.4 %copy-start.5 = (bf16[96,4,96]{2,1,0:T(4,128)(2,1)S(1)}, bf16[96,4,96]{2,1,0:T(4,128)(2,1)}, u32[]{:S(2)}) copy-start(bf16[96,4,96]{2,1,0:T(4,128)(2,1)} %get-tuple-element.33) | copy-start | bytes 221188
  59.9 1.7 copy-start.2
  63.4 26.9 %all-to-all-start = ((f32[64,1,288]{2,1,0:T(1,128)}), f32[64,1,288]{2,1,0:T(1,128)S(1)}, u32[]{:S(2)}, u32[]{:S(2)}) async-start(f32[64,1,288]{2,1,0:T(1,128)} %broadcast_in_dim.70), calls=%async_computation | async-start | bytes 196608 | tf_op jit(solution)/shard_map/all_to_all | solution.py:40
  93.3 5.6 %collective-permute-start.10 = (bf16[384,2048]{1,0:T(8,128)(2,1)}, bf16[384,2048]{1,0:T(8,128)(2,1)}, u32[]{:S(2)}, u32[]{:S(2)}) collective-permute-start(bf16[384,2048]{1,0:T(8,128)(2,1)} %convolution_convert_fusion), channel_id=1, source_target_pairs={{0,1},{1,0},{2,3},{3,2},{4,5},{5,4},{6,7},{7,6},{8,9},{9,8},{10,11... | collective-permute-start | bytes 4718600 | tf_op jit(solution)/shard_map/ppermute | solution.py:27
  101.0 1.7 copy-start.1
  101.0 3.1 %copy-start.3 = (bf16[768,2048]{1,0:T(8,128)(2,1)S(1)}, bf16[768,2048]{1,0:T(8,128)(2,1)}, u32[]{:S(2)}) copy-start(bf16[768,2048]{1,0:T(8,128)(2,1)} %copy-done.2) | copy-start | bytes 9437188
  105.3 9.2 %collective-permute-start.12 = (bf16[48,2048]{1,0:T(8,128)(2,1)}, bf16[48,2048]{1,0:T(8,128)(2,1)}, u32[]{:S(2)}, u32[]{:S(2)}) collective-permute-start(bf16[48,2048]{1,0:T(8,128)(2,1)} %get-tuple-element.38), channel_id=1, source_target_pairs={{0,6},{2,0},{4,2},{6,4},{1,7},{3,1},{5,3},{7,5},{8,14},{10,8},{12,... | collective-permute-start | bytes 589832 | tf_op jit(solution)/shard_map/ppermute | solution.py:23
  108.9 9.9 %collective-permute-start.11 = (bf16[48,2048]{1,0:T(8,128)(2,1)S(1)}, bf16[48,2048]{1,0:T(8,128)(2,1)}, u32[]{:S(2)}, u32[]{:S(2)}) collective-permute-start(bf16[48,2048]{1,0:T(8,128)(2,1)S(1)} %get-tuple-element.40), channel_id=1, source_target_pairs={{0,2},{2,4},{4,6},{6,0},{1,3},{3,5},{5,7},{7,1},{8,10},{10,12},{12... | collective-permute-start | bytes 589832 | tf_op jit(solution)/shard_map/ppermute | solution.py:23
  121.6 13.6 %collective-permute-start.14 = (bf16[96,2048]{1,0:T(8,128)(2,1)}, bf16[96,2048]{1,0:T(8,128)(2,1)}, u32[]{:S(2)}, u32[]{:S(2)}) collective-permute-start(bf16[96,2048]{1,0:T(8,128)(2,1)} %pad_maximum_fusion.5), channel_id=1, source_target_pairs={{0,6},{2,0},{4,2},{6,4},{1,7},{3,1},{5,3},{7,5},{8,14},{10,8},{12,... | collective-permute-start | bytes 1179656 | tf_op jit(solution)/shard_map/ppermute | solution.py:23
  123.5 13.4 %collective-permute-start.13 = (bf16[96,2048]{1,0:T(8,128)(2,1)}, bf16[96,2048]{1,0:T(8,128)(2,1)}, u32[]{:S(2)}, u32[]{:S(2)}) collective-permute-start(bf16[96,2048]{1,0:T(8,128)(2,1)} %pad_maximum_fusion.4), channel_id=1, source_target_pairs={{0,2},{2,4},{4,6},{6,0},{1,3},{3,5},{5,7},{7,1},{8,10},{10,12},{12... | collective-permute-start | bytes 1179656 | tf_op jit(solution)/shard_map/ppermute | solution.py:23
  128.9 27.1 %all-to-all-start.1 = ((f32[64,1,1152]{2,1,0:T(1,128)}), f32[64,1,1152]{2,1,0:T(1,128)S(1)}, u32[]{:S(2)}, u32[]{:S(2)}) async-start(f32[64,1,1152]{2,1,0:T(1,128)} %copy.74), calls=%async_computation.1 | async-start | bytes 589824 | tf_op jit(solution)/shard_map/all_to_all | solution.py:186
  158.5 27.1 %all-to-all-start.2 = ((bf16[64,2,1152]{2,1,0:T(2,128)(2,1)}), bf16[64,2,1152]{2,1,0:T(2,128)(2,1)S(1)}, u32[]{:S(2)}, u32[]{:S(2)}) async-start(bf16[64,2,1152]{2,1,0:T(2,128)(2,1)} %reshape.178), calls=%async_computation.2 | async-start | bytes 589824 | tf_op jit(solution)/shard_map/all_to_all | solution.py:206

commit v4 on v3

v4 whole, which is shorter than its diff:
```python
import functools

import jax
import jax.numpy as jnp
import numpy as np
from jax import lax
from jax.experimental import pallas as pl
from jax.experimental.pallas import tpu as pltpu
from jax.sharding import Mesh
from jax.sharding import PartitionSpec as P

F32 = jnp.float32
BF16 = jnp.bfloat16
SEQ = ("x", "z")
LANES = 128


def along_y(value, shift):
    count = lax.axis_size("y")
    return lax.ppermute(value, "y", [(i, (i + shift) % count) for i in range(count)])


def other_core(value):
    return lax.ppermute(value, "c", [(0, 1), (1, 0)])


def outer_columns(cells, width):
    count = lax.axis_size(SEQ)
    left = lax.ppermute(cells[:, -width:], SEQ, [(i, i + 1) for i in range(count - 1)])
    right = lax.ppermute(cells[:, :width], SEQ, [(i + 1, i) for i in range(count - 1)])
    return left, right


def share(value, axes):
    count = lax.axis_size(axes)
    copies = jnp.broadcast_to(value.reshape(1, 1, -1), (count, 1, value.size))
    return lax.all_to_all(copies, axes, 0, 0, tiled=True)[:, 0]


def forward_kernel(cells, left, right, tap, hidden, slope, line):
    reach = left.shape[1]
    count = cells.shape[1]
    line[:, :LANES] = jnp.zeros((cells.shape[0], LANES), F32)
    line[:, LANES + count :] = jnp.zeros((cells.shape[0], LANES), F32)
    line[:, LANES - reach : LANES] = left[...].astype(F32)
    line[:, LANES + count : LANES + count + reach] = right[...].astype(F32)
    line[:, LANES : LANES + count] = cells[...].astype(F32)
    rows = 8

    @pl.loop(0, cells.shape[0] // 16)
    def _(block):
        both_hidden = []
        for part in range(2):
            at = pl.ds(pl.multiple_of(block * 16 + part * rows, rows), rows)
            whole = line[at, :]
            taps = tap[at, :]
            conv = jnp.zeros((rows, count), F32)
            for k in range(2 * reach + 1):
                shift = (reach - k) % whole.shape[1]
                moved = pltpu.roll(whole, shift, 1) if shift else whole
                conv = conv + taps[:, k : k + 1] * moved[:, LANES : LANES + count]
            sig = jax.nn.sigmoid(conv)
            both_hidden.append((conv * sig).astype(BF16))
            slope[at, :] = sig * (1.0 + conv * (1.0 - sig))
        out = pl.ds(pl.multiple_of(block * 16, 16), 16)
        hidden[out, :] = jnp.concatenate(both_hidden, axis=0)


def forward(cells, left, right, tap):
    rows, count = cells.shape
    return pl.pallas_call(
        forward_kernel,
        out_shape=(
            jax.ShapeDtypeStruct((rows, count), BF16),
            jax.ShapeDtypeStruct((rows, count), F32),
        ),
        scratch_shapes=[pltpu.VMEM((rows, count + 2 * LANES), F32)],
        compiler_params=pltpu.CompilerParams(vmem_limit_bytes=16 * 2**20),
        cost_estimate=pl.CostEstimate(
            flops=20 * rows * count, bytes_accessed=8 * rows * count, transcendentals=rows * count
        ),
        name="conv_silu",
    )(cells, left, right, tap)


def scatter_kernel(place, weight, grad, received, mine, one, two, three, total):
    width = mine.shape[0]
    chips = weight.shape[0] // width
    chunk = total.shape[1]
    for start in range(0, grad.shape[1], chunk):
        at = pl.ds(start, chunk)
        part = jnp.dot(weight[...], grad[:, at], preferred_element_type=F32)
        total[...] = part + received[:, at].astype(F32)
        for shift, out in enumerate((mine, one, two, three)):
            row = lax.rem(place[0] + shift, chips) * width
            out[:, at] = total[pl.ds(pl.multiple_of(row, 16), width), :].astype(out.dtype)


def scatter_blocks(place, weight, grad, received):
    features, tracks = weight.shape
    count = grad.shape[1]
    width = features // 4
    sent = jax.ShapeDtypeStruct((width, count), BF16)
    return pl.pallas_call(
        scatter_kernel,
        out_shape=(jax.ShapeDtypeStruct((width, count), F32), sent, sent, sent),
        in_specs=[pl.BlockSpec(memory_space=pltpu.SMEM)]
        + [pl.BlockSpec(memory_space=pltpu.VMEM)] * 3,
        scratch_shapes=[pltpu.VMEM((features, 512), F32)],
        compiler_params=pltpu.CompilerParams(vmem_limit_bytes=24 * 2**20),
        cost_estimate=pl.CostEstimate(
            flops=2 * features * tracks * count,
            bytes_accessed=5 * features * count,
            transcendentals=0,
        ),
        name="core_sum",
    )(place, weight, grad, received)


def outer_kernel(core, grad, mine, theirs, out, table):
    tracks = grad.shape[0]
    width = mine.shape[0] // 4
    along = (((1,), (1,)), ((), ()))
    for block, offset in ((mine, core[0]), (theirs, 1 - core[0])):
        part = lax.dot_general(block[...], grad[...], along, preferred_element_type=F32)
        for chip in range(4):
            row = (2 * chip + offset) * width
            at = pl.ds(pl.multiple_of(row, 16), width)
            table[at, :tracks] = part[chip * width : (chip + 1) * width]
    out[...] = table[...].T[:tracks]


def outer_product(core, grad, mine, theirs):
    tracks, count = grad.shape
    features = 2 * mine.shape[0]
    return pl.pallas_call(
        outer_kernel,
        out_shape=jax.ShapeDtypeStruct((tracks, features), F32),
        in_specs=[pl.BlockSpec(memory_space=pltpu.SMEM)]
        + [pl.BlockSpec(memory_space=pltpu.VMEM)] * 3,
        scratch_shapes=[pltpu.VMEM((features, LANES), F32)],
        compiler_params=pltpu.CompilerParams(vmem_limit_bytes=16 * 2**20),
        cost_estimate=pl.CostEstimate(
            flops=2 * features * tracks * count,
            bytes_accessed=2 * features * count,
            transcendentals=0,
        ),
        name="weight_part",
    )(core, grad, mine, theirs)


def backward_kernel(mine, one, two, three, slope, cells, left, right, grad, sums, line, table):
    reach = left.shape[1]
    count = cells.shape[1]
    rows = 16
    lane = lax.broadcasted_iota(jnp.int32, (rows, LANES), 1)
    line[:, :LANES] = jnp.zeros((rows, LANES), F32)
    line[:, LANES + count :] = jnp.zeros((rows, LANES), F32)

    @pl.loop(0, cells.shape[0] // rows)
    def _(block):
        at = pl.ds(pl.multiple_of(block * rows, rows), rows)
        total = mine[at, :] + one[at, :].astype(F32)
        total = total + two[at, :].astype(F32) + three[at, :].astype(F32)
        value = (total * slope[at, :]).astype(BF16)
        grad[at, :] = value
        value = value.astype(F32)
        line[:, LANES - reach : LANES] = left[at, :].astype(F32)
        line[:, LANES + count : LANES + count + reach] = right[at, :].astype(F32)
        line[:, LANES : LANES + count] = cells[at, :].astype(F32)
        whole = line[...]
        found = jnp.zeros((rows, LANES), F32)
        for k in range(2 * reach + 1):
            shift = (reach - k) % whole.shape[1]
            moved = pltpu.roll(whole, shift, 1) if shift else whole
            product = moved[:, LANES : LANES + count] * value
            found = jnp.where(lane == k, jnp.sum(product, axis=1, keepdims=True), found)
        table[at, :] = found

    sums[...] = table[...].T[: sums.shape[0]]


def backward(mine, parts, slope, cells, left, right):
    rows, count = cells.shape
    return pl.pallas_call(
        backward_kernel,
        out_shape=(
            jax.ShapeDtypeStruct((rows, count), BF16),
            jax.ShapeDtypeStruct((8, rows), F32),
        ),
        scratch_shapes=[
            pltpu.VMEM((16, count + 2 * LANES), F32),
            pltpu.VMEM((rows, LANES), F32),
        ],
        compiler_params=pltpu.CompilerParams(vmem_limit_bytes=16 * 2**20),
        cost_estimate=pl.CostEstimate(
            flops=20 * rows * count, bytes_accessed=18 * rows * count, transcendentals=0
        ),
        name="conv_grad",
    )(mine, *parts, slope, cells, left, right)


def shards(embeddings, taps, head_weight, targets):
    width = embeddings.shape[0]
    count = embeddings.shape[1]
    tracks = head_weight.shape[0]
    ntaps = taps.shape[0]
    reach = ntaps // 2
    y = lax.axis_index("y")
    c = lax.axis_index("c")
    ny = lax.axis_size("y")
    nseq = lax.axis_size(SEQ)
    me = lax.axis_index(SEQ)
    features = ny * 2 * width
    tap = taps.astype(F32)

    left, right = outer_columns(embeddings, reach)
    block, slope = forward(embeddings, left, right, jnp.pad(tap, ((0, 8 - ntaps), (0, 0))).T)

    mine = lax.all_to_all(
        jnp.broadcast_to(block[None], (ny, width, count)), "y", 0, 0, tiled=True
    ).reshape(ny * width, count)
    theirs = other_core(mine)
    late_weight, _ = lax.optimization_barrier((head_weight, block))
    blocks = late_weight.reshape(tracks, ny, 2, width)
    halves = blocks[:, :, 0].reshape(tracks, -1), blocks[:, :, 1].reshape(tracks, -1)
    first = jnp.where(c == 0, halves[0], halves[1])
    second = jnp.where(c == 0, halves[1], halves[0])

    logits = jnp.dot(first, mine, preferred_element_type=F32)
    logits = logits + jnp.dot(second, theirs, preferred_element_type=F32)
    top = jnp.max(logits, axis=1)
    expo = jnp.exp(logits - top[:, None])
    stats = jnp.concatenate([top, jnp.sum(expo, axis=1), jnp.sum(targets, axis=1)])
    every = share(stats, SEQ)
    tops = every[:, :tracks]
    peak = jnp.max(tops, axis=0)
    total = jnp.sum(every[:, tracks : 2 * tracks] * jnp.exp(tops - peak[None]), axis=0)
    counts = jnp.sum(every[:, 2 * tracks :], axis=0)
    scale = counts * jnp.exp(top - peak) / total
    logit_grad = (scale[:, None] * expo - targets).astype(BF16)

    sent = jnp.dot(second.T, logit_grad, preferred_element_type=F32).astype(BF16)
    received = other_core(sent)

    nx, nz = lax.axis_size("x"), lax.axis_size("z")
    late_grad, _ = lax.optimization_barrier((logit_grad, sent))
    local = outer_product(c.reshape(1), late_grad, mine, theirs)
    part = lax.all_to_all(local.reshape(nx, tracks // nx, features), "x", 0, 0, tiled=True)

    own, *blocks = scatter_blocks(y.reshape(1), first.T, logit_grad, received)
    parts = [along_y(block, shift) for shift, block in ((2, blocks[1]), (1, blocks[0]), (3, blocks[2]))]
    part = jnp.sum(part, axis=0).reshape(nz, 1, -1)
    part = jnp.sum(lax.all_to_all(part, "z", 0, 0, tiled=True), axis=0).reshape(-1)

    conv_grad, local_taps = backward(own, parts, slope, embeddings, left, right)
    local_taps = local_taps[:ntaps].reshape(-1)
    high = lax.reduce_precision(local_taps, 8, 7)
    low = local_taps - high
    row = jnp.arange(nseq)[:, None]
    head = conv_grad[:, :reach].T.reshape(1, -1)
    tail = conv_grad[:, -reach:].T.reshape(1, -1)
    zero = jnp.zeros((), BF16)
    edge = jnp.where(row == me + 1, tail, jnp.where(row == me - 1, head, zero))
    both = jnp.concatenate([high, low]).astype(BF16)
    both = jnp.broadcast_to(both[None], (nseq, both.size))
    same = jnp.broadcast_to(part.astype(BF16)[None], (nseq, part.size))
    message = jnp.stack([same, jnp.concatenate([both, edge], axis=1)], axis=1)
    slab = lax.all_to_all(message, SEQ, 0, 0, tiled=True)
    weight_grad = slab[:, 0].reshape(tracks, features).astype(F32)
    sums = jnp.sum(slab[:, 1, : both.shape[1]].astype(F32), axis=0).reshape(2, ntaps, width)
    taps_grad = sums[0] + sums[1]
    edges = slab[:, 1, both.shape[1] :]
    before = jnp.sum(jnp.where(row == me - 1, edges, zero).astype(F32), axis=0)
    after = jnp.sum(jnp.where(row == me + 1, edges, zero).astype(F32), axis=0)

    grad_pad = jnp.concatenate(
        [before.reshape(reach, width).T, conv_grad.astype(F32), after.reshape(reach, width).T], axis=1
    )
    embed_grad = jnp.zeros((width, count), F32)
    for k in range(ntaps):
        start = 2 * reach - k
        embed_grad = embed_grad + tap[k][:, None] * grad_pad[:, start : start + count]
    return embed_grad.astype(BF16), weight_grad, taps_grad


def solution(mesh):
    fine = Mesh(np.asarray(mesh.devices).reshape(4, 16, 4, 2), ("x", "z", "y", "c"))
    track = ("y", "c")
    return jax.shard_map(
        shards,
        mesh=fine,
        in_specs=(P(track, SEQ), P(None, track), P(track, None), P(track, SEQ)),
        out_specs=(P(track, SEQ), P(track, None), P(None, track)),
        check_vma=False,
    )
```

time: 191 us -> 160 us (0.84)
  blocking collectives: 0 us -> 46.8 us
  waiting for transfers between devices: 74 us -> 37.5 us
  starting transfers between devices: 74.4 us -> 42.2 us
  other arithmetic: 12.9 us -> 5.6 us
  Pallas kernels: 1.7 us -> 7.75 us
  matrix products: 6.46 us -> 2.65 us
  local copies, waits for them, and re-layouts: 19.2 us -> 15.7 us
    all_to_all x0 -> x2, blocking collectives: none -> 46.8 us  [the longest x1 23.7 us: shards(): lax.all_to_all(jnp.broadcast_to(block[None], (ny, width, count)), 'y', 0,...]
    ppermute x8 -> x3, waiting for transfers between devices: 19 us -> 0.01 us  [along_y(): lax.ppermute(value, 'y', [(i, (i + shift) % count) for i in range(count)])]
    all_to_all x3, waiting for transfers between devices: 49.9 us -> 33 us  [the longest x1 20.2 us: shards(): slab = lax.all_to_all(message, SEQ, 0, 0, tiled=True)]
    ppermute x8 -> x3, starting transfers between devices: 25.6 us -> 9.77 us  [along_y(): lax.ppermute(value, 'y', [(i, (i + shift) % count) for i in range(count)])]
    all_to_all x3, starting transfers between devices: 25.1 us -> 15 us  [the longest x1 6.66 us: shards(): slab = lax.all_to_all(message, SEQ, 0, 0, tiled=True)]
    ppermute x5 -> x2, starting transfers between devices: 10.1 us -> 3.82 us  [other_core(): return lax.ppermute(value, 'c', [(0, 1), (1, 0)])]
    pallas_call x0 -> x3, Pallas kernels: none -> 6.04 us  [the longest x1 3.2 us: scatter_blocks(): pl.pallas_call(scatter_kernel, out_shape=(jax.ShapeDtypeStruct((width, co...]
    ppermute x5 -> x2, waiting for transfers between devices: 5.12 us -> 0.01 us  [other_core(): return lax.ppermute(value, 'c', [(0, 1), (1, 0)])]
  transfers between devices with their start and end apart: 18 -> 10, of which waited for: 9 -> 3; matrix products, arithmetic and copies ran while one was open for 8% -> 4% of each run, Pallas kernels for 0% -> 3%
where the time goes in v4:
time: 160 us; the launch traced here: 159 us
  blocking collectives  46.8 us (29%)
  starting transfers between devices  42.2 us (26%)
  waiting for transfers between devices  37.5 us (23%)
  local copies, waits for them, and re-layouts  15.7 us (10%)
  Pallas kernels  7.75 us (5%)
  other arithmetic  5.6 us (4%)
  matrix products  2.65 us (2%)
    all_to_all x1, blocking collectives, shards(): lax.all_to_all(jnp.broadcast_to(block[None], (ny, width, count)), 'y', 0,...  23.7 us
    all_to_all x1, blocking collectives, share(): return lax.all_to_all(copies, axes, 0, 0, tiled=True)[:, 0]  23.1 us
    all_to_all x1, waiting for transfers between devices, shards(): slab = lax.all_to_all(message, SEQ, 0, 0, tiled=True)  20.2 us
    all_to_all x1, waiting for transfers between devices, shards(): lax.all_to_all(part, 'z', 0, 0, tiled=True)  12.9 us
    ppermute x1, starting transfers between devices, outer_columns(): lax.ppermute(cells[:, :width], SEQ, [(i + 1, i) for i in range(count - 1)])  11.7 us
    ppermute x3, starting transfers between devices, along_y(): lax.ppermute(value, 'y', [(i, (i + shift) % count) for i in range(count)])  9.77 us
    unnamed x34, local copies, waits for them, and re-layouts  8.87 us
    all_to_all x1, starting transfers between devices, shards(): slab = lax.all_to_all(message, SEQ, 0, 0, tiled=True)  6.66 us
  transfers between devices with their start and end apart: 10, of which 3 were waited for; matrix products, arithmetic and copies ran while one was open for 4% of the time, Pallas kernels for 3%

profile of v4, /device:TPU:6, one launch (start us, length us, event | category | flops | bytes accessed | tf_op | source)
XLA Modules:
  0.0 159.2 jit_solution(5771978152068337974)
XLA Ops:
  1.5 11.7 %collective-permute-start.1 = (bf16[96,2]{1,0:T(8,128)(2,1)S(1)}, bf16[96,2]{1,0:T(8,128)(2,1)S(1)}, u32[]{:S(2)}, u32[]{:S(2)}) collective-permute-start(bf16[96,2]{1,0:T(8,128)(2,1)S(1)} %get-tuple-element.34), channel_id=1, source_target_pairs={{8,0},{16,8},{24,16},{32,24},{40,32},{48,40},{56,48},{64,56},{72,6... | collective-permute-start | bytes 1160 | tf_op jit(solution)/shard_map/ppermute | solution.py:30
  13.1 1.9 %collective-permute-start = (bf16[96,2]{1,0:T(8,128)(2,1)S(1)}, bf16[96,2]{1,0:T(8,128)(2,1)S(1)}, u32[]{:S(2)}, u32[]{:S(2)}) collective-permute-start(bf16[96,2]{1,0:T(8,128)(2,1)S(1)} %get-tuple-element.35), channel_id=1, source_target_pairs={{0,8},{8,16},{16,24},{24,32},{32,40},{40,48},{48,56},{56,64},{64,7... | collective-permute-start | bytes 1160 | tf_op jit(solution)/shard_map/ppermute | solution.py:29
  16.5 4.5 %collective-permute-done.left = bf16[96,2]{1,0:T(8,128)(2,1)S(1)} collective-permute-done((bf16[96,2]{1,0:T(8,128)(2,1)S(1)}, bf16[96,2]{1,0:T(8,128)(2,1)S(1)}, u32[]{:S(2)}, u32[]{:S(2)}) %collective-permute-start) | collective-permute-done | bytes 416 | tf_op jit(solution)/shard_map/ppermute | solution.py:29
  22.0 1.7 %conv_silu.1 = (bf16[96,2048]{1,0:T(8,128)(2,1)S(1)}, f32[96,2048]{1,0:T(8,128)S(1)}) custom-call(bf16[96,2048]{1,0:T(8,128)(2,1)S(1)} %copy-done, bf16[96,2]{1,0:T(8,128)(2,1)S(1)} %collective-permute-done.left, bf16[96,2]{1,0:T(8,128)(2,1)S(1)} %collective-permute-done.1.right, f32[96,8]{1,0:T(8,128)S(1)} %pad_bitcast_fusion.tap), custom_call_target="tpu_custom_call" | custom-call | flops 3932160 | bytes 1572864 | tf_op jit(solution)/shard_map/conv_silu/pallas_call | solution.py:71
  24.8 23.7 %all_to_all.25 = bf16[4,96,2048]{2,1,0:T(8,128)(2,1)S(1)} all-to-all(bf16[4,96,2048]{2,1,0:T(8,128)(2,1)S(1)} %broadcast_in_dim.74), channel_id=1, replica_groups=mesh['x'=4,'z'=16,'y'=4,'c'=2] {'y'}, dimensions={0} | all-to-all | bytes 3145728 | tf_op jit(solution)/shard_map/all_to_all | solution.py:220
  48.4 1.9 %collective-permute-start.2 = (bf16[384,2048]{1,0:T(8,128)(2,1)S(1)}, bf16[384,2048]{1,0:T(8,128)(2,1)S(1)}, u32[]{:S(2)}, u32[]{:S(2)}) collective-permute-start(bf16[384,2048]{1,0:T(8,128)(2,1)S(1)} %bitcast.34), channel_id=1, source_target_pairs={{0,1},{1,0},{2,3},{3,2},{4,5},{5,4},{6,7},{7,6},{8,9},{9,8},{10,11... | collective-permute-start | bytes 4718600 | tf_op jit(solution)/shard_map/ppermute | solution.py:24
  50.4 1.3 reduce_sum.82
  52.8 1.1 copy.54
  55.7 23.1 %all_to_all.26 = f32[64,1,288]{2,1,0:T(1,128)S(1)} all-to-all(f32[64,1,288]{2,1,0:T(1,128)S(1)} %broadcast_in_dim.75), channel_id=1, replica_groups=mesh['x'=4,'z'=16,'y'=4,'c'=2] {'x','z'}, dimensions={0} | all-to-all | bytes 147456 | tf_op jit(solution)/shard_map/all_to_all | solution.py:37
  79.2 1.7 %convolution_convert_fusion = bf16[384,2048]{1,0:T(8,128)(2,1)} fusion(bf16[96,384]{0,1:T(8,128)(2,1)S(1)} %bitcast.42, bf16[96,2048]{1,0:T(8,128)(2,1)S(1)} %subtract_convert_fusion.grad), kind=kOutput, calls=%fused_computation | convolution fusion | flops 151781376 | bytes 2039808 | tf_op jit(solution)/shard_map/dot_general | solution.py:243
  80.9 1.9 %collective-permute-start.3 = (bf16[384,2048]{1,0:T(8,128)(2,1)}, bf16[384,2048]{1,0:T(8,128)(2,1)}, u32[]{:S(2)}, u32[]{:S(2)}) collective-permute-start(bf16[384,2048]{1,0:T(8,128)(2,1)} %convolution_convert_fusion), channel_id=1, source_target_pairs={{0,1},{1,0},{2,3},{3,2},{4,5},{5,4},{6,7},{7,6},{8,9},{9,8},{10,11... | collective-permute-start | bytes 4718600 | tf_op jit(solution)/shard_map/ppermute | solution.py:24
  82.8 1.1 weight_part.1
  84.6 4.8 %all-to-all-start.2 = ((f32[4,24,768]{2,1,0:T(8,128)}), f32[4,24,768]{2,1,0:T(8,128)S(1)}, u32[]{:S(2)}, u32[]{:S(2)}) async-start(f32[4,24,768]{2,1,0:T(8,128)} %bitcast.37), calls=%async_computation.2 | async-start | bytes 589824 | tf_op jit(solution)/shard_map/all_to_all | solution.py:249
  90.4 3.2 %core_sum.1 = (f32[96,2048]{1,0:T(8,128)S(1)}, bf16[96,2048]{1,0:T(8,128)(2,1)S(1)}, bf16[96,2048]{1,0:T(8,128)(2,1)}, bf16[96,2048]{1,0:T(8,128)(2,1)}) custom-call(s32[1]{0:T(128)} %bitcast.place, bf16[384,96]{1,0:T(8,128)(2,1)S(1)} %bitcast.39, bf16[96,2048]{1,0:T(8,128)(2,1)S(1)} %subtract_convert_fusion.grad, ...), custom_call_target="tpu_custom_call" | custom-call | flops 150994944 | bytes 3932160 | tf_op jit(solution)/shard_map/core_sum/pallas_call | solution.py:104
  93.6 2.7 %collective-permute-start.4 = (bf16[96,2048]{1,0:T(8,128)(2,1)}, bf16[96,2048]{1,0:T(8,128)(2,1)S(1)}, u32[]{:S(2)}, u32[]{:S(2)}) collective-permute-start(bf16[96,2048]{1,0:T(8,128)(2,1)} %get-tuple-element.16), channel_id=1, source_target_pairs={{0,4},{2,6},{4,0},{6,2},{1,5},{3,7},{5,1},{7,3},{8,12},{10,14},{12... | collective-permute-start | bytes 1179656 | tf_op jit(solution)/shard_map/ppermute | solution.py:20
  96.3 3.1 %collective-permute-start.5 = (bf16[96,2048]{1,0:T(8,128)(2,1)S(1)}, bf16[96,2048]{1,0:T(8,128)(2,1)S(1)}, u32[]{:S(2)}, u32[]{:S(2)}) collective-permute-start(bf16[96,2048]{1,0:T(8,128)(2,1)S(1)} %get-tuple-element.17), channel_id=1, source_target_pairs={{0,2},{2,4},{4,6},{6,0},{1,3},{3,5},{5,7},{7,1},{8,10},{10,12},{12... | collective-permute-start | bytes 1179656 | tf_op jit(solution)/shard_map/ppermute | solution.py:20
  99.4 3.9 %collective-permute-start.6 = (bf16[96,2048]{1,0:T(8,128)(2,1)}, bf16[96,2048]{1,0:T(8,128)(2,1)S(1)}, u32[]{:S(2)}, u32[]{:S(2)}) collective-permute-start(bf16[96,2048]{1,0:T(8,128)(2,1)} %get-tuple-element.18), channel_id=1, source_target_pairs={{0,6},{2,0},{4,2},{6,4},{1,7},{3,1},{5,3},{7,5},{8,14},{10,8},{12,... | collective-permute-start | bytes 1179656 | tf_op jit(solution)/shard_map/ppermute | solution.py:20
  104.1 3.6 %all-to-all-start.3 = ((f32[16,1,1152]{2,1,0:T(1,128)}), f32[16,1,1152]{2,1,0:T(1,128)S(1)}, u32[]{:S(2)}, u32[]{:S(2)}) async-start(f32[16,1,1152]{2,1,0:T(1,128)} %reshape.124), calls=%async_computation.3 | async-start | bytes 147456 | tf_op jit(solution)/shard_map/all_to_all | solution.py:254
  107.7 12.9 %all-to-all-done.3 = f32[16,1,1152]{2,1,0:T(1,128)S(1)} async-done(((f32[16,1,1152]{2,1,0:T(1,128)}), f32[16,1,1152]{2,1,0:T(1,128)S(1)}, u32[]{:S(2)}, u32[]{:S(2)}) %all-to-all-start.3) | async-done | bytes 73760 | tf_op jit(solution)/shard_map/all_to_all | solution.py:254
  120.7 1.1 copy-done.6
  123.3 1.7 %conv_grad.1 = (bf16[96,2048]{1,0:T(8,128)(2,1)S(1)}, f32[8,96]{1,0:T(8,128)S(1)}) custom-call(f32[96,2048]{1,0:T(8,128)S(1)} %get-tuple-element.15.mine, bf16[96,2048]{1,0:T(8,128)(2,1)S(1)} %collective-permute-done.4.one, bf16[96,2048]{1,0:T(8,128)(2,1)S(1)} %collective-permute-done.5.two, bf16[96,2048]{1,0:T(8,128)(2,1)S(1)} %collective-permute-done.6.three, ...), custom_call_target="tpu_custom_call" | custom-call | flops 3932160 | bytes 3538944 | tf_op jit(solution)/shard_map/conv_grad/pallas_call | solution.py:185
  126.9 6.7 %all-to-all-start.4 = ((bf16[64,2,1152]{2,1,0:T(2,128)(2,1)}), bf16[64,2,1152]{2,1,0:T(2,128)(2,1)S(1)}, u32[]{:S(2)}, u32[]{:S(2)}) async-start(bf16[64,2,1152]{2,1,0:T(2,128)(2,1)} %copy.48), calls=%async_computation.4 | async-start | bytes 589824 | tf_op jit(solution)/shard_map/all_to_all | solution.py:269
  133.9 20.2 %all-to-all-done.4 = bf16[64,2,1152]{2,1,0:T(2,128)(2,1)S(1)} async-done(((bf16[64,2,1152]{2,1,0:T(2,128)(2,1)}), bf16[64,2,1152]{2,1,0:T(2,128)(2,1)S(1)}, u32[]{:S(2)}, u32[]{:S(2)}) %all-to-all-start.4) | async-done | bytes 294944 | tf_op jit(solution)/shard_map/all_to_all | solution.py:269
  157.4 1.8 %fusion.4 = bf16[96,2048]{1,0:T(8,128)(2,1)} fusion(f32[96,2]{1,0:T(8,128)S(1)} %bitcast.45, f32[96,2048]{1,0:T(8,128)S(1)} %convert_element_type.44, f32[96,2]{1,0:T(8,128)S(1)} %bitcast.46, f32[96]{0:T(128)S(1)} %get-tuple-element.28, f32[96]{0:T(128)S(1)} %get-tuple-element.29, f32[96]{0:T(128)S(1)} %get-tuple-element.30, f32[96]{0:T(128)S(1)} %get-tuple-element.31, ...), kind=kLoop, calls=%fused_computation.10 | loop fusion | flops 2752512 | bytes 1183104 | tf_op jit(solution)/shard_map/convert_element_type | solution.py:284
  (85 shorter events, 17.0 us)
Async XLA Ops:
  1.5 14.4 %collective-permute-start.1 = (bf16[96,2]{1,0:T(8,128)(2,1)S(1)}, bf16[96,2]{1,0:T(8,128)(2,1)S(1)}, u32[]{:S(2)}, u32[]{:S(2)}) collective-permute-start(bf16[96,2]{1,0:T(8,128)(2,1)S(1)} %get-tuple-element.34), channel_id=1, source_target_pairs={{8,0},{16,8},{24,16},{32,24},{40,32},{48,40},{56,48},{64,56},{72,6... | collective-permute-start | bytes 1160 | tf_op jit(solution)/shard_map/ppermute | solution.py:30
  13.1 7.8 %collective-permute-start = (bf16[96,2]{1,0:T(8,128)(2,1)S(1)}, bf16[96,2]{1,0:T(8,128)(2,1)S(1)}, u32[]{:S(2)}, u32[]{:S(2)}) collective-permute-start(bf16[96,2]{1,0:T(8,128)(2,1)S(1)} %get-tuple-element.35), channel_id=1, source_target_pairs={{0,8},{8,16},{16,24},{24,32},{32,40},{40,48},{48,56},{56,64},{64,7... | collective-permute-start | bytes 1160 | tf_op jit(solution)/shard_map/ppermute | solution.py:29
  16.5 8.1 %copy-start.7 = (bf16[96,2]{1,0:T(8,128)(2,1)}, bf16[96,2]{1,0:T(8,128)(2,1)S(1)}, u32[]{:S(2)}) copy-start(bf16[96,2]{1,0:T(8,128)(2,1)S(1)} %collective-permute-done.1.right) | copy-start | bytes 1156
  21.0 1.0 copy-start
  22.0 2.6 %copy-start.9 = (bf16[96,2]{1,0:T(8,128)(2,1)}, bf16[96,2]{1,0:T(8,128)(2,1)S(1)}, u32[]{:S(2)}) copy-start(bf16[96,2]{1,0:T(8,128)(2,1)S(1)} %collective-permute-done.left) | copy-start | bytes 1156
  23.7 0.9 copy-start.5
  24.7 26.9 %copy-start.14 = (bf16[96,768]{1,0:T(8,128)(2,1)S(1)}, bf16[96,768]{1,0:T(8,128)(2,1)}, u32[]{:S(2)}) copy-start(bf16[96,768]{1,0:T(8,128)(2,1)} %param.6) | copy-start | bytes 442372
  48.4 6.1 %collective-permute-start.2 = (bf16[384,2048]{1,0:T(8,128)(2,1)S(1)}, bf16[384,2048]{1,0:T(8,128)(2,1)S(1)}, u32[]{:S(2)}, u32[]{:S(2)}) collective-permute-start(bf16[384,2048]{1,0:T(8,128)(2,1)S(1)} %bitcast.34), channel_id=1, source_target_pairs={{0,1},{1,0},{2,3},{3,2},{4,5},{5,4},{6,7},{7,6},{8,9},{9,8},{10,11... | collective-permute-start | bytes 4718600 | tf_op jit(solution)/shard_map/ppermute | solution.py:24
  54.1 0.6 copy-start.3
  54.7 24.2 %copy-start.11 = (f32[96,2048]{1,0:T(8,128)S(1)}, f32[96,2048]{1,0:T(8,128)}, u32[]{:S(2)}) copy-start(f32[96,2048]{1,0:T(8,128)} %param.7) | copy-start | bytes 2359300
  80.9 8.6 %collective-permute-start.3 = (bf16[384,2048]{1,0:T(8,128)(2,1)}, bf16[384,2048]{1,0:T(8,128)(2,1)}, u32[]{:S(2)}, u32[]{:S(2)}) collective-permute-start(bf16[384,2048]{1,0:T(8,128)(2,1)} %convolution_convert_fusion), channel_id=1, source_target_pairs={{0,1},{1,0},{2,3},{3,2},{4,5},{5,4},{6,7},{7,6},{8,9},{9,8},{10,11... | collective-permute-start | bytes 4718600 | tf_op jit(solution)/shard_map/ppermute | solution.py:24
  83.9 0.7 copy-start.2
  84.6 36.0 %copy-start.1 = (bf16[96,2048]{1,0:T(8,128)(2,1)S(1)}, bf16[96,2048]{1,0:T(8,128)(2,1)}, u32[]{:S(2)}) copy-start(bf16[96,2048]{1,0:T(8,128)(2,1)} %cells.3) | copy-start | bytes 1179652
  84.6 18.7 %all-to-all-start.2 = ((f32[4,24,768]{2,1,0:T(8,128)}), f32[4,24,768]{2,1,0:T(8,128)S(1)}, u32[]{:S(2)}, u32[]{:S(2)}) async-start(f32[4,24,768]{2,1,0:T(8,128)} %bitcast.37), calls=%async_computation.2 | async-start | bytes 589824 | tf_op jit(solution)/shard_map/all_to_all | solution.py:249
  89.5 0.9 copy-start.4
  93.6 27.1 %collective-permute-start.4 = (bf16[96,2048]{1,0:T(8,128)(2,1)}, bf16[96,2048]{1,0:T(8,128)(2,1)S(1)}, u32[]{:S(2)}, u32[]{:S(2)}) collective-permute-start(bf16[96,2048]{1,0:T(8,128)(2,1)} %get-tuple-element.16), channel_id=1, source_target_pairs={{0,4},{2,6},{4,0},{6,2},{1,5},{3,7},{5,1},{7,3},{8,12},{10,14},{12... | collective-permute-start | bytes 1179656 | tf_op jit(solution)/shard_map/ppermute | solution.py:20
  96.3 24.3 %collective-permute-start.5 = (bf16[96,2048]{1,0:T(8,128)(2,1)S(1)}, bf16[96,2048]{1,0:T(8,128)(2,1)S(1)}, u32[]{:S(2)}, u32[]{:S(2)}) collective-permute-start(bf16[96,2048]{1,0:T(8,128)(2,1)S(1)} %get-tuple-element.17), channel_id=1, source_target_pairs={{0,2},{2,4},{4,6},{6,0},{1,3},{3,5},{5,7},{7,1},{8,10},{10,12},{12... | collective-permute-start | bytes 1179656 | tf_op jit(solution)/shard_map/ppermute | solution.py:20
  99.4 21.2 %collective-permute-start.6 = (bf16[96,2048]{1,0:T(8,128)(2,1)}, bf16[96,2048]{1,0:T(8,128)(2,1)S(1)}, u32[]{:S(2)}, u32[]{:S(2)}) collective-permute-start(bf16[96,2048]{1,0:T(8,128)(2,1)} %get-tuple-element.18), channel_id=1, source_target_pairs={{0,6},{2,0},{4,2},{6,4},{1,7},{3,1},{5,3},{7,5},{8,14},{10,8},{12,... | collective-permute-start | bytes 1179656 | tf_op jit(solution)/shard_map/ppermute | solution.py:20
  104.1 16.4 %all-to-all-start.3 = ((f32[16,1,1152]{2,1,0:T(1,128)}), f32[16,1,1152]{2,1,0:T(1,128)S(1)}, u32[]{:S(2)}, u32[]{:S(2)}) async-start(f32[16,1,1152]{2,1,0:T(1,128)} %reshape.124), calls=%async_computation.3 | async-start | bytes 147456 | tf_op jit(solution)/shard_map/all_to_all | solution.py:254
  120.6 1.1 copy-start.6
  121.8 0.7 copy-start.8
  122.5 0.7 copy-start.10
  125.0 8.6 %copy-start.13 = (f32[5,96]{0,1:T(8,128)S(1)}, f32[5,96]{0,1:T(8,128)}, u32[]{:S(2)}) copy-start(f32[5,96]{0,1:T(8,128)} %copy-done.12) | copy-start | bytes 5764
  126.9 27.2 %all-to-all-start.4 = ((bf16[64,2,1152]{2,1,0:T(2,128)(2,1)}), bf16[64,2,1152]{2,1,0:T(2,128)(2,1)S(1)}, u32[]{:S(2)}, u32[]{:S(2)}) async-start(bf16[64,2,1152]{2,1,0:T(2,128)(2,1)} %copy.48), calls=%async_computation.4 | async-start | bytes 589824 | tf_op jit(solution)/shard_map/all_to_all | solution.py:269
  (1 other events, 0.6 us)

commit v5 on v4

v5 whole, which is shorter than its diff:
```python
import functools

import jax
import jax.numpy as jnp
import numpy as np
from jax import lax
from jax.experimental import pallas as pl
from jax.experimental.pallas import tpu as pltpu
from jax.sharding import Mesh
from jax.sharding import PartitionSpec as P

F32 = jnp.float32
BF16 = jnp.bfloat16
SEQ = ("x", "z")
LANES = 128


def along_y(value, shift):
    count = lax.axis_size("y")
    return lax.ppermute(value, "y", [(i, (i + shift) % count) for i in range(count)])


def other_core(value):
    return lax.ppermute(value, "c", [(0, 1), (1, 0)])


def outer_columns(cells, width):
    count = lax.axis_size(SEQ)
    left = lax.ppermute(cells[:, -width:], SEQ, [(i, i + 1) for i in range(count - 1)])
    right = lax.ppermute(cells[:, :width], SEQ, [(i + 1, i) for i in range(count - 1)])
    return left, right


def share(value, axes):
    count = lax.axis_size(axes)
    copies = jnp.broadcast_to(value.reshape(1, 1, -1), (count, 1, value.size))
    return lax.all_to_all(copies, axes, 0, 0, tiled=True)[:, 0]


def tap_columns(tap, square):
    count, features = tap.shape
    square[:, :] = jnp.zeros(square.shape, F32)
    square[:count, :features] = tap[...].astype(F32)
    return square[...].T


def forward_kernel(
    cells_hbm, left, right, tap_hbm, hidden, line, square, columns, cells, tap, sems
):
    reads = [
        pltpu.make_async_copy(tap_hbm, tap, sems.at[0]),
        pltpu.make_async_copy(cells_hbm, cells, sems.at[1]),
    ]
    for read in reads:
        read.start()
    reach = left.shape[1]
    count = cells.shape[1]
    line[:, :LANES] = jnp.zeros((cells.shape[0], LANES), F32)
    line[:, LANES + count :] = jnp.zeros((cells.shape[0], LANES), F32)
    line[:, LANES - reach : LANES] = left[...].astype(F32)
    line[:, LANES + count : LANES + count + reach] = right[...].astype(F32)
    rows = 8
    reads[0].wait()
    columns[...] = tap_columns(tap, square)
    reads[1].wait()
    line[:, LANES : LANES + count] = cells[...].astype(F32)

    @pl.loop(0, cells.shape[0] // 16)
    def _(block):
        both_hidden = []
        for part in range(2):
            at = pl.ds(pl.multiple_of(block * 16 + part * rows, rows), rows)
            whole = line[at, :]
            taps = columns[at, :]
            conv = jnp.zeros((rows, count), F32)
            for k in range(2 * reach + 1):
                shift = (reach - k) % whole.shape[1]
                moved = pltpu.roll(whole, shift, 1) if shift else whole
                conv = conv + taps[:, k : k + 1] * moved[:, LANES : LANES + count]
            sig = jax.nn.sigmoid(conv)
            both_hidden.append((conv * sig).astype(BF16))
        out = pl.ds(pl.multiple_of(block * 16, 16), 16)
        hidden[out, :] = jnp.concatenate(both_hidden, axis=0)


def forward(cells, left, right, tap):
    rows, count = cells.shape
    return pl.pallas_call(
        forward_kernel,
        out_shape=jax.ShapeDtypeStruct((rows, count), BF16),
        in_specs=[
            pl.BlockSpec(memory_space=pl.ANY),
            pl.BlockSpec(memory_space=pltpu.VMEM),
            pl.BlockSpec(memory_space=pltpu.VMEM),
            pl.BlockSpec(memory_space=pl.ANY),
        ],
        scratch_shapes=[
            pltpu.VMEM((rows, count + 2 * LANES), F32),
            pltpu.VMEM((8, LANES), F32),
            pltpu.VMEM((LANES, 8), F32),
            pltpu.VMEM(cells.shape, cells.dtype),
            pltpu.VMEM(tap.shape, tap.dtype),
            pltpu.SemaphoreType.DMA((2,)),
        ],
        compiler_params=pltpu.CompilerParams(vmem_limit_bytes=8 * 2**20),
        cost_estimate=pl.CostEstimate(
            flops=20 * rows * count, bytes_accessed=4 * rows * count, transcendentals=rows * count
        ),
        name="conv_silu",
    )(cells, left, right, tap)


def pick_rows(weight, picked, blocks):
    width = picked.shape[0] // 4
    for chip, block in enumerate(blocks):
        at = pl.ds(pl.multiple_of(block * width, 16), width)
        picked[chip * width : (chip + 1) * width, :] = weight[at, :]


TURN = (((0,), (0,)), ((), ()))


def near_kernel(place, weight, hidden, targets, logits, counts, picked):
    pick_rows(weight, picked, [2 * chip + place[1] for chip in range(4)])
    logits[...] = lax.dot_general(picked[...], hidden[...], TURN, preferred_element_type=F32)
    counts[...] = jnp.broadcast_to(jnp.sum(targets[...], axis=1, keepdims=True), counts.shape)


def far_kernel(place, weight, hidden, near, counts, expo, stats, picked, table):
    tracks = near.shape[0]
    pick_rows(weight, picked, [2 * chip + 1 - place[1] for chip in range(4)])
    logits = lax.dot_general(picked[...], hidden[...], TURN, preferred_element_type=F32)
    logits = logits + near[...]
    top = jnp.max(logits, axis=1, keepdims=True)
    value = jnp.exp(logits - top)
    expo[...] = value
    total = jnp.sum(value, axis=1, keepdims=True)
    lane = lax.broadcasted_iota(jnp.int32, (tracks, LANES), 1)
    table[...] = jnp.zeros(table.shape, F32)
    table[:tracks, :] = jnp.where(lane == 0, top, jnp.where(lane == 1, total, counts[...]))
    stats[...] = table[...].T[: stats.shape[0]]


def kernel_call(body, name, outs, scratch, place, *operands, flops=0):
    size = sum(o.size * o.dtype.itemsize for o in operands)
    size += sum(o.size * o.dtype.itemsize for o in outs)
    return pl.pallas_call(
        body,
        out_shape=outs,
        in_specs=[pl.BlockSpec(memory_space=pltpu.SMEM)]
        + [pl.BlockSpec(memory_space=pltpu.VMEM)] * len(operands),
        scratch_shapes=scratch,
        compiler_params=pltpu.CompilerParams(vmem_limit_bytes=size + 4 * 2**20),
        cost_estimate=pl.CostEstimate(flops=flops, bytes_accessed=size, transcendentals=0),
        name=name,
    )(place, *operands)


def near_logits(place, weight, hidden, targets):
    tracks, count = targets.shape
    outs = (
        jax.ShapeDtypeStruct((tracks, count), F32),
        jax.ShapeDtypeStruct((tracks, LANES), F32),
    )
    scratch = [pltpu.VMEM((hidden.shape[0], tracks), BF16)]
    return kernel_call(
        near_kernel, "near_logits", outs, scratch, place, weight, hidden, targets,
        flops=2 * hidden.size * tracks,
    )


def far_logits(place, weight, hidden, near, counts):
    tracks = near.shape[0]
    outs = (
        jax.ShapeDtypeStruct(near.shape, F32),
        jax.ShapeDtypeStruct((8, LANES), F32),
    )
    scratch = [
        pltpu.VMEM((hidden.shape[0], tracks), BF16),
        pltpu.VMEM((LANES, LANES), F32),
    ]
    return kernel_call(
        far_kernel, "far_logits", outs, scratch, place, weight, hidden, near, counts,
        flops=2 * hidden.size * tracks,
    )


def grad_kernel(place, weight, scale, expo, targets, grad, sent, picked):
    tracks = expo.shape[0]
    column = scale[...].T[:tracks, 0:1]
    value = (column * expo[...] - targets[...]).astype(BF16)
    grad[...] = value
    blocks = [2 * lax.rem(place[0] + shift, 4) + 1 - place[1] for shift in range(4)]
    pick_rows(weight, picked, blocks)
    sent[...] = jnp.dot(picked[...], value, preferred_element_type=F32).astype(BF16)


def logit_gradient(place, weight, scale, expo, targets):
    tracks, count = expo.shape
    outs = (
        jax.ShapeDtypeStruct((tracks, count), BF16),
        jax.ShapeDtypeStruct((weight.shape[0] // 2, count), BF16),
    )
    scratch = [pltpu.VMEM((weight.shape[0] // 2, tracks), BF16)]
    return kernel_call(
        grad_kernel, "logit_grad", outs, scratch, place, weight, scale, expo, targets,
        flops=weight.size * count,
    )


def scatter_kernel(place, weight, grad, received, mine, one, two, three, picked):
    width = mine.shape[0]
    blocks = [2 * lax.rem(place[0] + shift, 4) + place[1] for shift in range(4)]
    pick_rows(weight, picked, blocks)
    part = jnp.dot(picked[...], grad[...], preferred_element_type=F32)
    for shift, out in enumerate((mine, one, two, three)):
        at = slice(shift * width, (shift + 1) * width)
        out[...] = (part[at] + received[at, :].astype(F32)).astype(out.dtype)


def scatter_blocks(place, weight, grad, received):
    tracks, count = grad.shape
    width = received.shape[0] // 4
    block = jax.ShapeDtypeStruct((width, count), BF16)
    outs = (jax.ShapeDtypeStruct((width, count), F32), block, block, block)
    scratch = [pltpu.VMEM((received.shape[0], tracks), BF16)]
    return kernel_call(
        scatter_kernel, "core_sum", outs, scratch, place, weight, grad, received,
        flops=weight.size * count,
    )


def outer_kernel(place, grad, mine, theirs, out, table):
    tracks = grad.shape[0]
    width = mine.shape[0] // 4
    along = (((1,), (1,)), ((), ()))
    for block, offset in ((mine, place[1]), (theirs, 1 - place[1])):
        part = lax.dot_general(block[...], grad[...], along, preferred_element_type=F32)
        for chip in range(4):
            row = (2 * chip + offset) * width
            at = pl.ds(pl.multiple_of(row, 16), width)
            table[at, :tracks] = part[chip * width : (chip + 1) * width]
    out[...] = table[...].T[:tracks]


def outer_product(place, grad, mine, theirs):
    tracks = grad.shape[0]
    features = 2 * mine.shape[0]
    return kernel_call(
        outer_kernel, "weight_part", (jax.ShapeDtypeStruct((tracks, features), F32),),
        [pltpu.VMEM((features, LANES), F32)], place, grad, mine, theirs,
        flops=2 * features * grad.size,
    )[0]


def rows_kernel(parts, out):
    wide = parts.shape[2] // LANES
    tiles = out.shape[2] // LANES
    for tile in range(parts.shape[1] // 8 * wide):
        row, lane = tile // wide * 8, tile % wide * LANES
        group, spot = tile // tiles, tile % tiles * LANES
        total = jnp.sum(parts[:, row : row + 8, lane : lane + LANES], axis=0)
        out[group * 8 : group * 8 + 8, 0, spot : spot + LANES] = total


def sum_to_rows(parts, rows):
    size = parts.shape[1] * parts.shape[2]
    return pl.pallas_call(
        rows_kernel,
        out_shape=jax.ShapeDtypeStruct((rows, 1, size // rows), F32),
        compiler_params=pltpu.CompilerParams(vmem_limit_bytes=8 * 2**20),
        cost_estimate=pl.CostEstimate(flops=4 * size, bytes_accessed=20 * size, transcendentals=0),
        name="sum_to_rows",
    )(parts)


def from_rows(rows, tracks, features):
    tiles = rows.reshape(-1, 8, rows.shape[1] // LANES, LANES).transpose(0, 2, 1, 3)
    tiles = tiles.reshape(tracks // 8, features // LANES, 8, LANES).transpose(0, 2, 1, 3)
    return tiles.reshape(tracks, features)


def backward_kernel(
    mine, one, two, three, cells, left, right, tap, grad, rows_out, line, table, sides, sems,
    square, columns,
):
    reach = left.shape[1]
    count = cells.shape[1]
    rows = 16
    copies = [
        pltpu.make_async_copy(side, sides.at[i], sems.at[i])
        for i, side in enumerate((left, right))
    ]
    for copy in copies:
        copy.start()
    lane = lax.broadcasted_iota(jnp.int32, (rows, LANES), 1)
    columns[...] = tap_columns(tap, square)
    line[:, :LANES] = jnp.zeros((rows, LANES), F32)
    line[:, LANES + count :] = jnp.zeros((rows, LANES), F32)
    for copy in copies:
        copy.wait()

    @pl.loop(0, cells.shape[0] // rows)
    def _(block):
        at = pl.ds(pl.multiple_of(block * rows, rows), rows)
        line[:, LANES - reach : LANES] = sides[0, at, :].astype(F32)
        line[:, LANES + count : LANES + count + reach] = sides[1, at, :].astype(F32)
        line[:, LANES : LANES + count] = cells[at, :].astype(F32)
        whole = line[...]
        taps = columns[at, :]
        moved = []
        conv = jnp.zeros((rows, count), F32)
        for k in range(2 * reach + 1):
            shift = (reach - k) % whole.shape[1]
            turned = pltpu.roll(whole, shift, 1) if shift else whole
            moved.append(turned[:, LANES : LANES + count])
            conv = conv + taps[:, k : k + 1] * moved[k]
        sig = jax.nn.sigmoid(conv)
        total = mine[at, :] + one[at, :].astype(F32)
        total = total + two[at, :].astype(F32) + three[at, :].astype(F32)
        value = (total * (sig * (1.0 + conv * (1.0 - sig)))).astype(BF16)
        grad[at, :] = value
        value = value.astype(F32)
        found = jnp.zeros((rows, LANES), F32)
        for k in range(2 * reach + 1):
            found = jnp.where(lane == k, jnp.sum(moved[k] * value, axis=1, keepdims=True), found)
        for k in range(reach):
            found = jnp.where(lane == 8 + k, value[:, k : k + 1], found)
            last = count - reach + k
            found = jnp.where(lane == 8 + reach + k, value[:, last : last + 1], found)
        table[at, :] = found

    rows_out[...] = table[...].T[: rows_out.shape[0]]


def backward(mine, parts, cells, left, right, tap):
    rows, count = cells.shape
    return pl.pallas_call(
        backward_kernel,
        out_shape=(
            jax.ShapeDtypeStruct((rows, count), BF16),
            jax.ShapeDtypeStruct((16, rows), F32),
        ),
        in_specs=[pl.BlockSpec(memory_space=pltpu.VMEM)] * 5
        + [pl.BlockSpec(memory_space=pl.ANY)] * 2
        + [pl.BlockSpec(memory_space=pltpu.VMEM)],
        scratch_shapes=[
            pltpu.VMEM((16, count + 2 * LANES), F32),
            pltpu.VMEM((rows, LANES), F32),
            pltpu.VMEM((2,) + left.shape, left.dtype),
            pltpu.SemaphoreType.DMA((2,)),
            pltpu.VMEM((8, LANES), F32),
            pltpu.VMEM((LANES, 8), F32),
        ],
        compiler_params=pltpu.CompilerParams(vmem_limit_bytes=8 * 2**20),
        cost_estimate=pl.CostEstimate(
            flops=40 * rows * count, bytes_accessed=14 * rows * count, transcendentals=0
        ),
        name="conv_grad",
    )(mine, *parts, cells, left, right, tap)


def spread_kernel(grad, tap, embed, ends, line, square, columns):
    count = grad.shape[1]
    rows = 16
    reach = tap.shape[0] // 2
    columns[...] = tap_columns(tap, square)
    line[:, :LANES] = jnp.zeros((rows, LANES), F32)
    line[:, LANES + count :] = jnp.zeros((rows, LANES), F32)

    @pl.loop(0, grad.shape[0] // rows)
    def _(block):
        at = pl.ds(pl.multiple_of(block * rows, rows), rows)
        line[:, LANES : LANES + count] = grad[at, :].astype(F32)
        whole = line[...]
        taps = columns[at, :]
        total = jnp.zeros((rows, count), F32)
        for k in range(2 * reach + 1):
            shift = (k - reach) % whole.shape[1]
            moved = pltpu.roll(whole, shift, 1) if shift else whole
            total = total + taps[:, k : k + 1] * moved[:, LANES : LANES + count]
        embed[at, :] = total.astype(BF16)
        ends[at, :LANES] = total[:, :LANES]
        ends[at, LANES:] = total[:, count - LANES :]


def spread(grad, tap):
    rows, count = grad.shape
    return pl.pallas_call(
        spread_kernel,
        out_shape=(
            jax.ShapeDtypeStruct((rows, count), BF16),
            jax.ShapeDtypeStruct((rows, 2 * LANES), F32),
        ),
        scratch_shapes=[
            pltpu.VMEM((16, count + 2 * LANES), F32),
            pltpu.VMEM((8, LANES), F32),
            pltpu.VMEM((LANES, 8), F32),
        ],
        compiler_params=pltpu.CompilerParams(vmem_limit_bytes=8 * 2**20),
        cost_estimate=pl.CostEstimate(
            flops=10 * rows * count, bytes_accessed=4 * rows * count, transcendentals=0
        ),
        name="embed_grad",
    )(grad, tap)


def finish_kernel(
    place, slab, ends, tap, given, embed, sums, square, columns, edges, tiles, sems
):
    del given
    ntaps, width = tap.shape
    reach = ntaps // 2
    devices = slab.shape[0]
    me = place[0]
    columns[...] = tap_columns(tap, square)

    edges[...] = jnp.zeros(edges.shape, F32)
    start = 2 * ntaps * width
    for side, other in enumerate((me - 1, me + 1)):
        row = slab[pl.ds(jnp.clip(other, 0, devices - 1), 1), :]
        row = jnp.where((other >= 0) & (other < devices), row, 0.0)
        for k in range(reach):
            turned = pltpu.roll(row, row.shape[1] - start - k * width, 1)
            edges[side * reach + k : side * reach + k + 1, :] = turned[:, :LANES]
    outer = edges[...].T[:width]

    lane = lax.broadcasted_iota(jnp.int32, (width, LANES), 1)
    first, last = ends[:, :LANES], ends[:, LANES:]
    for column in range(reach):
        for k in range(ntaps):
            source = column - k + reach
            if source < 0:
                mirror = ntaps - 1 - k
                before = outer[:, reach + source : reach + source + 1]
                after = outer[:, reach - 1 - source : reach - source]
                value = columns[:width, k : k + 1] * before
                first = first + jnp.where(lane == column, value, 0.0)
                value = columns[:width, mirror : mirror + 1] * after
                last = last + jnp.where(lane == LANES - 1 - column, value, 0.0)
    count = embed.shape[1]
    writes = []
    for n, (tile, at) in enumerate(((first, 0), (last, count - LANES))):
        tiles[n] = tile.astype(BF16)
        writes.append(
            pltpu.make_async_copy(tiles.at[n], embed.at[:, pl.ds(at, LANES)], sems.at[n])
        )
        writes[n].start()

    total = jnp.sum(slab[...], axis=0, keepdims=True)
    for k in range(ntaps):
        high = pltpu.roll(total, total.shape[1] - k * width, 1) if k else total
        low = pltpu.roll(total, total.shape[1] - (ntaps + k) * width, 1)
        sums[k : k + 1, :] = (high + low)[:, :width]
    for write in writes:
        write.wait()


def finish(place, slab, ends, tap, embed):
    ntaps, width = tap.shape
    return pl.pallas_call(
        finish_kernel,
        out_shape=(
            jax.ShapeDtypeStruct(embed.shape, embed.dtype),
            jax.ShapeDtypeStruct((ntaps, width), F32),
        ),
        in_specs=[pl.BlockSpec(memory_space=pltpu.SMEM)]
        + [pl.BlockSpec(memory_space=pltpu.VMEM)] * 3
        + [pl.BlockSpec(memory_space=pl.ANY)],
        out_specs=(
            pl.BlockSpec(memory_space=pl.ANY),
            pl.BlockSpec(memory_space=pltpu.VMEM),
        ),
        input_output_aliases={4: 0},
        scratch_shapes=[
            pltpu.VMEM((8, LANES), F32),
            pltpu.VMEM((LANES, 8), F32),
            pltpu.VMEM((8, LANES), F32),
            pltpu.VMEM((2, width, LANES), BF16),
            pltpu.SemaphoreType.DMA((2,)),
        ],
        compiler_params=pltpu.CompilerParams(vmem_limit_bytes=8 * 2**20),
        cost_estimate=pl.CostEstimate(
            flops=slab.size, bytes_accessed=8 * slab.size, transcendentals=0
        ),
        name="finish",
    )(place, slab, ends, tap, embed)


def shards(embeddings, taps, head_weight, targets):
    width = embeddings.shape[0]
    count = embeddings.shape[1]
    tracks = head_weight.shape[0]
    ntaps = taps.shape[0]
    reach = ntaps // 2
    y = lax.axis_index("y")
    c = lax.axis_index("c")
    ny = lax.axis_size("y")
    nseq = lax.axis_size(SEQ)
    me = lax.axis_index(SEQ)
    features = ny * 2 * width

    place = jnp.stack([y, c])
    left, right = outer_columns(embeddings, reach)
    block = forward(embeddings, left, right, taps)

    mine = lax.all_to_all(
        jnp.broadcast_to(block[None], (ny, width, count)), "y", 0, 0, tiled=True
    ).reshape(ny * width, count)
    theirs = other_core(mine)
    weight = head_weight.T
    near, counts = near_logits(place, weight, mine, targets)
    expo, stats = far_logits(place, weight, theirs, near, counts)
    every = share(stats[:3].reshape(-1), SEQ)
    tops = every[:, :LANES]
    peak = jnp.max(tops, axis=0)
    total = jnp.sum(every[:, LANES : 2 * LANES] * jnp.exp(tops - peak[None]), axis=0)
    counts = jnp.sum(every[:, 2 * LANES :], axis=0)
    scale = counts * jnp.exp(stats[0] - peak) / jnp.where(total > 0.0, total, 1.0)
    logit_grad, sent = logit_gradient(
        place, weight, jnp.broadcast_to(scale[None], (8, LANES)), expo, targets
    )
    received = other_core(sent)

    nx, nz = lax.axis_size("x"), lax.axis_size("z")
    late_grad, _ = lax.optimization_barrier((logit_grad, sent))
    local = outer_product(place, late_grad, mine, theirs)
    part = lax.all_to_all(local.reshape(nx, tracks // nx, features), "x", 0, 0, tiled=True)

    own, *blocks = scatter_blocks(place, weight, logit_grad, received)
    parts = [along_y(blocks[shift - 1], shift) for shift in (2, 1, 3)]
    part = lax.all_to_all(sum_to_rows(part, nz), "z", 0, 0, tiled=True)

    conv_grad, found = backward(own, parts, embeddings, left, right, taps)
    part, found = lax.optimization_barrier((part, found))
    part = jnp.sum(part, axis=0).reshape(-1)
    local_taps = found[:ntaps].reshape(-1)
    head = found[8 : 8 + reach].reshape(1, -1).astype(BF16)
    tail = found[8 + reach : 8 + 2 * reach].reshape(1, -1).astype(BF16)

    high = lax.reduce_precision(local_taps, 8, 7)
    low = local_taps - high
    row = jnp.arange(nseq)[:, None]
    zero = jnp.zeros((), BF16)
    edge = jnp.where(row == me + 1, tail, jnp.where(row == me - 1, head, zero))
    both = jnp.concatenate([high, low]).astype(BF16)
    both = jnp.broadcast_to(both[None], (nseq, both.size))
    same = jnp.broadcast_to(part.astype(BF16)[None], (nseq, part.size))
    message = jnp.stack([same, jnp.concatenate([both, edge], axis=1)], axis=1)
    slab = lax.all_to_all(message, SEQ, 0, 0, tiled=True)
    weight_grad = from_rows(slab[:, 0], tracks, features).astype(F32)
    embed_grad, ends = spread(conv_grad, taps)
    embed_grad, taps_grad = finish(
        me.reshape(1), slab[:, 1].astype(F32), ends, taps, embed_grad
    )
    return embed_grad, weight_grad, taps_grad


def solution(mesh):
    fine = Mesh(np.asarray(mesh.devices).reshape(4, 16, 4, 2), ("x", "z", "y", "c"))
    track = ("y", "c")
    return jax.shard_map(
        shards,
        mesh=fine,
        in_specs=(P(track, SEQ), P(None, track), P(track, None), P(track, SEQ)),
        out_specs=(P(track, SEQ), P(track, None), P(None, track)),
        check_vma=False,
    )
```

time: 160 us -> 155 us (0.969)
  Pallas kernels: 7.75 us -> 19 us
  local copies, waits for them, and re-layouts: 15.7 us -> 7.5 us
  other arithmetic: 5.6 us -> 1.27 us
  matrix products: 2.65 us -> 0 us
    all_to_all x1, waiting for transfers between devices: 12.9 us -> 1.89 us  [shards(): part = lax.all_to_all(sum_to_rows(part, nz), 'z', 0, 0, tiled=True)]
    pallas_call x3 -> x9, Pallas kernels: 6.04 us -> 16.5 us  [the longest x5 9.24 us: kernel_call(): pl.pallas_call(body, out_shape=outs, in_specs=[pl.BlockSpec(memory_space=...]
    ppermute x3, waiting for transfers between devices: 0.01 us -> 8.28 us  [along_y(): lax.ppermute(value, 'y', [(i, (i + shift) % count) for i in range(count)])]
    unnamed x34 -> x22, local copies, waits for them, and re-layouts: 8.87 us -> 4.71 us
    dot_general x3 -> x0, matrix products: 2.65 us -> none  [the longest x1 1.7 us: shards(): jnp.dot(second.T, logit_grad, preferred_element_type=F32).astype(BF16)]
    convert_element_type x5 -> x2, other arithmetic: 2.87 us -> 0.76 us  [the longest x1 0.73 us: shards(): weight_grad = from_rows(slab[:, 0], tracks, features).astype(F32)]
    reduce_sum x7 -> x2, other arithmetic: 2.2 us -> 0.1 us  [the longest x1 0.07 us: shards(): part = jnp.sum(part, axis=0).reshape(-1)]
  transfers between devices with their start and end apart: 10 -> 10, of which waited for: 3 -> 6; matrix products, arithmetic and copies ran while one was open for 4% -> 0% of each run, Pallas kernels for 3% -> 8%
where the time goes in v5:
time: 155 us; the launch traced here: 154 us
  blocking collectives  46.5 us (30%)
  starting transfers between devices  43.1 us (28%)
  waiting for transfers between devices  36.1 us (23%)
  Pallas kernels  19 us (12%)
  local copies, waits for them, and re-layouts  7.5 us (5%)
    all_to_all x1, blocking collectives, shards(): lax.all_to_all(jnp.broadcast_to(block[None], (ny, width, count)), 'y', 0,...  23.7 us
    all_to_all x1, blocking collectives, share(): return lax.all_to_all(copies, axes, 0, 0, tiled=True)[:, 0]  22.8 us
    all_to_all x1, waiting for transfers between devices, shards(): slab = lax.all_to_all(message, SEQ, 0, 0, tiled=True)  19.1 us
    ppermute x1, starting transfers between devices, outer_columns(): lax.ppermute(cells[:, :width], SEQ, [(i + 1, i) for i in range(count - 1)])  11.7 us
    ppermute x3, starting transfers between devices, along_y(): lax.ppermute(value, 'y', [(i, (i + shift) % count) for i in range(count)])  9.77 us
    pallas_call x5, Pallas kernels, kernel_call(): pl.pallas_call(body, out_shape=outs, in_specs=[pl.BlockSpec(memory_space=...  9.24 us
    ppermute x3, waiting for transfers between devices, along_y(): lax.ppermute(value, 'y', [(i, (i + shift) % count) for i in range(count)])  8.28 us
    all_to_all x1, starting transfers between devices, shards(): slab = lax.all_to_all(message, SEQ, 0, 0, tiled=True)  6.72 us
  transfers between devices with their start and end apart: 10, of which 6 were waited for; matrix products, arithmetic and copies ran while one was open for 0% of the time, Pallas kernels for 8%

profile of v5, /device:TPU:6, one launch (start us, length us, event | category | flops | bytes accessed | tf_op | source)
XLA Modules:
  0.0 154.4 jit_solution(9681990687900878647)
XLA Ops:
  1.5 11.7 %collective-permute-start.1 = (bf16[96,2]{1,0:T(8,128)(2,1)S(1)}, bf16[96,2]{1,0:T(8,128)(2,1)S(1)}, u32[]{:S(2)}, u32[]{:S(2)}) collective-permute-start(bf16[96,2]{1,0:T(8,128)(2,1)S(1)} %get-tuple-element.42), channel_id=1, source_target_pairs={{8,0},{16,8},{24,16},{32,24},{40,32},{48,40},{56,48},{64,56},{72,6... | collective-permute-start | bytes 1160 | tf_op jit(solution)/shard_map/ppermute | solution.py:30
  13.1 1.9 %collective-permute-start = (bf16[96,2]{1,0:T(8,128)(2,1)S(1)}, bf16[96,2]{1,0:T(8,128)(2,1)S(1)}, u32[]{:S(2)}, u32[]{:S(2)}) collective-permute-start(bf16[96,2]{1,0:T(8,128)(2,1)S(1)} %get-tuple-element.43), channel_id=1, source_target_pairs={{0,8},{8,16},{16,24},{24,32},{32,40},{40,48},{48,56},{56,64},{64,7... | collective-permute-start | bytes 1160 | tf_op jit(solution)/shard_map/ppermute | solution.py:29
  15.1 5.9 %collective-permute-done.left = bf16[96,2]{1,0:T(8,128)(2,1)S(1)} collective-permute-done((bf16[96,2]{1,0:T(8,128)(2,1)S(1)}, bf16[96,2]{1,0:T(8,128)(2,1)S(1)}, u32[]{:S(2)}, u32[]{:S(2)}) %collective-permute-start) | collective-permute-done | bytes 416 | tf_op jit(solution)/shard_map/ppermute | solution.py:29
  22.6 2.0 %conv_silu.1 = bf16[96,2048]{1,0:T(8,128)(2,1)S(1)} custom-call(bf16[96,2048]{1,0:T(8,128)(2,1)S(1)} %copy-done.2, bf16[96,2]{1,0:T(8,128)(2,1)S(1)} %collective-permute-done.left, bf16[96,2]{1,0:T(8,128)(2,1)S(1)} %collective-permute-done.1.right, bf16[5,96]{1,0:T(8,128)(2,1)S(1)} %copy-done.7), custom_call_target="tpu_custom_call" | custom-call | flops 3932160 | bytes 786432 | tf_op jit(solution)/shard_map/conv_silu/pallas_call | solution.py:88
  24.8 23.7 %all_to_all.25 = bf16[4,96,2048]{2,1,0:T(8,128)(2,1)S(1)} all-to-all(bf16[4,96,2048]{2,1,0:T(8,128)(2,1)S(1)} %broadcast_in_dim.70), channel_id=1, replica_groups=mesh['x'=4,'z'=16,'y'=4,'c'=2] {'y'}, dimensions={0} | all-to-all | bytes 3145728 | tf_op jit(solution)/shard_map/all_to_all | solution.py:507
  48.5 1.9 %collective-permute-start.2 = (bf16[384,2048]{1,0:T(8,128)(2,1)S(1)}, bf16[384,2048]{1,0:T(8,128)(2,1)S(1)}, u32[]{:S(2)}, u32[]{:S(2)}) collective-permute-start(bf16[384,2048]{1,0:T(8,128)(2,1)S(1)} %bitcast.50), channel_id=1, source_target_pairs={{0,1},{1,0},{2,3},{3,2},{4,5},{5,4},{6,7},{7,6},{8,9},{9,8},{10,11... | collective-permute-start | bytes 4718600 | tf_op jit(solution)/shard_map/ppermute | solution.py:24
  55.2 22.8 %all_to_all.26 = f32[64,1,384]{2,1,0:T(1,128)S(1)} all-to-all(f32[64,1,384]{2,1,0:T(1,128)S(1)} %broadcast_in_dim.72), channel_id=1, replica_groups=mesh['x'=4,'z'=16,'y'=4,'c'=2] {'x','z'}, dimensions={0} | all-to-all | bytes 196608 | tf_op jit(solution)/shard_map/all_to_all | solution.py:37
  78.1 2.4 %logit_grad.1 = (bf16[96,2048]{1,0:T(8,128)(2,1)S(1)}, bf16[384,2048]{1,0:T(8,128)(2,1)}) custom-call(s32[2]{0:T(128)S(1)} %pad_add_fusion.place, bf16[768,96]{1,0:T(8,128)(2,1)S(1)} %bitcast.55, f32[8,128]{1,0:T(8,128)S(1)} %broadcast_in_dim.75.scale, f32[96,2048]{1,0:T(8,128)S(1)} %get-tuple-element.25.expo, f32[96,2048]{1,0:T(8,128)S(1)} %copy-done.1), custom_call_target="tpu_custom_call" | custom-call | flops 150994944 | bytes 3690496 | tf_op jit(solution)/shard_map/logit_grad/pallas_call | solution.py:147
  80.5 1.9 %collective-permute-start.3 = (bf16[384,2048]{1,0:T(8,128)(2,1)}, bf16[384,2048]{1,0:T(8,128)(2,1)}, u32[]{:S(2)}, u32[]{:S(2)}) collective-permute-start(bf16[384,2048]{1,0:T(8,128)(2,1)} %get-tuple-element.27), channel_id=1, source_target_pairs={{0,1},{1,0},{2,3},{3,2},{4,5},{5,4},{6,7},{7,6},{8,9},{9,8},{10,11... | collective-permute-start | bytes 4718600 | tf_op jit(solution)/shard_map/ppermute | solution.py:24
  82.5 1.7 %weight_part.1 = f32[96,768]{1,0:T(8,128)S(1)} custom-call(s32[2]{0:T(128)S(1)} %pad_add_fusion.place, bf16[96,2048]{1,0:T(8,128)(2,1)S(1)} %get-tuple-element.26.grad, bf16[384,2048]{1,0:T(8,128)(2,1)S(1)} %bitcast.52, bf16[384,2048]{1,0:T(8,128)(2,1)S(1)} %collective-permute-done.2.hidden.theirs), custom_call_target="tpu_custom_call" | custom-call | flops 301989888 | bytes 3833856 | tf_op jit(solution)/shard_map/weight_part/pallas_call | solution.py:147
  84.9 5.7 %all-to-all-start.2 = ((f32[4,24,768]{2,1,0:T(8,128)}), f32[4,24,768]{2,1,0:T(8,128)}, u32[]{:S(2)}, u32[]{:S(2)}) async-start(f32[4,24,768]{2,1,0:T(8,128)} %bitcast.57), calls=%async_computation.2 | async-start | bytes 589824 | tf_op jit(solution)/shard_map/all_to_all | solution.py:528
  91.5 2.9 %core_sum.1 = (f32[96,2048]{1,0:T(8,128)S(1)}, bf16[96,2048]{1,0:T(8,128)(2,1)S(1)}, bf16[96,2048]{1,0:T(8,128)(2,1)}, bf16[96,2048]{1,0:T(8,128)(2,1)}) custom-call(s32[2]{0:T(128)S(1)} %pad_add_fusion.place, bf16[768,96]{1,0:T(8,128)(2,1)S(1)} %bitcast.56, bf16[96,2048]{1,0:T(8,128)(2,1)S(1)} %copy-done.5, bf16[384,2048]{1,0:T(8,128)(2,1)} %collective-permute-done.3.received), custom_call_target="tpu_custom_call" | custom-call | flops 150994944 | bytes 4079616 | tf_op jit(solution)/shard_map/core_sum/pallas_call | solution.py:147
  94.4 2.7 %collective-permute-start.4 = (bf16[96,2048]{1,0:T(8,128)(2,1)}, bf16[96,2048]{1,0:T(8,128)(2,1)S(1)}, u32[]{:S(2)}, u32[]{:S(2)}) collective-permute-start(bf16[96,2048]{1,0:T(8,128)(2,1)} %get-tuple-element.29), channel_id=1, source_target_pairs={{0,4},{2,6},{4,0},{6,2},{1,5},{3,7},{5,1},{7,3},{8,12},{10,14},{12... | collective-permute-start | bytes 1179656 | tf_op jit(solution)/shard_map/ppermute | solution.py:20
  97.1 3.1 %collective-permute-start.5 = (bf16[96,2048]{1,0:T(8,128)(2,1)S(1)}, bf16[96,2048]{1,0:T(8,128)(2,1)S(1)}, u32[]{:S(2)}, u32[]{:S(2)}) collective-permute-start(bf16[96,2048]{1,0:T(8,128)(2,1)S(1)} %get-tuple-element.30), channel_id=1, source_target_pairs={{0,2},{2,4},{4,6},{6,0},{1,3},{3,5},{5,7},{7,1},{8,10},{10,12},{12... | collective-permute-start | bytes 1179656 | tf_op jit(solution)/shard_map/ppermute | solution.py:20
  100.2 3.9 %collective-permute-start.6 = (bf16[96,2048]{1,0:T(8,128)(2,1)}, bf16[96,2048]{1,0:T(8,128)(2,1)S(1)}, u32[]{:S(2)}, u32[]{:S(2)}) collective-permute-start(bf16[96,2048]{1,0:T(8,128)(2,1)} %get-tuple-element.31), channel_id=1, source_target_pairs={{0,6},{2,0},{4,2},{6,4},{1,7},{3,1},{5,3},{7,5},{8,14},{10,8},{12,... | collective-permute-start | bytes 1179656 | tf_op jit(solution)/shard_map/ppermute | solution.py:20
  104.2 1.6 %sum_to_rows.1 = f32[16,1,1152]{2,1,0:T(1,128)} custom-call(f32[4,24,768]{2,1,0:T(8,128)} %all-to-all-done.2.parts), custom_call_target="tpu_custom_call" | custom-call | flops 73728 | bytes 368640 | tf_op jit(solution)/shard_map/sum_to_rows/pallas_call | solution.py:268
  105.8 3.5 %all-to-all-start.3 = ((f32[16,1,1152]{2,1,0:T(1,128)}), f32[16,1,1152]{2,1,0:T(1,128)S(1)}, u32[]{:S(2)}, u32[]{:S(2)}) async-start(f32[16,1,1152]{2,1,0:T(1,128)} %sum_to_rows.1), calls=%async_computation.3 | async-start | bytes 147456 | tf_op jit(solution)/shard_map/all_to_all | solution.py:532
  110.0 7.7 %collective-permute-done.5.two = bf16[96,2048]{1,0:T(8,128)(2,1)S(1)} collective-permute-done((bf16[96,2048]{1,0:T(8,128)(2,1)S(1)}, bf16[96,2048]{1,0:T(8,128)(2,1)S(1)}, u32[]{:S(2)}, u32[]{:S(2)}) %collective-permute-start.5) | collective-permute-done | bytes 393248 | tf_op jit(solution)/shard_map/ppermute | solution.py:20
  117.7 2.5 %conv_grad.1 = (bf16[96,2048]{1,0:T(8,128)(2,1)S(1)}, f32[16,96]{1,0:T(8,128)S(1)}) custom-call(f32[96,2048]{1,0:T(8,128)S(1)} %get-tuple-element.28.mine, bf16[96,2048]{1,0:T(8,128)(2,1)S(1)} %collective-permute-done.4.one, bf16[96,2048]{1,0:T(8,128)(2,1)S(1)} %collective-permute-done.5.two, bf16[96,2048]{1,0:T(8,128)(2,1)S(1)} %collective-permute-done.6.three, ...), custom_call_target="tpu_custom_call" | custom-call | flops 7864320 | bytes 2752512 | tf_op jit(solution)/shard_map/conv_grad/pallas_call | solution.py:338
  120.2 1.9 %all-to-all-done.3 = f32[16,1,1152]{2,1,0:T(1,128)S(1)} async-done(((f32[16,1,1152]{2,1,0:T(1,128)}), f32[16,1,1152]{2,1,0:T(1,128)S(1)}, u32[]{:S(2)}, u32[]{:S(2)}) %all-to-all-start.3) | async-done | bytes 73760 | tf_op jit(solution)/shard_map/all_to_all | solution.py:532
  123.8 6.7 %all-to-all-start.4 = ((bf16[64,2,1152]{2,1,0:T(2,128)(2,1)}), bf16[64,2,1152]{2,1,0:T(2,128)(2,1)S(1)}, u32[]{:S(2)}, u32[]{:S(2)}) async-start(bf16[64,2,1152]{2,1,0:T(2,128)(2,1)} %copy.20), calls=%async_computation.4 | async-start | bytes 589824 | tf_op jit(solution)/shard_map/all_to_all | solution.py:550
  130.5 1.9 %embed_grad.1 = (bf16[96,2048]{1,0:T(8,128)(2,1)}, f32[96,256]{1,0:T(8,128)S(1)}) custom-call(bf16[96,2048]{1,0:T(8,128)(2,1)S(1)} %get-tuple-element.35.grad, bf16[5,96]{1,0:T(8,128)(2,1)S(1)} %copy-done.8), custom_call_target="tpu_custom_call" | custom-call | flops 1966080 | bytes 786432 | tf_op jit(solution)/shard_map/embed_grad/pallas_call | solution.py:389
  132.4 19.1 %all-to-all-done.4 = bf16[64,2,1152]{2,1,0:T(2,128)(2,1)S(1)} async-done(((bf16[64,2,1152]{2,1,0:T(2,128)(2,1)}), bf16[64,2,1152]{2,1,0:T(2,128)(2,1)S(1)}, u32[]{:S(2)}, u32[]{:S(2)}) %all-to-all-start.4) | async-done | bytes 294944 | tf_op jit(solution)/shard_map/all_to_all | solution.py:550
  152.7 1.7 %finish.1 = (bf16[96,2048]{1,0:T(8,128)(2,1)}, f32[5,96]{1,0:T(8,128)}) custom-call(s32[1]{0:T(128)} %bitcast.place, f32[64,1152]{1,0:T(8,128)S(1)} %fusion.1.slab, f32[96,256]{1,0:T(8,128)S(1)} %get-tuple-element.36.ends, bf16[5,96]{1,0:T(8,128)(2,1)S(1)} %copy-done.8, bf16[96,2048]{1,0:T(8,128)(2,1)} %get-tuple-element.37.given), custom_call_target="tpu_custom_call", output_to_operand_aliasing={{0}: (4, {})} | custom-call | flops 73728 | bytes 589824 | tf_op jit(solution)/shard_map/finish/pallas_call | solution.py:461
  (57 shorter events, 12.6 us)
Async XLA Ops:
  1.5 13.6 %collective-permute-start.1 = (bf16[96,2]{1,0:T(8,128)(2,1)S(1)}, bf16[96,2]{1,0:T(8,128)(2,1)S(1)}, u32[]{:S(2)}, u32[]{:S(2)}) collective-permute-start(bf16[96,2]{1,0:T(8,128)(2,1)S(1)} %get-tuple-element.42), channel_id=1, source_target_pairs={{8,0},{16,8},{24,16},{32,24},{40,32},{48,40},{56,48},{64,56},{72,6... | collective-permute-start | bytes 1160 | tf_op jit(solution)/shard_map/ppermute | solution.py:30
  13.1 7.8 %collective-permute-start = (bf16[96,2]{1,0:T(8,128)(2,1)S(1)}, bf16[96,2]{1,0:T(8,128)(2,1)S(1)}, u32[]{:S(2)}, u32[]{:S(2)}) collective-permute-start(bf16[96,2]{1,0:T(8,128)(2,1)S(1)} %get-tuple-element.43), channel_id=1, source_target_pairs={{0,8},{8,16},{16,24},{24,32},{32,40},{40,48},{48,56},{56,64},{64,7... | collective-permute-start | bytes 1160 | tf_op jit(solution)/shard_map/ppermute | solution.py:29
  21.0 1.0 copy-start.2
  22.0 0.7 copy-start.7
  24.8 25.6 %copy-start.9 = (bf16[96,768]{1,0:T(8,128)(2,1)S(1)}, bf16[96,768]{1,0:T(8,128)(2,1)}, u32[]{:S(2)}) copy-start(bf16[96,768]{1,0:T(8,128)(2,1)} %param.6) | copy-start | bytes 442372
  48.5 5.3 %collective-permute-start.2 = (bf16[384,2048]{1,0:T(8,128)(2,1)S(1)}, bf16[384,2048]{1,0:T(8,128)(2,1)S(1)}, u32[]{:S(2)}, u32[]{:S(2)}) collective-permute-start(bf16[384,2048]{1,0:T(8,128)(2,1)S(1)} %bitcast.50), channel_id=1, source_target_pairs={{0,1},{1,0},{2,3},{3,2},{4,5},{5,4},{6,7},{7,6},{8,9},{9,8},{10,11... | collective-permute-start | bytes 4718600 | tf_op jit(solution)/shard_map/ppermute | solution.py:24
  50.7 1.1 copy-start
  53.8 24.3 %copy-start.1 = (f32[96,2048]{1,0:T(8,128)S(1)}, f32[96,2048]{1,0:T(8,128)}, u32[]{:S(2)}) copy-start(f32[96,2048]{1,0:T(8,128)} %targets.3) | copy-start | bytes 2359300
  80.5 3.6 %copy-start.4 = (bf16[96,2048]{1,0:T(8,128)(2,1)}, bf16[96,2048]{1,0:T(8,128)(2,1)S(1)}, u32[]{:S(2)}) copy-start(bf16[96,2048]{1,0:T(8,128)(2,1)S(1)} %get-tuple-element.26.grad) | copy-start | bytes 1179652
  80.5 10.0 %collective-permute-start.3 = (bf16[384,2048]{1,0:T(8,128)(2,1)}, bf16[384,2048]{1,0:T(8,128)(2,1)}, u32[]{:S(2)}, u32[]{:S(2)}) collective-permute-start(bf16[384,2048]{1,0:T(8,128)(2,1)} %get-tuple-element.27), channel_id=1, source_target_pairs={{0,1},{1,0},{2,3},{3,2},{4,5},{5,4},{6,7},{7,6},{8,9},{9,8},{10,11... | collective-permute-start | bytes 4718600 | tf_op jit(solution)/shard_map/ppermute | solution.py:24
  84.1 0.7 copy-start.6
  84.9 32.8 %copy-start.3 = (bf16[96,2048]{1,0:T(8,128)(2,1)S(1)}, bf16[96,2048]{1,0:T(8,128)(2,1)}, u32[]{:S(2)}) copy-start(bf16[96,2048]{1,0:T(8,128)(2,1)} %cells.1) | copy-start | bytes 1179652
  84.9 32.8 %copy-start.8 = (bf16[5,96]{1,0:T(8,128)(2,1)S(1)}, bf16[5,96]{1,0:T(8,128)(2,1)}, u32[]{:S(2)}) copy-start(bf16[5,96]{1,0:T(8,128)(2,1)} %tap.5) | copy-start | bytes 2884
  84.9 19.3 %all-to-all-start.2 = ((f32[4,24,768]{2,1,0:T(8,128)}), f32[4,24,768]{2,1,0:T(8,128)}, u32[]{:S(2)}, u32[]{:S(2)}) async-start(f32[4,24,768]{2,1,0:T(8,128)} %bitcast.57), calls=%async_computation.2 | async-start | bytes 589824 | tf_op jit(solution)/shard_map/all_to_all | solution.py:528
  90.5 1.0 copy-start.5
  94.4 15.6 %collective-permute-start.4 = (bf16[96,2048]{1,0:T(8,128)(2,1)}, bf16[96,2048]{1,0:T(8,128)(2,1)S(1)}, u32[]{:S(2)}, u32[]{:S(2)}) collective-permute-start(bf16[96,2048]{1,0:T(8,128)(2,1)} %get-tuple-element.29), channel_id=1, source_target_pairs={{0,4},{2,6},{4,0},{6,2},{1,5},{3,7},{5,1},{7,3},{8,12},{10,14},{12... | collective-permute-start | bytes 1179656 | tf_op jit(solution)/shard_map/ppermute | solution.py:20
  97.1 20.5 %collective-permute-start.5 = (bf16[96,2048]{1,0:T(8,128)(2,1)S(1)}, bf16[96,2048]{1,0:T(8,128)(2,1)S(1)}, u32[]{:S(2)}, u32[]{:S(2)}) collective-permute-start(bf16[96,2048]{1,0:T(8,128)(2,1)S(1)} %get-tuple-element.30), channel_id=1, source_target_pairs={{0,2},{2,4},{4,6},{6,0},{1,3},{3,5},{5,7},{7,1},{8,10},{10,12},{12... | collective-permute-start | bytes 1179656 | tf_op jit(solution)/shard_map/ppermute | solution.py:20
  100.2 17.4 %collective-permute-start.6 = (bf16[96,2048]{1,0:T(8,128)(2,1)}, bf16[96,2048]{1,0:T(8,128)(2,1)S(1)}, u32[]{:S(2)}, u32[]{:S(2)}) collective-permute-start(bf16[96,2048]{1,0:T(8,128)(2,1)} %get-tuple-element.31), channel_id=1, source_target_pairs={{0,6},{2,0},{4,2},{6,4},{1,7},{3,1},{5,3},{7,5},{8,14},{10,8},{12,... | collective-permute-start | bytes 1179656 | tf_op jit(solution)/shard_map/ppermute | solution.py:20
  105.8 16.3 %all-to-all-start.3 = ((f32[16,1,1152]{2,1,0:T(1,128)}), f32[16,1,1152]{2,1,0:T(1,128)S(1)}, u32[]{:S(2)}, u32[]{:S(2)}) async-start(f32[16,1,1152]{2,1,0:T(1,128)} %sum_to_rows.1), calls=%async_computation.3 | async-start | bytes 147456 | tf_op jit(solution)/shard_map/all_to_all | solution.py:532
  123.8 27.8 %all-to-all-start.4 = ((bf16[64,2,1152]{2,1,0:T(2,128)(2,1)}), bf16[64,2,1152]{2,1,0:T(2,128)(2,1)S(1)}, u32[]{:S(2)}, u32[]{:S(2)}) async-start(bf16[64,2,1152]{2,1,0:T(2,128)(2,1)} %copy.20), calls=%async_computation.4 | async-start | bytes 589824 | tf_op jit(solution)/shard_map/all_to_all | solution.py:550

commit v6 on v5

--- a/solution.py
+++ b/solution.py
@@ -44,70 +44,98 @@
     return square[...].T
 
 
-def forward_kernel(
-    cells_hbm, left, right, tap_hbm, hidden, line, square, columns, cells, tap, sems
-):
-    reads = [
-        pltpu.make_async_copy(tap_hbm, tap, sems.at[0]),
-        pltpu.make_async_copy(cells_hbm, cells, sems.at[1]),
-    ]
-    for read in reads:
-        read.start()
-    reach = left.shape[1]
+def forward_kernel(cells, tap, hidden, line, square, columns):
+    rows = 16
     count = cells.shape[1]
-    line[:, :LANES] = jnp.zeros((cells.shape[0], LANES), F32)
-    line[:, LANES + count :] = jnp.zeros((cells.shape[0], LANES), F32)
-    line[:, LANES - reach : LANES] = left[...].astype(F32)
-    line[:, LANES + count : LANES + count + reach] = right[...].astype(F32)
-    rows = 8
-    reads[0].wait()
+    reach = tap.shape[0] // 2
     columns[...] = tap_columns(tap, square)
-    reads[1].wait()
-    line[:, LANES : LANES + count] = cells[...].astype(F32)
-
-    @pl.loop(0, cells.shape[0] // 16)
+    line[:, :LANES] = jnp.zeros((rows, LANES), F32)
+    line[:, LANES + count :] = jnp.zeros((rows, LANES), F32)
+
+    @pl.loop(0, cells.shape[0] // rows)
     def _(block):
-        both_hidden = []
-        for part in range(2):
-            at = pl.ds(pl.multiple_of(block * 16 + part * rows, rows), rows)
-            whole = line[at, :]
-            taps = columns[at, :]
-            conv = jnp.zeros((rows, count), F32)
-            for k in range(2 * reach + 1):
-                shift = (reach - k) % whole.shape[1]
-                moved = pltpu.roll(whole, shift, 1) if shift else whole
-                conv = conv + taps[:, k : k + 1] * moved[:, LANES : LANES + count]
-            sig = jax.nn.sigmoid(conv)
-            both_hidden.append((conv * sig).astype(BF16))
-        out = pl.ds(pl.multiple_of(block * 16, 16), 16)
-        hidden[out, :] = jnp.concatenate(both_hidden, axis=0)
-
-
-def forward(cells, left, right, tap):
+        at = pl.ds(pl.multiple_of(block * rows, rows), rows)
+        line[:, LANES : LANES + count] = cells[at, :].astype(F32)
+        whole = line[...]
+        taps = columns[at, :]
+        conv = jnp.zeros((rows, count), F32)
+        for k in range(2 * reach + 1):
+            shift = (reach - k) % whole.shape[1]
+            moved = pltpu.roll(whole, shift, 1) if shift else whole
+            conv = conv + taps[:, k : k + 1] * moved[:, LANES : LANES + count]
+        hidden[at, :] = (conv * jax.nn.sigmoid(conv)).astype(BF16)
+
+
+def forward(cells, tap):
     rows, count = cells.shape
     return pl.pallas_call(
         forward_kernel,
         out_shape=jax.ShapeDtypeStruct((rows, count), BF16),
-        in_specs=[
-            pl.BlockSpec(memory_space=pl.ANY),
-            pl.BlockSpec(memory_space=pltpu.VMEM),
-            pl.BlockSpec(memory_space=pltpu.VMEM),
-            pl.BlockSpec(memory_space=pl.ANY),
-        ],
         scratch_shapes=[
-            pltpu.VMEM((rows, count + 2 * LANES), F32),
+            pltpu.VMEM((16, count + 2 * LANES), F32),
             pltpu.VMEM((8, LANES), F32),
             pltpu.VMEM((LANES, 8), F32),
-            pltpu.VMEM(cells.shape, cells.dtype),
-            pltpu.VMEM(tap.shape, tap.dtype),
+        ],
+        compiler_params=pltpu.CompilerParams(vmem_limit_bytes=4 * 2**20),
+        cost_estimate=pl.CostEstimate(
+            flops=20 * rows * count, bytes_accessed=4 * rows * count, transcendentals=rows * count
+        ),
+        name="conv_silu",
+    )(cells, tap)
+
+
+def rim_kernel(cells, left, right, tap, given, hidden, line, square, columns, tiles, sems):
+    del given
+    width, count = cells.shape
+    reach = left.shape[1]
+    columns[...] = tap_columns(tap, square)
+    taps = columns[:width, :]
+    line[...] = jnp.zeros(line.shape, F32)
+    writes = []
+    for side, at in enumerate((0, count - LANES)):
+        line[:, LANES : 2 * LANES] = cells[:, at : at + LANES].astype(F32)
+        if side == 0:
+            line[:, LANES - reach : LANES] = left[...].astype(F32)
+            line[:, 2 * LANES :] = cells[:, at + LANES : at + 2 * LANES].astype(F32)
+        else:
+            line[:, :LANES] = cells[:, at - LANES : at].astype(F32)
+            line[:, 2 * LANES : 2 * LANES + reach] = right[...].astype(F32)
+        whole = line[...]
+        conv = jnp.zeros((width, LANES), F32)
+        for k in range(2 * reach + 1):
+            shift = (reach - k) % whole.shape[1]
+            moved = pltpu.roll(whole, shift, 1) if shift else whole
+            conv = conv + taps[:, k : k + 1] * moved[:, LANES : 2 * LANES]
+        tiles[side] = (conv * jax.nn.sigmoid(conv)).astype(BF16)
+        spot = hidden.at[:, pl.ds(at, LANES)]
+        writes.append(pltpu.make_async_copy(tiles.at[side], spot, sems.at[side]))
+        writes[side].start()
+    for write in writes:
+        write.wait()
+
+
+def with_rim(cells, left, right, tap, hidden):
+    width, _ = cells.shape
+    return pl.pallas_call(
+        rim_kernel,
+        out_shape=jax.ShapeDtypeStruct(hidden.shape, hidden.dtype),
+        in_specs=[pl.BlockSpec(memory_space=pltpu.VMEM)] * 4
+        + [pl.BlockSpec(memory_space=pl.ANY)],
+        out_specs=pl.BlockSpec(memory_space=pl.ANY),
+        input_output_aliases={4: 0},
+        scratch_shapes=[
+            pltpu.VMEM((width, 3 * LANES), F32),
+            pltpu.VMEM((8, LANES), F32),
+            pltpu.VMEM((LANES, 8), F32),
+            pltpu.VMEM((2, width, LANES), BF16),
             pltpu.SemaphoreType.DMA((2,)),
         ],
-        compiler_params=pltpu.CompilerParams(vmem_limit_bytes=8 * 2**20),
+        compiler_params=pltpu.CompilerParams(vmem_limit_bytes=4 * 2**20),
         cost_estimate=pl.CostEstimate(
-            flops=20 * rows * count, bytes_accessed=4 * rows * count, transcendentals=rows * count
-        ),
-        name="conv_silu",
-    )(cells, left, right, tap)
+            flops=40 * width * LANES, bytes_accessed=8 * width * LANES, transcendentals=0
+        ),
+        name="outer_columns",
+    )(cells, left, right, tap, hidden)
 
 
 def pick_rows(weight, picked, blocks):
@@ -502,7 +530,7 @@
 
     place = jnp.stack([y, c])
     left, right = outer_columns(embeddings, reach)
-    block = forward(embeddings, left, right, taps)
+    block = with_rim(embeddings, left, right, taps, forward(embeddings, taps))
 
     mine = lax.all_to_all(
         jnp.broadcast_to(block[None], (ny, width, count)), "y", 0, 0, tiled=True
@@ -525,12 +553,13 @@
     nx, nz = lax.axis_size("x"), lax.axis_size("z")
     late_grad, _ = lax.optimization_barrier((logit_grad, sent))
     local = outer_product(place, late_grad, mine, theirs)
-    part = lax.all_to_all(local.reshape(nx, tracks // nx, features), "x", 0, 0, tiled=True)
-
     own, *blocks = scatter_blocks(place, weight, logit_grad, received)
     parts = [along_y(blocks[shift - 1], shift) for shift in (2, 1, 3)]
-    part = lax.all_to_all(sum_to_rows(part, nz), "z", 0, 0, tiled=True)
-
+
+    local, own = lax.optimization_barrier((local, own))
+    part = lax.all_to_all(local.reshape(nx, tracks // nx, features), "x", 0, 0, tiled=True)
+    part, own = lax.optimization_barrier((sum_to_rows(part, nz), own))
+    part = lax.all_to_all(part, "z", 0, 0, tiled=True)
     conv_grad, found = backward(own, parts, embeddings, left, right, taps)
     part, found = lax.optimization_barrier((part, found))
     part = jnp.sum(part, axis=0).reshape(-1)

time: 155 us -> 149 us (0.961)
  Pallas kernels: 19 us -> 16.5 us
  local copies, waits for them, and re-layouts: 7.5 us -> 5.79 us
  waiting for transfers between devices: 36.1 us -> 34.4 us
    ppermute x1, waiting for transfers between devices: 5.89 us -> 2.93 us  [outer_columns(): lax.ppermute(cells[:, -width:], SEQ, [(i, i + 1) for i in range(count - 1)])]
    unnamed x22 -> x16, local copies, waits for them, and re-layouts: 4.71 us -> 3 us
  transfers between devices with their start and end apart: 10 -> 10, of which waited for: 6 -> 7; matrix products, arithmetic and copies ran while one was open for 0% -> 0% of each run, Pallas kernels for 8% -> 7%
where the time goes in v6:
time: 149 us; the launch traced here: 148 us
  blocking collectives  47.1 us (32%)
  starting transfers between devices  42.2 us (28%)
  waiting for transfers between devices  34.4 us (23%)
  Pallas kernels  16.5 us (11%)
  local copies, waits for them, and re-layouts  5.79 us (4%)
    all_to_all x1, blocking collectives, shards(): lax.all_to_all(jnp.broadcast_to(block[None], (ny, width, count)), 'y', 0,...  23.7 us
    all_to_all x1, blocking collectives, share(): return lax.all_to_all(copies, axes, 0, 0, tiled=True)[:, 0]  23.4 us
    all_to_all x1, waiting for transfers between devices, shards(): slab = lax.all_to_all(message, SEQ, 0, 0, tiled=True)  19.4 us
    ppermute x1, starting transfers between devices, outer_columns(): lax.ppermute(cells[:, :width], SEQ, [(i + 1, i) for i in range(count - 1)])  11.7 us
    ppermute x3, starting transfers between devices, along_y(): lax.ppermute(value, 'y', [(i, (i + shift) % count) for i in range(count)])  9.76 us
    ppermute x3, waiting for transfers between devices, along_y(): lax.ppermute(value, 'y', [(i, (i + shift) % count) for i in range(count)])  8.88 us
    pallas_call x5, Pallas kernels, kernel_call(): pl.pallas_call(body, out_shape=outs, in_specs=[pl.BlockSpec(memory_space=...  7.87 us
    all_to_all x1, starting transfers between devices, shards(): slab = lax.all_to_all(message, SEQ, 0, 0, tiled=True)  6.68 us
  transfers between devices with their start and end apart: 10, of which 7 were waited for; matrix products, arithmetic and copies ran while one was open for 0% of the time, Pallas kernels for 7%

profile of v6, /device:TPU:6, one launch (start us, length us, event | category | flops | bytes accessed | tf_op | source)
XLA Modules:
  0.0 148.2 jit_solution(8307805024713651382)
XLA Ops:
  1.5 11.7 %collective-permute-start.1 = (bf16[96,2]{1,0:T(8,128)(2,1)S(1)}, bf16[96,2]{1,0:T(8,128)(2,1)S(1)}, u32[]{:S(2)}, u32[]{:S(2)}) collective-permute-start(bf16[96,2]{1,0:T(8,128)(2,1)S(1)} %get-tuple-element.50), channel_id=1, source_target_pairs={{8,0},{16,8},{24,16},{32,24},{40,32},{48,40},{56,48},{64,56},{72,6... | collective-permute-start | bytes 1160 | tf_op jit(solution)/shard_map/ppermute | solution.py:30
  13.1 1.9 %collective-permute-start = (bf16[96,2]{1,0:T(8,128)(2,1)S(1)}, bf16[96,2]{1,0:T(8,128)(2,1)S(1)}, u32[]{:S(2)}, u32[]{:S(2)}) collective-permute-start(bf16[96,2]{1,0:T(8,128)(2,1)S(1)} %get-tuple-element.51), channel_id=1, source_target_pairs={{0,8},{8,16},{16,24},{24,32},{32,40},{40,48},{48,56},{56,64},{64,7... | collective-permute-start | bytes 1160 | tf_op jit(solution)/shard_map/ppermute | solution.py:29
  16.7 1.3 conv_silu.1.given
  18.0 2.9 %collective-permute-done.left = bf16[96,2]{1,0:T(8,128)(2,1)S(1)} collective-permute-done((bf16[96,2]{1,0:T(8,128)(2,1)S(1)}, bf16[96,2]{1,0:T(8,128)(2,1)S(1)}, u32[]{:S(2)}, u32[]{:S(2)}) %collective-permute-start) | collective-permute-done | bytes 416 | tf_op jit(solution)/shard_map/ppermute | solution.py:29
  21.7 23.7 %all_to_all.25 = bf16[4,96,2048]{2,1,0:T(8,128)(2,1)S(1)} all-to-all(bf16[4,96,2048]{2,1,0:T(8,128)(2,1)S(1)} %broadcast_in_dim.70), channel_id=1, replica_groups=mesh['x'=4,'z'=16,'y'=4,'c'=2] {'y'}, dimensions={0} | all-to-all | bytes 3145728 | tf_op jit(solution)/shard_map/all_to_all | solution.py:535
  45.4 1.9 %collective-permute-start.2 = (bf16[384,2048]{1,0:T(8,128)(2,1)S(1)}, bf16[384,2048]{1,0:T(8,128)(2,1)S(1)}, u32[]{:S(2)}, u32[]{:S(2)}) collective-permute-start(bf16[384,2048]{1,0:T(8,128)(2,1)S(1)} %bitcast.50), channel_id=1, source_target_pairs={{0,1},{1,0},{2,3},{3,2},{4,5},{5,4},{6,7},{7,6},{8,9},{9,8},{10,11... | collective-permute-start | bytes 4718600 | tf_op jit(solution)/shard_map/ppermute | solution.py:24
  50.7 1.3 far_logits.1
  52.1 23.4 %all_to_all.26 = f32[64,1,384]{2,1,0:T(1,128)S(1)} all-to-all(f32[64,1,384]{2,1,0:T(1,128)S(1)} %broadcast_in_dim.72), channel_id=1, replica_groups=mesh['x'=4,'z'=16,'y'=4,'c'=2] {'x','z'}, dimensions={0} | all-to-all | bytes 196608 | tf_op jit(solution)/shard_map/all_to_all | solution.py:37
  76.8 1.9 %collective-permute-start.3 = (bf16[384,2048]{1,0:T(8,128)(2,1)S(1)}, bf16[384,2048]{1,0:T(8,128)(2,1)S(1)}, u32[]{:S(2)}, u32[]{:S(2)}) collective-permute-start(bf16[384,2048]{1,0:T(8,128)(2,1)S(1)} %get-tuple-element.31), channel_id=1, source_target_pairs={{0,1},{1,0},{2,3},{3,2},{4,5},{5,4},{6,7},{7,6},{8,9},{9,8},{10,11... | collective-permute-start | bytes 4718600 | tf_op jit(solution)/shard_map/ppermute | solution.py:24
  78.7 2.4 %weight_part.1 = f32[96,768]{1,0:T(8,128)} custom-call(s32[2]{0:T(128)S(1)} %pad_add_fusion.place, bf16[96,2048]{1,0:T(8,128)(2,1)S(1)} %get-tuple-element.30.grad, bf16[384,2048]{1,0:T(8,128)(2,1)S(1)} %bitcast.52, bf16[384,2048]{1,0:T(8,128)(2,1)S(1)} %collective-permute-done.2.hidden.theirs), custom_call_target="tpu_custom_call" | custom-call | flops 301989888 | bytes 3833856 | tf_op jit(solution)/shard_map/weight_part/pallas_call | solution.py:175
  82.1 1.9 %core_sum.1 = (f32[96,2048]{1,0:T(8,128)S(1)}, bf16[96,2048]{1,0:T(8,128)(2,1)}, bf16[96,2048]{1,0:T(8,128)(2,1)}, bf16[96,2048]{1,0:T(8,128)(2,1)S(1)}) custom-call(s32[2]{0:T(128)S(1)} %pad_add_fusion.place, bf16[768,96]{1,0:T(8,128)(2,1)S(1)} %bitcast.56, bf16[96,2048]{1,0:T(8,128)(2,1)S(1)} %get-tuple-element.30.grad, ...), custom_call_target="tpu_custom_call" | custom-call | flops 150994944 | bytes 4079616 | tf_op jit(solution)/shard_map/core_sum/pallas_call | solution.py:175
  84.0 4.9 %all-to-all-start.2 = ((f32[4,24,768]{2,1,0:T(8,128)}), f32[4,24,768]{2,1,0:T(8,128)S(1)}, u32[]{:S(2)}, u32[]{:S(2)}) async-start(f32[4,24,768]{2,1,0:T(8,128)} %bitcast.10), calls=%async_computation.2 | async-start | bytes 589824 | tf_op jit(solution)/shard_map/all_to_all | solution.py:560
  88.9 2.7 %collective-permute-start.4 = (bf16[96,2048]{1,0:T(8,128)(2,1)}, bf16[96,2048]{1,0:T(8,128)(2,1)S(1)}, u32[]{:S(2)}, u32[]{:S(2)}) collective-permute-start(bf16[96,2048]{1,0:T(8,128)(2,1)} %get-tuple-element.37), channel_id=1, source_target_pairs={{0,4},{2,6},{4,0},{6,2},{1,5},{3,7},{5,1},{7,3},{8,12},{10,14},{12... | collective-permute-start | bytes 1179656 | tf_op jit(solution)/shard_map/ppermute | solution.py:20
  91.7 3.1 %collective-permute-start.5 = (bf16[96,2048]{1,0:T(8,128)(2,1)}, bf16[96,2048]{1,0:T(8,128)(2,1)S(1)}, u32[]{:S(2)}, u32[]{:S(2)}) collective-permute-start(bf16[96,2048]{1,0:T(8,128)(2,1)} %get-tuple-element.38), channel_id=1, source_target_pairs={{0,2},{2,4},{4,6},{6,0},{1,3},{3,5},{5,7},{7,1},{8,10},{10,12},{12... | collective-permute-start | bytes 1179656 | tf_op jit(solution)/shard_map/ppermute | solution.py:20
  94.8 3.9 %collective-permute-start.6 = (bf16[96,2048]{1,0:T(8,128)(2,1)S(1)}, bf16[96,2048]{1,0:T(8,128)(2,1)S(1)}, u32[]{:S(2)}, u32[]{:S(2)}) collective-permute-start(bf16[96,2048]{1,0:T(8,128)(2,1)S(1)} %get-tuple-element.39), channel_id=1, source_target_pairs={{0,6},{2,0},{4,2},{6,4},{1,7},{3,1},{5,3},{7,5},{8,14},{10,8},{12,... | collective-permute-start | bytes 1179656 | tf_op jit(solution)/shard_map/ppermute | solution.py:20
  99.4 3.5 %all-to-all-start.3 = ((f32[16,1,1152]{2,1,0:T(1,128)}), f32[16,1,1152]{2,1,0:T(1,128)S(1)}, u32[]{:S(2)}, u32[]{:S(2)}) async-start(f32[16,1,1152]{2,1,0:T(1,128)} %sum_to_rows.1), calls=%async_computation.3 | async-start | bytes 147456 | tf_op jit(solution)/shard_map/all_to_all | solution.py:562
  103.0 1.6 %collective-permute-done.4.one = bf16[96,2048]{1,0:T(8,128)(2,1)S(1)} collective-permute-done((bf16[96,2048]{1,0:T(8,128)(2,1)}, bf16[96,2048]{1,0:T(8,128)(2,1)S(1)}, u32[]{:S(2)}, u32[]{:S(2)}) %collective-permute-start.4) | collective-permute-done | bytes 393248 | tf_op jit(solution)/shard_map/ppermute | solution.py:20
  104.6 7.3 %collective-permute-done.5.two = bf16[96,2048]{1,0:T(8,128)(2,1)S(1)} collective-permute-done((bf16[96,2048]{1,0:T(8,128)(2,1)}, bf16[96,2048]{1,0:T(8,128)(2,1)S(1)}, u32[]{:S(2)}, u32[]{:S(2)}) %collective-permute-start.5) | collective-permute-done | bytes 393248 | tf_op jit(solution)/shard_map/ppermute | solution.py:20
  111.8 2.5 %conv_grad.1 = (bf16[96,2048]{1,0:T(8,128)(2,1)S(1)}, f32[16,96]{1,0:T(8,128)S(1)}) custom-call(f32[96,2048]{1,0:T(8,128)S(1)} %get-tuple-element.36.mine, bf16[96,2048]{1,0:T(8,128)(2,1)S(1)} %collective-permute-done.4.one, bf16[96,2048]{1,0:T(8,128)(2,1)S(1)} %collective-permute-done.5.two, bf16[96,2048]{1,0:T(8,128)(2,1)S(1)} %collective-permute-done.6.three, ...), custom_call_target="tpu_custom_call" | custom-call | flops 7864320 | bytes 2752512 | tf_op jit(solution)/shard_map/conv_grad/pallas_call | solution.py:366
  114.4 1.3 all-to-all-done.3
  117.4 6.7 %all-to-all-start.4 = ((bf16[64,2,1152]{2,1,0:T(2,128)(2,1)}), bf16[64,2,1152]{2,1,0:T(2,128)(2,1)S(1)}, u32[]{:S(2)}, u32[]{:S(2)}) async-start(bf16[64,2,1152]{2,1,0:T(2,128)(2,1)} %copy.21), calls=%async_computation.4 | async-start | bytes 589824 | tf_op jit(solution)/shard_map/all_to_all | solution.py:579
  124.1 1.9 %embed_grad.1 = (bf16[96,2048]{1,0:T(8,128)(2,1)}, f32[96,256]{1,0:T(8,128)S(1)}) custom-call(bf16[96,2048]{1,0:T(8,128)(2,1)S(1)} %get-tuple-element.43.grad, bf16[5,96]{1,0:T(8,128)(2,1)S(1)} %copy-done.5), custom_call_target="tpu_custom_call" | custom-call | flops 1966080 | bytes 786432 | tf_op jit(solution)/shard_map/embed_grad/pallas_call | solution.py:417
  126.0 19.4 %all-to-all-done.4 = bf16[64,2,1152]{2,1,0:T(2,128)(2,1)S(1)} async-done(((bf16[64,2,1152]{2,1,0:T(2,128)(2,1)}), bf16[64,2,1152]{2,1,0:T(2,128)(2,1)S(1)}, u32[]{:S(2)}, u32[]{:S(2)}) %all-to-all-start.4) | async-done | bytes 294944 | tf_op jit(solution)/shard_map/all_to_all | solution.py:579
  146.5 1.7 %finish.1 = (bf16[96,2048]{1,0:T(8,128)(2,1)}, f32[5,96]{1,0:T(8,128)}) custom-call(s32[1]{0:T(128)} %bitcast.place, f32[64,1152]{1,0:T(8,128)S(1)} %fusion.1.slab, f32[96,256]{1,0:T(8,128)S(1)} %get-tuple-element.44.ends, bf16[5,96]{1,0:T(8,128)(2,1)S(1)} %copy-done.5, bf16[96,2048]{1,0:T(8,128)(2,1)} %get-tuple-element.45.given), custom_call_target="tpu_custom_call", output_to_operand_aliasing={{0}: (4, {})} | custom-call | flops 73728 | bytes 589824 | tf_op jit(solution)/shard_map/finish/pallas_call | solution.py:489
  (52 shorter events, 12.5 us)
Async XLA Ops:
  1.5 16.6 %collective-permute-start.1 = (bf16[96,2]{1,0:T(8,128)(2,1)S(1)}, bf16[96,2]{1,0:T(8,128)(2,1)S(1)}, u32[]{:S(2)}, u32[]{:S(2)}) collective-permute-start(bf16[96,2]{1,0:T(8,128)(2,1)S(1)} %get-tuple-element.50), channel_id=1, source_target_pairs={{8,0},{16,8},{24,16},{32,24},{40,32},{48,40},{56,48},{64,56},{72,6... | collective-permute-start | bytes 1160 | tf_op jit(solution)/shard_map/ppermute | solution.py:30
  13.1 7.8 %collective-permute-start = (bf16[96,2]{1,0:T(8,128)(2,1)S(1)}, bf16[96,2]{1,0:T(8,128)(2,1)S(1)}, u32[]{:S(2)}, u32[]{:S(2)}) collective-permute-start(bf16[96,2]{1,0:T(8,128)(2,1)S(1)} %get-tuple-element.51), channel_id=1, source_target_pairs={{0,8},{8,16},{16,24},{24,32},{32,40},{40,48},{48,56},{56,64},{64,7... | collective-permute-start | bytes 1160 | tf_op jit(solution)/shard_map/ppermute | solution.py:29
  15.1 1.0 copy-start
  16.1 0.7 copy-start.4
  21.7 25.6 %copy-start.6 = (bf16[96,768]{1,0:T(8,128)(2,1)S(1)}, bf16[96,768]{1,0:T(8,128)(2,1)}, u32[]{:S(2)}) copy-start(bf16[96,768]{1,0:T(8,128)(2,1)} %param.6) | copy-start | bytes 442372
  45.4 5.3 %collective-permute-start.2 = (bf16[384,2048]{1,0:T(8,128)(2,1)S(1)}, bf16[384,2048]{1,0:T(8,128)(2,1)S(1)}, u32[]{:S(2)}, u32[]{:S(2)}) collective-permute-start(bf16[384,2048]{1,0:T(8,128)(2,1)S(1)} %bitcast.50), channel_id=1, source_target_pairs={{0,1},{1,0},{2,3},{3,2},{4,5},{5,4},{6,7},{7,6},{8,9},{9,8},{10,11... | collective-permute-start | bytes 4718600 | tf_op jit(solution)/shard_map/ppermute | solution.py:24
  47.6 1.1 copy-start.2
  50.7 24.9 %copy-start.3 = (f32[96,2048]{1,0:T(8,128)S(1)}, f32[96,2048]{1,0:T(8,128)}, u32[]{:S(2)}) copy-start(f32[96,2048]{1,0:T(8,128)} %targets.3) | copy-start | bytes 2359300
  76.8 5.3 %collective-permute-start.3 = (bf16[384,2048]{1,0:T(8,128)(2,1)S(1)}, bf16[384,2048]{1,0:T(8,128)(2,1)S(1)}, u32[]{:S(2)}, u32[]{:S(2)}) collective-permute-start(bf16[384,2048]{1,0:T(8,128)(2,1)S(1)} %get-tuple-element.31), channel_id=1, source_target_pairs={{0,1},{1,0},{2,3},{3,2},{4,5},{5,4},{6,7},{7,6},{8,9},{9,8},{10,11... | collective-permute-start | bytes 4718600 | tf_op jit(solution)/shard_map/ppermute | solution.py:24
  81.1 30.7 %copy-start.1 = (bf16[96,2048]{1,0:T(8,128)(2,1)S(1)}, bf16[96,2048]{1,0:T(8,128)(2,1)}, u32[]{:S(2)}) copy-start(bf16[96,2048]{1,0:T(8,128)(2,1)} %cells.5) | copy-start | bytes 1179652
  81.1 30.7 %copy-start.5 = (bf16[5,96]{1,0:T(8,128)(2,1)S(1)}, bf16[5,96]{1,0:T(8,128)(2,1)}, u32[]{:S(2)}) copy-start(bf16[5,96]{1,0:T(8,128)(2,1)} %tap.9) | copy-start | bytes 2884
  84.0 14.7 %all-to-all-start.2 = ((f32[4,24,768]{2,1,0:T(8,128)}), f32[4,24,768]{2,1,0:T(8,128)S(1)}, u32[]{:S(2)}, u32[]{:S(2)}) async-start(f32[4,24,768]{2,1,0:T(8,128)} %bitcast.10), calls=%async_computation.2 | async-start | bytes 589824 | tf_op jit(solution)/shard_map/all_to_all | solution.py:560
  88.9 15.6 %collective-permute-start.4 = (bf16[96,2048]{1,0:T(8,128)(2,1)}, bf16[96,2048]{1,0:T(8,128)(2,1)S(1)}, u32[]{:S(2)}, u32[]{:S(2)}) collective-permute-start(bf16[96,2048]{1,0:T(8,128)(2,1)} %get-tuple-element.37), channel_id=1, source_target_pairs={{0,4},{2,6},{4,0},{6,2},{1,5},{3,7},{5,1},{7,3},{8,12},{10,14},{12... | collective-permute-start | bytes 1179656 | tf_op jit(solution)/shard_map/ppermute | solution.py:20
  91.7 20.2 %collective-permute-start.5 = (bf16[96,2048]{1,0:T(8,128)(2,1)}, bf16[96,2048]{1,0:T(8,128)(2,1)S(1)}, u32[]{:S(2)}, u32[]{:S(2)}) collective-permute-start(bf16[96,2048]{1,0:T(8,128)(2,1)} %get-tuple-element.38), channel_id=1, source_target_pairs={{0,2},{2,4},{4,6},{6,0},{1,3},{3,5},{5,7},{7,1},{8,10},{10,12},{12... | collective-permute-start | bytes 1179656 | tf_op jit(solution)/shard_map/ppermute | solution.py:20
  94.8 17.1 %collective-permute-start.6 = (bf16[96,2048]{1,0:T(8,128)(2,1)S(1)}, bf16[96,2048]{1,0:T(8,128)(2,1)S(1)}, u32[]{:S(2)}, u32[]{:S(2)}) collective-permute-start(bf16[96,2048]{1,0:T(8,128)(2,1)S(1)} %get-tuple-element.39), channel_id=1, source_target_pairs={{0,6},{2,0},{4,2},{6,4},{1,7},{3,1},{5,3},{7,5},{8,14},{10,8},{12,... | collective-permute-start | bytes 1179656 | tf_op jit(solution)/shard_map/ppermute | solution.py:20
  99.4 16.3 %all-to-all-start.3 = ((f32[16,1,1152]{2,1,0:T(1,128)}), f32[16,1,1152]{2,1,0:T(1,128)S(1)}, u32[]{:S(2)}, u32[]{:S(2)}) async-start(f32[16,1,1152]{2,1,0:T(1,128)} %sum_to_rows.1), calls=%async_computation.3 | async-start | bytes 147456 | tf_op jit(solution)/shard_map/all_to_all | solution.py:562
  117.4 28.0 %all-to-all-start.4 = ((bf16[64,2,1152]{2,1,0:T(2,128)(2,1)}), bf16[64,2,1152]{2,1,0:T(2,128)(2,1)S(1)}, u32[]{:S(2)}, u32[]{:S(2)}) async-start(bf16[64,2,1152]{2,1,0:T(2,128)(2,1)} %copy.21), calls=%async_computation.4 | async-start | bytes 589824 | tf_op jit(solution)/shard_map/all_to_all | solution.py:579

commit v7 on v6

--- a/solution.py
+++ b/solution.py
@@ -300,12 +300,6 @@
         cost_estimate=pl.CostEstimate(flops=4 * size, bytes_accessed=20 * size, transcendentals=0),
         name="sum_to_rows",
     )(parts)
-
-
-def from_rows(rows, tracks, features):
-    tiles = rows.reshape(-1, 8, rows.shape[1] // LANES, LANES).transpose(0, 2, 1, 3)
-    tiles = tiles.reshape(tracks // 8, features // LANES, 8, LANES).transpose(0, 2, 1, 3)
-    return tiles.reshape(tracks, features)
 
 
 def backward_kernel(
@@ -433,23 +427,78 @@
     )(grad, tap)
 
 
+def message_kernel(place, slices, found, out, rows, mixed):
+    me = place[0]
+    devices, _, size = out.shape
+    width = found.shape[1]
+    ntaps, reach = place_taps(size, width)
+    rows[...] = jnp.zeros(rows.shape, F32)
+    rows[:, :width] = found[...]
+    taps = rows[0:8, :]
+    high = taps.astype(BF16).astype(F32)
+    low = taps - high
+    parts = [high[k : k + 1] for k in range(ntaps)] + [low[k : k + 1] for k in range(ntaps)]
+    sides = [rows[8 + k : 9 + k, :] for k in range(2 * reach)]
+
+    def line(pieces, first):
+        total = jnp.zeros((1, size), F32)
+        for n, piece in enumerate(pieces):
+            total = total + (pltpu.roll(piece, (first + n) * width, 1) if first + n else piece)
+        return total
+
+    row = lax.broadcasted_iota(jnp.int32, (devices, size), 0)
+    value = jnp.broadcast_to(line(parts, 0), (devices, size))
+    value = jnp.where(row == me - 1, value + line(sides[:reach], 2 * ntaps), value)
+    value = jnp.where(row == me + 1, value + line(sides[reach:], 2 * ntaps), value)
+    part = jnp.sum(slices[:, 0, :], axis=0, keepdims=True)
+    mixed[:, 0, :] = jnp.broadcast_to(part, (devices, size))
+    mixed[:, 1, :] = value
+    out[...] = mixed[...].astype(BF16)
+
+
+def place_taps(size, width):
+    reach = (size // width - 2) // 5
+    return 2 * reach + 1, reach
+
+
+def last_message(place, slices, found, devices):
+    size = slices.shape[2]
+    return pl.pallas_call(
+        message_kernel,
+        out_shape=jax.ShapeDtypeStruct((devices, 2, size), BF16),
+        in_specs=[pl.BlockSpec(memory_space=pltpu.SMEM)]
+        + [pl.BlockSpec(memory_space=pltpu.VMEM)] * 2,
+        scratch_shapes=[
+            pltpu.VMEM((found.shape[0], size), F32),
+            pltpu.VMEM((devices, 2, size), F32),
+        ],
+        compiler_params=pltpu.CompilerParams(vmem_limit_bytes=6 * 2**20),
+        cost_estimate=pl.CostEstimate(
+            flops=4 * devices * size, bytes_accessed=8 * devices * size, transcendentals=0
+        ),
+        name="message",
+    )(place, slices, found)
+
+
 def finish_kernel(
-    place, slab, ends, tap, given, embed, sums, square, columns, edges, tiles, sems
+    place, slab, ends, tap, given, embed, weight, sums,
+    square, columns, edges, tiles, plain, sems,
 ):
     del given
     ntaps, width = tap.shape
     reach = ntaps // 2
-    devices = slab.shape[0]
+    devices, _, size = slab.shape
     me = place[0]
+    plain[...] = slab[...].astype(F32)
     columns[...] = tap_columns(tap, square)
 
     edges[...] = jnp.zeros(edges.shape, F32)
     start = 2 * ntaps * width
     for side, other in enumerate((me - 1, me + 1)):
-        row = slab[pl.ds(jnp.clip(other, 0, devices - 1), 1), :]
+        row = plain[jnp.clip(other, 0, devices - 1), 1:2, :]
         row = jnp.where((other >= 0) & (other < devices), row, 0.0)
         for k in range(reach):
-            turned = pltpu.roll(row, row.shape[1] - start - k * width, 1)
+            turned = pltpu.roll(row, size - start - k * width, 1)
             edges[side * reach + k : side * reach + k + 1, :] = turned[:, :LANES]
     outer = edges[...].T[:width]
 
@@ -475,21 +524,30 @@
         )
         writes[n].start()
 
-    total = jnp.sum(slab[...], axis=0, keepdims=True)
+    per_row, wide = size // LANES, weight.shape[1] // LANES
+    for tile in range(devices // 8 * per_row):
+        group, spot = tile // per_row, tile % per_row * LANES
+        row, col = tile // wide * 8, tile % wide * LANES
+        weight[row : row + 8, col : col + LANES] = plain[
+            group * 8 : group * 8 + 8, 0, spot : spot + LANES
+        ]
+
+    total = jnp.sum(plain[:, 1, :], axis=0, keepdims=True)
     for k in range(ntaps):
-        high = pltpu.roll(total, total.shape[1] - k * width, 1) if k else total
-        low = pltpu.roll(total, total.shape[1] - (ntaps + k) * width, 1)
+        high = pltpu.roll(total, size - k * width, 1) if k else total
+        low = pltpu.roll(total, size - (ntaps + k) * width, 1)
         sums[k : k + 1, :] = (high + low)[:, :width]
     for write in writes:
         write.wait()
 
 
-def finish(place, slab, ends, tap, embed):
+def finish(place, slab, ends, tap, embed, weight_shape):
     ntaps, width = tap.shape
     return pl.pallas_call(
         finish_kernel,
         out_shape=(
             jax.ShapeDtypeStruct(embed.shape, embed.dtype),
+            jax.ShapeDtypeStruct(weight_shape, F32),
             jax.ShapeDtypeStruct((ntaps, width), F32),
         ),
         in_specs=[pl.BlockSpec(memory_space=pltpu.SMEM)]
@@ -498,6 +556,7 @@
         out_specs=(
             pl.BlockSpec(memory_space=pl.ANY),
             pl.BlockSpec(memory_space=pltpu.VMEM),
+            pl.BlockSpec(memory_space=pltpu.VMEM),
         ),
         input_output_aliases={4: 0},
         scratch_shapes=[
@@ -505,6 +564,7 @@
             pltpu.VMEM((LANES, 8), F32),
             pltpu.VMEM((8, LANES), F32),
             pltpu.VMEM((2, width, LANES), BF16),
+            pltpu.VMEM(slab.shape, F32),
             pltpu.SemaphoreType.DMA((2,)),
         ],
         compiler_params=pltpu.CompilerParams(vmem_limit_bytes=8 * 2**20),
@@ -561,26 +621,12 @@
     part, own = lax.optimization_barrier((sum_to_rows(part, nz), own))
     part = lax.all_to_all(part, "z", 0, 0, tiled=True)
     conv_grad, found = backward(own, parts, embeddings, left, right, taps)
-    part, found = lax.optimization_barrier((part, found))
-    part = jnp.sum(part, axis=0).reshape(-1)
-    local_taps = found[:ntaps].reshape(-1)
-    head = found[8 : 8 + reach].reshape(1, -1).astype(BF16)
-    tail = found[8 + reach : 8 + 2 * reach].reshape(1, -1).astype(BF16)
-
-    high = lax.reduce_precision(local_taps, 8, 7)
-    low = local_taps - high
-    row = jnp.arange(nseq)[:, None]
-    zero = jnp.zeros((), BF16)
-    edge = jnp.where(row == me + 1, tail, jnp.where(row == me - 1, head, zero))
-    both = jnp.concatenate([high, low]).astype(BF16)
-    both = jnp.broadcast_to(both[None], (nseq, both.size))
-    same = jnp.broadcast_to(part.astype(BF16)[None], (nseq, part.size))
-    message = jnp.stack([same, jnp.concatenate([both, edge], axis=1)], axis=1)
+
+    message = last_message(me.reshape(1), part, found, nseq)
     slab = lax.all_to_all(message, SEQ, 0, 0, tiled=True)
-    weight_grad = from_rows(slab[:, 0], tracks, features).astype(F32)
     embed_grad, ends = spread(conv_grad, taps)
-    embed_grad, taps_grad = finish(
-        me.reshape(1), slab[:, 1].astype(F32), ends, taps, embed_grad
+    embed_grad, weight_grad, taps_grad = finish(
+        me.reshape(1), slab, ends, taps, embed_grad, (tracks, features)
     )
     return embed_grad, weight_grad, taps_grad
 

time: 149 us -> 148 us (level)
  local copies, waits for them, and re-layouts: 5.79 us -> 4.09 us
where the time goes in v7:
time: 148 us; the launch traced here: 147 us
  blocking collectives  47.1 us (32%)
  starting transfers between devices  42.2 us (29%)
  waiting for transfers between devices  34.5 us (23%)
  Pallas kernels  17.9 us (12%)
  local copies, waits for them, and re-layouts  4.09 us (3%)
    all_to_all x1, blocking collectives, shards(): lax.all_to_all(jnp.broadcast_to(block[None], (ny, width, count)), 'y', 0,...  23.7 us
    all_to_all x1, blocking collectives, share(): return lax.all_to_all(copies, axes, 0, 0, tiled=True)[:, 0]  23.4 us
    all_to_all x1, waiting for transfers between devices, shards(): slab = lax.all_to_all(message, SEQ, 0, 0, tiled=True)  19.4 us
    ppermute x1, starting transfers between devices, outer_columns(): lax.ppermute(cells[:, :width], SEQ, [(i + 1, i) for i in range(count - 1)])  11.7 us
    ppermute x3, starting transfers between devices, along_y(): lax.ppermute(value, 'y', [(i, (i + shift) % count) for i in range(count)])  9.76 us
    ppermute x3, waiting for transfers between devices, along_y(): lax.ppermute(value, 'y', [(i, (i + shift) % count) for i in range(count)])  8.89 us
    pallas_call x5, Pallas kernels, kernel_call(): pl.pallas_call(body, out_shape=outs, in_specs=[pl.BlockSpec(memory_space=...  7.87 us
    all_to_all x1, starting transfers between devices, shards(): slab = lax.all_to_all(message, SEQ, 0, 0, tiled=True)  6.68 us
  transfers between devices with their start and end apart: 10, of which 7 were waited for; matrix products, arithmetic and copies ran while one was open for 0% of the time, Pallas kernels for 7%

profile of v7, /device:TPU:6, one launch (start us, length us, event | category | flops | bytes accessed | tf_op | source)
XLA Modules:
  0.0 146.8 jit_solution(9419754893271772950)
XLA Ops:
  1.5 11.7 %collective-permute-start.1 = (bf16[96,2]{1,0:T(8,128)(2,1)S(1)}, bf16[96,2]{1,0:T(8,128)(2,1)S(1)}, u32[]{:S(2)}, u32[]{:S(2)}) collective-permute-start(bf16[96,2]{1,0:T(8,128)(2,1)S(1)} %get-tuple-element.42), channel_id=1, source_target_pairs={{8,0},{16,8},{24,16},{32,24},{40,32},{48,40},{56,48},{64,56},{72,6... | collective-permute-start | bytes 1160 | tf_op jit(solution)/shard_map/ppermute | solution.py:30
  13.1 1.9 %collective-permute-start = (bf16[96,2]{1,0:T(8,128)(2,1)S(1)}, bf16[96,2]{1,0:T(8,128)(2,1)S(1)}, u32[]{:S(2)}, u32[]{:S(2)}) collective-permute-start(bf16[96,2]{1,0:T(8,128)(2,1)S(1)} %get-tuple-element.43), channel_id=1, source_target_pairs={{0,8},{8,16},{16,24},{24,32},{32,40},{40,48},{48,56},{56,64},{64,7... | collective-permute-start | bytes 1160 | tf_op jit(solution)/shard_map/ppermute | solution.py:29
  16.7 1.3 conv_silu.1.given
  18.0 2.9 %collective-permute-done.left = bf16[96,2]{1,0:T(8,128)(2,1)S(1)} collective-permute-done((bf16[96,2]{1,0:T(8,128)(2,1)S(1)}, bf16[96,2]{1,0:T(8,128)(2,1)S(1)}, u32[]{:S(2)}, u32[]{:S(2)}) %collective-permute-start) | collective-permute-done | bytes 416 | tf_op jit(solution)/shard_map/ppermute | solution.py:29
  21.7 23.7 %all_to_all.25 = bf16[4,96,2048]{2,1,0:T(8,128)(2,1)S(1)} all-to-all(bf16[4,96,2048]{2,1,0:T(8,128)(2,1)S(1)} %broadcast_in_dim.26), channel_id=1, replica_groups=mesh['x'=4,'z'=16,'y'=4,'c'=2] {'y'}, dimensions={0} | all-to-all | bytes 3145728 | tf_op jit(solution)/shard_map/all_to_all | solution.py:595
  45.4 1.9 %collective-permute-start.2 = (bf16[384,2048]{1,0:T(8,128)(2,1)S(1)}, bf16[384,2048]{1,0:T(8,128)(2,1)S(1)}, u32[]{:S(2)}, u32[]{:S(2)}) collective-permute-start(bf16[384,2048]{1,0:T(8,128)(2,1)S(1)} %bitcast.31), channel_id=1, source_target_pairs={{0,1},{1,0},{2,3},{3,2},{4,5},{5,4},{6,7},{7,6},{8,9},{9,8},{10,11... | collective-permute-start | bytes 4718600 | tf_op jit(solution)/shard_map/ppermute | solution.py:24
  50.7 1.3 far_logits.1
  52.1 23.4 %all_to_all.26 = f32[64,1,384]{2,1,0:T(1,128)S(1)} all-to-all(f32[64,1,384]{2,1,0:T(1,128)S(1)} %broadcast_in_dim.28), channel_id=1, replica_groups=mesh['x'=4,'z'=16,'y'=4,'c'=2] {'x','z'}, dimensions={0} | all-to-all | bytes 196608 | tf_op jit(solution)/shard_map/all_to_all | solution.py:37
  76.8 1.9 %collective-permute-start.3 = (bf16[384,2048]{1,0:T(8,128)(2,1)S(1)}, bf16[384,2048]{1,0:T(8,128)(2,1)S(1)}, u32[]{:S(2)}, u32[]{:S(2)}) collective-permute-start(bf16[384,2048]{1,0:T(8,128)(2,1)S(1)} %get-tuple-element.27), channel_id=1, source_target_pairs={{0,1},{1,0},{2,3},{3,2},{4,5},{5,4},{6,7},{7,6},{8,9},{9,8},{10,11... | collective-permute-start | bytes 4718600 | tf_op jit(solution)/shard_map/ppermute | solution.py:24
  78.7 2.4 %weight_part.1 = f32[96,768]{1,0:T(8,128)} custom-call(s32[2]{0:T(128)S(1)} %pad_add_fusion.place, bf16[96,2048]{1,0:T(8,128)(2,1)S(1)} %get-tuple-element.26.grad, bf16[384,2048]{1,0:T(8,128)(2,1)S(1)} %bitcast.33, bf16[384,2048]{1,0:T(8,128)(2,1)S(1)} %collective-permute-done.2.hidden.theirs), custom_call_target="tpu_custom_call" | custom-call | flops 301989888 | bytes 3833856 | tf_op jit(solution)/shard_map/weight_part/pallas_call | solution.py:175
  82.1 1.9 %core_sum.1 = (f32[96,2048]{1,0:T(8,128)S(1)}, bf16[96,2048]{1,0:T(8,128)(2,1)}, bf16[96,2048]{1,0:T(8,128)(2,1)}, bf16[96,2048]{1,0:T(8,128)(2,1)S(1)}) custom-call(s32[2]{0:T(128)S(1)} %pad_add_fusion.place, bf16[768,96]{1,0:T(8,128)(2,1)S(1)} %bitcast.37, bf16[96,2048]{1,0:T(8,128)(2,1)S(1)} %get-tuple-element.26.grad, ...), custom_call_target="tpu_custom_call" | custom-call | flops 150994944 | bytes 4079616 | tf_op jit(solution)/shard_map/core_sum/pallas_call | solution.py:175
  84.0 4.9 %all-to-all-start.2 = ((f32[4,24,768]{2,1,0:T(8,128)}), f32[4,24,768]{2,1,0:T(8,128)S(1)}, u32[]{:S(2)}, u32[]{:S(2)}) async-start(f32[4,24,768]{2,1,0:T(8,128)} %bitcast.10), calls=%async_computation.2 | async-start | bytes 589824 | tf_op jit(solution)/shard_map/all_to_all | solution.py:620
  88.9 2.7 %collective-permute-start.4 = (bf16[96,2048]{1,0:T(8,128)(2,1)}, bf16[96,2048]{1,0:T(8,128)(2,1)S(1)}, u32[]{:S(2)}, u32[]{:S(2)}) collective-permute-start(bf16[96,2048]{1,0:T(8,128)(2,1)} %get-tuple-element.33), channel_id=1, source_target_pairs={{0,4},{2,6},{4,0},{6,2},{1,5},{3,7},{5,1},{7,3},{8,12},{10,14},{12... | collective-permute-start | bytes 1179656 | tf_op jit(solution)/shard_map/ppermute | solution.py:20
  91.7 3.1 %collective-permute-start.5 = (bf16[96,2048]{1,0:T(8,128)(2,1)}, bf16[96,2048]{1,0:T(8,128)(2,1)S(1)}, u32[]{:S(2)}, u32[]{:S(2)}) collective-permute-start(bf16[96,2048]{1,0:T(8,128)(2,1)} %get-tuple-element.34), channel_id=1, source_target_pairs={{0,2},{2,4},{4,6},{6,0},{1,3},{3,5},{5,7},{7,1},{8,10},{10,12},{12... | collective-permute-start | bytes 1179656 | tf_op jit(solution)/shard_map/ppermute | solution.py:20
  94.8 3.9 %collective-permute-start.6 = (bf16[96,2048]{1,0:T(8,128)(2,1)S(1)}, bf16[96,2048]{1,0:T(8,128)(2,1)S(1)}, u32[]{:S(2)}, u32[]{:S(2)}) collective-permute-start(bf16[96,2048]{1,0:T(8,128)(2,1)S(1)} %get-tuple-element.35), channel_id=1, source_target_pairs={{0,6},{2,0},{4,2},{6,4},{1,7},{3,1},{5,3},{7,5},{8,14},{10,8},{12,... | collective-permute-start | bytes 1179656 | tf_op jit(solution)/shard_map/ppermute | solution.py:20
  99.4 3.5 %all-to-all-start.3 = ((f32[16,1,1152]{2,1,0:T(1,128)}), f32[16,1,1152]{2,1,0:T(1,128)S(1)}, u32[]{:S(2)}, u32[]{:S(2)}) async-start(f32[16,1,1152]{2,1,0:T(1,128)} %sum_to_rows.1), calls=%async_computation.3 | async-start | bytes 147456 | tf_op jit(solution)/shard_map/all_to_all | solution.py:622
  102.9 1.6 %collective-permute-done.4.one = bf16[96,2048]{1,0:T(8,128)(2,1)S(1)} collective-permute-done((bf16[96,2048]{1,0:T(8,128)(2,1)}, bf16[96,2048]{1,0:T(8,128)(2,1)S(1)}, u32[]{:S(2)}, u32[]{:S(2)}) %collective-permute-start.4) | collective-permute-done | bytes 393248 | tf_op jit(solution)/shard_map/ppermute | solution.py:20
  104.6 7.3 %collective-permute-done.5.two = bf16[96,2048]{1,0:T(8,128)(2,1)S(1)} collective-permute-done((bf16[96,2048]{1,0:T(8,128)(2,1)}, bf16[96,2048]{1,0:T(8,128)(2,1)S(1)}, u32[]{:S(2)}, u32[]{:S(2)}) %collective-permute-start.5) | collective-permute-done | bytes 393248 | tf_op jit(solution)/shard_map/ppermute | solution.py:20
  111.8 2.5 %conv_grad.1 = (bf16[96,2048]{1,0:T(8,128)(2,1)S(1)}, f32[16,96]{1,0:T(8,128)S(1)}) custom-call(f32[96,2048]{1,0:T(8,128)S(1)} %get-tuple-element.32.mine, bf16[96,2048]{1,0:T(8,128)(2,1)S(1)} %collective-permute-done.4.one, bf16[96,2048]{1,0:T(8,128)(2,1)S(1)} %collective-permute-done.5.two, bf16[96,2048]{1,0:T(8,128)(2,1)S(1)} %collective-permute-done.6.three, ...), custom_call_target="tpu_custom_call" | custom-call | flops 7864320 | bytes 2752512 | tf_op jit(solution)/shard_map/conv_grad/pallas_call | solution.py:360
  114.4 1.3 all-to-all-done.3.slices
  117.0 6.7 %all-to-all-start.4 = ((bf16[64,2,1152]{2,1,0:T(2,128)(2,1)}), bf16[64,2,1152]{2,1,0:T(2,128)(2,1)S(1)}, u32[]{:S(2)}, u32[]{:S(2)}) async-start(bf16[64,2,1152]{2,1,0:T(2,128)(2,1)} %message.1), calls=%async_computation.4 | async-start | bytes 589824 | tf_op jit(solution)/shard_map/all_to_all | solution.py:626
  123.7 1.9 %embed_grad.1 = (bf16[96,2048]{1,0:T(8,128)(2,1)}, f32[96,256]{1,0:T(8,128)S(1)}) custom-call(bf16[96,2048]{1,0:T(8,128)(2,1)S(1)} %get-tuple-element.37.grad, bf16[5,96]{1,0:T(8,128)(2,1)S(1)} %copy-done.5), custom_call_target="tpu_custom_call" | custom-call | flops 1966080 | bytes 786432 | tf_op jit(solution)/shard_map/embed_grad/pallas_call | solution.py:411
  125.6 19.4 %all-to-all-done.4.slab = bf16[64,2,1152]{2,1,0:T(2,128)(2,1)S(1)} async-done(((bf16[64,2,1152]{2,1,0:T(2,128)(2,1)}), bf16[64,2,1152]{2,1,0:T(2,128)(2,1)S(1)}, u32[]{:S(2)}, u32[]{:S(2)}) %all-to-all-start.4) | async-done | bytes 294944 | tf_op jit(solution)/shard_map/all_to_all | solution.py:626
  144.9 1.9 %finish.1 = (bf16[96,2048]{1,0:T(8,128)(2,1)}, f32[96,768]{1,0:T(8,128)}, f32[5,96]{1,0:T(8,128)}) custom-call(s32[1]{0:T(128)} %bitcast.place, bf16[64,2,1152]{2,1,0:T(2,128)(2,1)S(1)} %all-to-all-done.4.slab, f32[96,256]{1,0:T(8,128)S(1)} %get-tuple-element.38.ends, bf16[5,96]{1,0:T(8,128)(2,1)S(1)} %copy-done.5, ...), custom_call_target="tpu_custom_call", output_to_operand_aliasing={{0}: (4, {})} | custom-call | flops 147456 | bytes 1179648 | tf_op jit(solution)/shard_map/finish/pallas_call | solution.py:546
  (35 shorter events, 10.9 us)
Async XLA Ops:
  1.5 16.6 %collective-permute-start.1 = (bf16[96,2]{1,0:T(8,128)(2,1)S(1)}, bf16[96,2]{1,0:T(8,128)(2,1)S(1)}, u32[]{:S(2)}, u32[]{:S(2)}) collective-permute-start(bf16[96,2]{1,0:T(8,128)(2,1)S(1)} %get-tuple-element.42), channel_id=1, source_target_pairs={{8,0},{16,8},{24,16},{32,24},{40,32},{48,40},{56,48},{64,56},{72,6... | collective-permute-start | bytes 1160 | tf_op jit(solution)/shard_map/ppermute | solution.py:30
  13.1 7.8 %collective-permute-start = (bf16[96,2]{1,0:T(8,128)(2,1)S(1)}, bf16[96,2]{1,0:T(8,128)(2,1)S(1)}, u32[]{:S(2)}, u32[]{:S(2)}) collective-permute-start(bf16[96,2]{1,0:T(8,128)(2,1)S(1)} %get-tuple-element.43), channel_id=1, source_target_pairs={{0,8},{8,16},{16,24},{24,32},{32,40},{40,48},{48,56},{56,64},{64,7... | collective-permute-start | bytes 1160 | tf_op jit(solution)/shard_map/ppermute | solution.py:29
  15.1 1.0 copy-start
  16.1 0.7 copy-start.4
  21.7 25.6 %copy-start.6 = (bf16[96,768]{1,0:T(8,128)(2,1)S(1)}, bf16[96,768]{1,0:T(8,128)(2,1)}, u32[]{:S(2)}) copy-start(bf16[96,768]{1,0:T(8,128)(2,1)} %param.6) | copy-start | bytes 442372
  45.4 5.3 %collective-permute-start.2 = (bf16[384,2048]{1,0:T(8,128)(2,1)S(1)}, bf16[384,2048]{1,0:T(8,128)(2,1)S(1)}, u32[]{:S(2)}, u32[]{:S(2)}) collective-permute-start(bf16[384,2048]{1,0:T(8,128)(2,1)S(1)} %bitcast.31), channel_id=1, source_target_pairs={{0,1},{1,0},{2,3},{3,2},{4,5},{5,4},{6,7},{7,6},{8,9},{9,8},{10,11... | collective-permute-start | bytes 4718600 | tf_op jit(solution)/shard_map/ppermute | solution.py:24
  47.6 1.1 copy-start.2
  50.7 24.9 %copy-start.3 = (f32[96,2048]{1,0:T(8,128)S(1)}, f32[96,2048]{1,0:T(8,128)}, u32[]{:S(2)}) copy-start(f32[96,2048]{1,0:T(8,128)} %targets.3) | copy-start | bytes 2359300
  76.8 5.3 %collective-permute-start.3 = (bf16[384,2048]{1,0:T(8,128)(2,1)S(1)}, bf16[384,2048]{1,0:T(8,128)(2,1)S(1)}, u32[]{:S(2)}, u32[]{:S(2)}) collective-permute-start(bf16[384,2048]{1,0:T(8,128)(2,1)S(1)} %get-tuple-element.27), channel_id=1, source_target_pairs={{0,1},{1,0},{2,3},{3,2},{4,5},{5,4},{6,7},{7,6},{8,9},{9,8},{10,11... | collective-permute-start | bytes 4718600 | tf_op jit(solution)/shard_map/ppermute | solution.py:24
  81.1 30.7 %copy-start.1 = (bf16[96,2048]{1,0:T(8,128)(2,1)S(1)}, bf16[96,2048]{1,0:T(8,128)(2,1)}, u32[]{:S(2)}) copy-start(bf16[96,2048]{1,0:T(8,128)(2,1)} %cells.5) | copy-start | bytes 1179652
  81.1 30.7 %copy-start.5 = (bf16[5,96]{1,0:T(8,128)(2,1)S(1)}, bf16[5,96]{1,0:T(8,128)(2,1)}, u32[]{:S(2)}) copy-start(bf16[5,96]{1,0:T(8,128)(2,1)} %tap.9) | copy-start | bytes 2884
  84.0 14.7 %all-to-all-start.2 = ((f32[4,24,768]{2,1,0:T(8,128)}), f32[4,24,768]{2,1,0:T(8,128)S(1)}, u32[]{:S(2)}, u32[]{:S(2)}) async-start(f32[4,24,768]{2,1,0:T(8,128)} %bitcast.10), calls=%async_computation.2 | async-start | bytes 589824 | tf_op jit(solution)/shard_map/all_to_all | solution.py:620
  88.9 15.6 %collective-permute-start.4 = (bf16[96,2048]{1,0:T(8,128)(2,1)}, bf16[96,2048]{1,0:T(8,128)(2,1)S(1)}, u32[]{:S(2)}, u32[]{:S(2)}) collective-permute-start(bf16[96,2048]{1,0:T(8,128)(2,1)} %get-tuple-element.33), channel_id=1, source_target_pairs={{0,4},{2,6},{4,0},{6,2},{1,5},{3,7},{5,1},{7,3},{8,12},{10,14},{12... | collective-permute-start | bytes 1179656 | tf_op jit(solution)/shard_map/ppermute | solution.py:20
  91.7 20.2 %collective-permute-start.5 = (bf16[96,2048]{1,0:T(8,128)(2,1)}, bf16[96,2048]{1,0:T(8,128)(2,1)S(1)}, u32[]{:S(2)}, u32[]{:S(2)}) collective-permute-start(bf16[96,2048]{1,0:T(8,128)(2,1)} %get-tuple-element.34), channel_id=1, source_target_pairs={{0,2},{2,4},{4,6},{6,0},{1,3},{3,5},{5,7},{7,1},{8,10},{10,12},{12... | collective-permute-start | bytes 1179656 | tf_op jit(solution)/shard_map/ppermute | solution.py:20
  94.8 17.1 %collective-permute-start.6 = (bf16[96,2048]{1,0:T(8,128)(2,1)S(1)}, bf16[96,2048]{1,0:T(8,128)(2,1)S(1)}, u32[]{:S(2)}, u32[]{:S(2)}) collective-permute-start(bf16[96,2048]{1,0:T(8,128)(2,1)S(1)} %get-tuple-element.35), channel_id=1, source_target_pairs={{0,6},{2,0},{4,2},{6,4},{1,7},{3,1},{5,3},{7,5},{8,14},{10,8},{12,... | collective-permute-start | bytes 1179656 | tf_op jit(solution)/shard_map/ppermute | solution.py:20
  99.4 16.3 %all-to-all-start.3 = ((f32[16,1,1152]{2,1,0:T(1,128)}), f32[16,1,1152]{2,1,0:T(1,128)S(1)}, u32[]{:S(2)}, u32[]{:S(2)}) async-start(f32[16,1,1152]{2,1,0:T(1,128)} %sum_to_rows.1), calls=%async_computation.3 | async-start | bytes 147456 | tf_op jit(solution)/shard_map/all_to_all | solution.py:622
  117.0 28.0 %all-to-all-start.4 = ((bf16[64,2,1152]{2,1,0:T(2,128)(2,1)}), bf16[64,2,1152]{2,1,0:T(2,128)(2,1)S(1)}, u32[]{:S(2)}, u32[]{:S(2)}) async-start(bf16[64,2,1152]{2,1,0:T(2,128)(2,1)} %message.1), calls=%async_computation.4 | async-start | bytes 589824 | tf_op jit(solution)/shard_map/all_to_all | solution.py:626

commit v8 on v7

--- a/solution.py
+++ b/solution.py
@@ -427,29 +427,35 @@
     )(grad, tap)
 
 
+def in_line(pieces, width, size, first=0):
+    total = jnp.zeros((1, size), F32)
+    for n, piece in enumerate(pieces):
+        total = total + (pltpu.roll(piece, (first + n) * width, 1) if first + n else piece)
+    return total
+
+
+def high_and_low(line, ntaps, width):
+    taps = lax.broadcasted_iota(jnp.int32, line.shape, 1) < ntaps * width
+    line = jnp.where(taps, line, 0.0)
+    high = line.astype(BF16).astype(F32)
+    return high + pltpu.roll(line - high, ntaps * width, 1)
+
+
 def message_kernel(place, slices, found, out, rows, mixed):
-    me = place[0]
+    z = place[0]
     devices, _, size = out.shape
     width = found.shape[1]
     ntaps, reach = place_taps(size, width)
     rows[...] = jnp.zeros(rows.shape, F32)
     rows[:, :width] = found[...]
-    taps = rows[0:8, :]
-    high = taps.astype(BF16).astype(F32)
-    low = taps - high
-    parts = [high[k : k + 1] for k in range(ntaps)] + [low[k : k + 1] for k in range(ntaps)]
     sides = [rows[8 + k : 9 + k, :] for k in range(2 * reach)]
-
-    def line(pieces, first):
-        total = jnp.zeros((1, size), F32)
-        for n, piece in enumerate(pieces):
-            total = total + (pltpu.roll(piece, (first + n) * width, 1) if first + n else piece)
-        return total
-
     row = lax.broadcasted_iota(jnp.int32, (devices, size), 0)
-    value = jnp.broadcast_to(line(parts, 0), (devices, size))
-    value = jnp.where(row == me - 1, value + line(sides[:reach], 2 * ntaps), value)
-    value = jnp.where(row == me + 1, value + line(sides[reach:], 2 * ntaps), value)
+    taps = in_line([rows[k : k + 1, :] for k in range(ntaps)], width, size)
+    value = jnp.broadcast_to(high_and_low(taps, ntaps, width), (devices, size))
+    head = in_line(sides[:reach], width, size, 2 * ntaps)
+    tail = in_line(sides[reach:], width, size, 2 * ntaps)
+    value = jnp.where(row == lax.rem(z + devices - 1, devices), value + head, value)
+    value = jnp.where(row == lax.rem(z + 1, devices), value + tail, value)
     part = jnp.sum(slices[:, 0, :], axis=0, keepdims=True)
     mixed[:, 0, :] = jnp.broadcast_to(part, (devices, size))
     mixed[:, 1, :] = value
@@ -480,23 +486,73 @@
     )(place, slices, found)
 
 
+def tap_line(total, ntaps, width):
+    return total + pltpu.roll(total, total.shape[1] - ntaps * width, 1)
+
+
+def onward_kernel(width, place, slab, out, plain, last):
+    z, nz, x = place[0], place[1], place[2]
+    devices, _, size = out.shape
+    ntaps, _ = place_taps(size, width)
+    count = slab.shape[0]
+    plain[...] = slab[...].astype(F32)
+    total = jnp.sum(plain[:, 1, :], axis=0, keepdims=True)
+    value = high_and_low(tap_line(total, ntaps, width), ntaps, width)
+    halo = lax.broadcasted_iota(jnp.int32, (1, size), 1) >= 2 * ntaps * width
+    up = jnp.where(halo & (z == 0), plain[count - 1, 1:2, :], 0.0)
+    down = jnp.where(halo & (z == nz - 1), plain[0, 1:2, :], 0.0)
+    slices = plain[:, 0, :].astype(BF16)
+    last[...] = jnp.zeros(last.shape, F32)
+    for other in range(devices):
+        out[other, :count, :] = slices
+        passed = jnp.where(x + 1 == other, up, 0.0) + jnp.where(x - 1 == other, down, 0.0)
+        last[0:1, :] = value + passed
+        out[other, count:, :] = last[...].astype(BF16)
+
+
+def onward(place, slab, devices, width):
+    count, _, size = slab.shape
+    return pl.pallas_call(
+        functools.partial(onward_kernel, width),
+        out_shape=jax.ShapeDtypeStruct((devices, count + 16, size), BF16),
+        in_specs=[
+            pl.BlockSpec(memory_space=pltpu.SMEM),
+            pl.BlockSpec(memory_space=pltpu.VMEM),
+        ],
+        scratch_shapes=[
+            pltpu.VMEM(slab.shape, F32),
+            pltpu.VMEM((16, size), F32),
+        ],
+        compiler_params=pltpu.CompilerParams(vmem_limit_bytes=6 * 2**20),
+        cost_estimate=pl.CostEstimate(
+            flops=2 * slab.size, bytes_accessed=12 * slab.size, transcendentals=0
+        ),
+        name="onward",
+    )(place, slab)
+
+
 def finish_kernel(
-    place, slab, ends, tap, given, embed, weight, sums,
+    place, slab, wide, ends, tap, given, embed, weight, sums,
     square, columns, edges, tiles, plain, sems,
 ):
     del given
     ntaps, width = tap.shape
     reach = ntaps // 2
-    devices, _, size = slab.shape
-    me = place[0]
+    nz, _, size = slab.shape
+    nx = wide.shape[0]
+    z, x = place[0], place[2]
     plain[...] = slab[...].astype(F32)
     columns[...] = tap_columns(tap, square)
 
     edges[...] = jnp.zeros(edges.shape, F32)
     start = 2 * ntaps * width
-    for side, other in enumerate((me - 1, me + 1)):
-        row = plain[jnp.clip(other, 0, devices - 1), 1:2, :]
-        row = jnp.where((other >= 0) & (other < devices), row, 0.0)
+    lasts = [wide[n, nz:, :].astype(F32)[0:1, :] for n in range(nx)]
+    for side, step in enumerate((-1, 1)):
+        inner = (z + step >= 0) & (z + step < nz)
+        row = jnp.zeros((1, size), F32)
+        for n in range(nx):
+            row = jnp.where(x + step == n, lasts[n], row)
+        row = jnp.where(inner, plain[jnp.clip(z + step, 0, nz - 1), 1:2, :], row)
         for k in range(reach):
             turned = pltpu.roll(row, size - start - k * width, 1)
             edges[side * reach + k : side * reach + k + 1, :] = turned[:, :LANES]
@@ -524,24 +580,26 @@
         )
         writes[n].start()
 
-    per_row, wide = size // LANES, weight.shape[1] // LANES
-    for tile in range(devices // 8 * per_row):
-        group, spot = tile // per_row, tile % per_row * LANES
-        row, col = tile // wide * 8, tile % wide * LANES
-        weight[row : row + 8, col : col + LANES] = plain[
-            group * 8 : group * 8 + 8, 0, spot : spot + LANES
-        ]
-
-    total = jnp.sum(plain[:, 1, :], axis=0, keepdims=True)
+    per_row, across = size // LANES, weight.shape[1] // LANES
+    for n in range(nx):
+        block = wide[n, :nz, :].astype(F32)
+        for tile in range(nz // 8 * per_row):
+            group, spot = tile // per_row, tile % per_row * LANES
+            number = n * (nz // 8 * per_row) + tile
+            row, col = number // across * 8, number % across * LANES
+            weight[row : row + 8, col : col + LANES] = block[
+                group * 8 : group * 8 + 8, spot : spot + LANES
+            ]
+
+    line = tap_line(sum(lasts), ntaps, width)
     for k in range(ntaps):
-        high = pltpu.roll(total, size - k * width, 1) if k else total
-        low = pltpu.roll(total, size - (ntaps + k) * width, 1)
-        sums[k : k + 1, :] = (high + low)[:, :width]
+        found = pltpu.roll(line, size - k * width, 1) if k else line
+        sums[k : k + 1, :] = found[:, :width]
     for write in writes:
         write.wait()
 
 
-def finish(place, slab, ends, tap, embed, weight_shape):
+def finish(place, slab, wide, ends, tap, embed, weight_shape):
     ntaps, width = tap.shape
     return pl.pallas_call(
         finish_kernel,
@@ -551,14 +609,14 @@
             jax.ShapeDtypeStruct((ntaps, width), F32),
         ),
         in_specs=[pl.BlockSpec(memory_space=pltpu.SMEM)]
-        + [pl.BlockSpec(memory_space=pltpu.VMEM)] * 3
+        + [pl.BlockSpec(memory_space=pltpu.VMEM)] * 4
         + [pl.BlockSpec(memory_space=pl.ANY)],
         out_specs=(
             pl.BlockSpec(memory_space=pl.ANY),
             pl.BlockSpec(memory_space=pltpu.VMEM),
             pl.BlockSpec(memory_space=pltpu.VMEM),
         ),
-        input_output_aliases={4: 0},
+        input_output_aliases={5: 0},
         scratch_shapes=[
             pltpu.VMEM((8, LANES), F32),
             pltpu.VMEM((LANES, 8), F32),
@@ -572,7 +630,7 @@
             flops=slab.size, bytes_accessed=8 * slab.size, transcendentals=0
         ),
         name="finish",
-    )(place, slab, ends, tap, embed)
+    )(place, slab, wide, ends, tap, embed)
 
 
 def shards(embeddings, taps, head_weight, targets):
@@ -584,8 +642,6 @@
     y = lax.axis_index("y")
     c = lax.axis_index("c")
     ny = lax.axis_size("y")
-    nseq = lax.axis_size(SEQ)
-    me = lax.axis_index(SEQ)
     features = ny * 2 * width
 
     place = jnp.stack([y, c])
@@ -622,11 +678,13 @@
     part = lax.all_to_all(part, "z", 0, 0, tiled=True)
     conv_grad, found = backward(own, parts, embeddings, left, right, taps)
 
-    message = last_message(me.reshape(1), part, found, nseq)
-    slab = lax.all_to_all(message, SEQ, 0, 0, tiled=True)
+    spot = jnp.stack([lax.axis_index("z"), nz, lax.axis_index("x")])
+    message = last_message(spot, part, found, nz)
+    slab = lax.all_to_all(message, "z", 0, 0, tiled=True)
+    wide = lax.all_to_all(onward(spot, slab, nx, width), "x", 0, 0, tiled=True)
     embed_grad, ends = spread(conv_grad, taps)
     embed_grad, weight_grad, taps_grad = finish(
-        me.reshape(1), slab, ends, taps, embed_grad, (tracks, features)
+        spot, slab, wide, ends, taps, embed_grad, (tracks, features)
     )
     return embed_grad, weight_grad, taps_grad
 

time: 148 us -> 147 us (level)
  waiting for transfers between devices: 34.5 us -> 17.9 us
  blocking collectives: 47.1 us -> 62.9 us
  starting transfers between devices: 42.2 us -> 40.4 us
  Pallas kernels: 17.9 us -> 19.5 us
    all_to_all x1, waiting for transfers between devices: 19.4 us -> 2.87 us  [shards(): wide = lax.all_to_all(onward(spot, slab, nx, width), 'x', 0, 0, tiled=True)]
    all_to_all x0 -> x1, blocking collectives: none -> 15.8 us  [shards(): slab = lax.all_to_all(message, 'z', 0, 0, tiled=True)]
    all_to_all x1, starting transfers between devices: 6.68 us -> 4.79 us  [shards(): wide = lax.all_to_all(onward(spot, slab, nx, width), 'x', 0, 0, tiled=True)]
    pallas_call x0 -> x1, Pallas kernels: none -> 1.55 us  [onward(): pl.pallas_call(functools.partial(onward_kernel, width), out_shape=jax.Sha...]
where the time goes in v8:
time: 147 us; the launch traced here: 146 us
  blocking collectives  62.9 us (43%)
  starting transfers between devices  40.4 us (27%)
  Pallas kernels  19.5 us (13%)
  waiting for transfers between devices  17.9 us (12%)
  local copies, waits for them, and re-layouts  4.09 us (3%)
    all_to_all x1, blocking collectives, shards(): lax.all_to_all(jnp.broadcast_to(block[None], (ny, width, count)), 'y', 0,...  23.7 us
    all_to_all x1, blocking collectives, share(): return lax.all_to_all(copies, axes, 0, 0, tiled=True)[:, 0]  23.4 us
    all_to_all x1, blocking collectives, shards(): slab = lax.all_to_all(message, 'z', 0, 0, tiled=True)  15.8 us
    ppermute x1, starting transfers between devices, outer_columns(): lax.ppermute(cells[:, :width], SEQ, [(i + 1, i) for i in range(count - 1)])  11.7 us
    ppermute x3, starting transfers between devices, along_y(): lax.ppermute(value, 'y', [(i, (i + shift) % count) for i in range(count)])  9.76 us
    ppermute x3, waiting for transfers between devices, along_y(): lax.ppermute(value, 'y', [(i, (i + shift) % count) for i in range(count)])  8.82 us
    pallas_call x5, Pallas kernels, kernel_call(): pl.pallas_call(body, out_shape=outs, in_specs=[pl.BlockSpec(memory_space=...  7.87 us
    all_to_all x1, starting transfers between devices, shards(): lax.all_to_all(local.reshape(nx, tracks // nx, features), 'x', 0, 0, tile...  4.89 us
  transfers between devices with their start and end apart: 10, of which 7 were waited for; matrix products, arithmetic and copies ran while one was open for 0% of the time, Pallas kernels for 7%

profile of v8, /device:TPU:6, one launch (start us, length us, event | category | flops | bytes accessed | tf_op | source)
XLA Modules:
  0.0 145.8 jit_solution(16993137531769772809)
XLA Ops:
  1.5 11.7 %collective-permute-start.1 = (bf16[96,2]{1,0:T(8,128)(2,1)S(1)}, bf16[96,2]{1,0:T(8,128)(2,1)S(1)}, u32[]{:S(2)}, u32[]{:S(2)}) collective-permute-start(bf16[96,2]{1,0:T(8,128)(2,1)S(1)} %get-tuple-element.42), channel_id=1, source_target_pairs={{8,0},{16,8},{24,16},{32,24},{40,32},{48,40},{56,48},{64,56},{72,6... | collective-permute-start | bytes 1160 | tf_op jit(solution)/shard_map/ppermute | solution.py:30
  13.1 1.9 %collective-permute-start = (bf16[96,2]{1,0:T(8,128)(2,1)S(1)}, bf16[96,2]{1,0:T(8,128)(2,1)S(1)}, u32[]{:S(2)}, u32[]{:S(2)}) collective-permute-start(bf16[96,2]{1,0:T(8,128)(2,1)S(1)} %get-tuple-element.43), channel_id=1, source_target_pairs={{0,8},{8,16},{16,24},{24,32},{32,40},{40,48},{48,56},{56,64},{64,7... | collective-permute-start | bytes 1160 | tf_op jit(solution)/shard_map/ppermute | solution.py:29
  18.0 2.9 %collective-permute-done.left = bf16[96,2]{1,0:T(8,128)(2,1)S(1)} collective-permute-done((bf16[96,2]{1,0:T(8,128)(2,1)S(1)}, bf16[96,2]{1,0:T(8,128)(2,1)S(1)}, u32[]{:S(2)}, u32[]{:S(2)}) %collective-permute-start) | collective-permute-done | bytes 416 | tf_op jit(solution)/shard_map/ppermute | solution.py:29
  21.7 23.7 %all_to_all.30 = bf16[4,96,2048]{2,1,0:T(8,128)(2,1)S(1)} all-to-all(bf16[4,96,2048]{2,1,0:T(8,128)(2,1)S(1)} %broadcast_in_dim.26), channel_id=1, replica_groups=mesh['x'=4,'z'=16,'y'=4,'c'=2] {'y'}, dimensions={0} | all-to-all | bytes 3145728 | tf_op jit(solution)/shard_map/all_to_all | solution.py:651
  45.4 1.9 %collective-permute-start.2 = (bf16[384,2048]{1,0:T(8,128)(2,1)S(1)}, bf16[384,2048]{1,0:T(8,128)(2,1)S(1)}, u32[]{:S(2)}, u32[]{:S(2)}) collective-permute-start(bf16[384,2048]{1,0:T(8,128)(2,1)S(1)} %bitcast.32), channel_id=1, source_target_pairs={{0,1},{1,0},{2,3},{3,2},{4,5},{5,4},{6,7},{7,6},{8,9},{9,8},{10,11... | collective-permute-start | bytes 4718600 | tf_op jit(solution)/shard_map/ppermute | solution.py:24
  52.1 23.4 %all_to_all.31 = f32[64,1,384]{2,1,0:T(1,128)S(1)} all-to-all(f32[64,1,384]{2,1,0:T(1,128)S(1)} %broadcast_in_dim.28), channel_id=1, replica_groups=mesh['x'=4,'z'=16,'y'=4,'c'=2] {'x','z'}, dimensions={0} | all-to-all | bytes 196608 | tf_op jit(solution)/shard_map/all_to_all | solution.py:37
  76.8 1.9 %collective-permute-start.3 = (bf16[384,2048]{1,0:T(8,128)(2,1)S(1)}, bf16[384,2048]{1,0:T(8,128)(2,1)S(1)}, u32[]{:S(2)}, u32[]{:S(2)}) collective-permute-start(bf16[384,2048]{1,0:T(8,128)(2,1)S(1)} %get-tuple-element.27), channel_id=1, source_target_pairs={{0,1},{1,0},{2,3},{3,2},{4,5},{5,4},{6,7},{7,6},{8,9},{9,8},{10,11... | collective-permute-start | bytes 4718600 | tf_op jit(solution)/shard_map/ppermute | solution.py:24
  78.7 2.4 %weight_part.1 = f32[96,768]{1,0:T(8,128)} custom-call(s32[2]{0:T(128)S(1)} %pad_add_fusion.1.place, bf16[96,2048]{1,0:T(8,128)(2,1)S(1)} %get-tuple-element.26.grad, bf16[384,2048]{1,0:T(8,128)(2,1)S(1)} %bitcast.34, bf16[384,2048]{1,0:T(8,128)(2,1)S(1)} %collective-permute-done.2.hidden.theirs), custom_call_target="tpu_custom_call" | custom-call | flops 301989888 | bytes 3833856 | tf_op jit(solution)/shard_map/weight_part/pallas_call | solution.py:175
  82.1 1.9 %core_sum.1 = (f32[96,2048]{1,0:T(8,128)S(1)}, bf16[96,2048]{1,0:T(8,128)(2,1)}, bf16[96,2048]{1,0:T(8,128)(2,1)}, bf16[96,2048]{1,0:T(8,128)(2,1)S(1)}) custom-call(s32[2]{0:T(128)S(1)} %pad_add_fusion.1.place, bf16[768,96]{1,0:T(8,128)(2,1)S(1)} %bitcast.38, bf16[96,2048]{1,0:T(8,128)(2,1)S(1)} %get-tuple-element.26.grad, ...), custom_call_target="tpu_custom_call" | custom-call | flops 150994944 | bytes 4079616 | tf_op jit(solution)/shard_map/core_sum/pallas_call | solution.py:175
  84.0 4.9 %all-to-all-start.2 = ((f32[4,24,768]{2,1,0:T(8,128)}), f32[4,24,768]{2,1,0:T(8,128)S(1)}, u32[]{:S(2)}, u32[]{:S(2)}) async-start(f32[4,24,768]{2,1,0:T(8,128)} %bitcast.11), calls=%async_computation.2 | async-start | bytes 589824 | tf_op jit(solution)/shard_map/all_to_all | solution.py:676
  88.9 2.7 %collective-permute-start.4 = (bf16[96,2048]{1,0:T(8,128)(2,1)}, bf16[96,2048]{1,0:T(8,128)(2,1)S(1)}, u32[]{:S(2)}, u32[]{:S(2)}) collective-permute-start(bf16[96,2048]{1,0:T(8,128)(2,1)} %get-tuple-element.33), channel_id=1, source_target_pairs={{0,4},{2,6},{4,0},{6,2},{1,5},{3,7},{5,1},{7,3},{8,12},{10,14},{12... | collective-permute-start | bytes 1179656 | tf_op jit(solution)/shard_map/ppermute | solution.py:20
  91.7 3.1 %collective-permute-start.5 = (bf16[96,2048]{1,0:T(8,128)(2,1)}, bf16[96,2048]{1,0:T(8,128)(2,1)S(1)}, u32[]{:S(2)}, u32[]{:S(2)}) collective-permute-start(bf16[96,2048]{1,0:T(8,128)(2,1)} %get-tuple-element.34), channel_id=1, source_target_pairs={{0,2},{2,4},{4,6},{6,0},{1,3},{3,5},{5,7},{7,1},{8,10},{10,12},{12... | collective-permute-start | bytes 1179656 | tf_op jit(solution)/shard_map/ppermute | solution.py:20
  94.8 3.9 %collective-permute-start.6 = (bf16[96,2048]{1,0:T(8,128)(2,1)S(1)}, bf16[96,2048]{1,0:T(8,128)(2,1)S(1)}, u32[]{:S(2)}, u32[]{:S(2)}) collective-permute-start(bf16[96,2048]{1,0:T(8,128)(2,1)S(1)} %get-tuple-element.35), channel_id=1, source_target_pairs={{0,6},{2,0},{4,2},{6,4},{1,7},{3,1},{5,3},{7,5},{8,14},{10,8},{12,... | collective-permute-start | bytes 1179656 | tf_op jit(solution)/shard_map/ppermute | solution.py:20
  99.4 3.5 %all-to-all-start.3 = ((f32[16,1,1152]{2,1,0:T(1,128)}), f32[16,1,1152]{2,1,0:T(1,128)S(1)}, u32[]{:S(2)}, u32[]{:S(2)}) async-start(f32[16,1,1152]{2,1,0:T(1,128)} %sum_to_rows.1), calls=%async_computation.3 | async-start | bytes 147456 | tf_op jit(solution)/shard_map/all_to_all | solution.py:678
  103.0 1.6 %collective-permute-done.4.one = bf16[96,2048]{1,0:T(8,128)(2,1)S(1)} collective-permute-done((bf16[96,2048]{1,0:T(8,128)(2,1)}, bf16[96,2048]{1,0:T(8,128)(2,1)S(1)}, u32[]{:S(2)}, u32[]{:S(2)}) %collective-permute-start.4) | collective-permute-done | bytes 393248 | tf_op jit(solution)/shard_map/ppermute | solution.py:20
  104.6 7.3 %collective-permute-done.5.two = bf16[96,2048]{1,0:T(8,128)(2,1)S(1)} collective-permute-done((bf16[96,2048]{1,0:T(8,128)(2,1)}, bf16[96,2048]{1,0:T(8,128)(2,1)S(1)}, u32[]{:S(2)}, u32[]{:S(2)}) %collective-permute-start.5) | collective-permute-done | bytes 393248 | tf_op jit(solution)/shard_map/ppermute | solution.py:20
  111.8 2.5 %conv_grad.1 = (bf16[96,2048]{1,0:T(8,128)(2,1)S(1)}, f32[16,96]{1,0:T(8,128)S(1)}) custom-call(f32[96,2048]{1,0:T(8,128)S(1)} %get-tuple-element.32.mine, bf16[96,2048]{1,0:T(8,128)(2,1)S(1)} %collective-permute-done.4.one, bf16[96,2048]{1,0:T(8,128)(2,1)S(1)} %collective-permute-done.5.two, bf16[96,2048]{1,0:T(8,128)(2,1)S(1)} %collective-permute-done.6.three, ...), custom_call_target="tpu_custom_call" | custom-call | flops 7864320 | bytes 2752512 | tf_op jit(solution)/shard_map/conv_grad/pallas_call | solution.py:360
  114.4 1.3 all-to-all-done.3.slices
  116.5 15.8 %all_to_all.32.slab = bf16[16,2,1152]{2,1,0:T(2,128)(2,1)S(1)} all-to-all(bf16[16,2,1152]{2,1,0:T(2,128)(2,1)S(1)} %message.1), channel_id=1, replica_groups=mesh['x'=4,'z'=16,'y'=4,'c'=2] {'z'}, dimensions={0} | all-to-all | bytes 147456 | tf_op jit(solution)/shard_map/all_to_all | solution.py:683
  132.3 1.6 %onward.1 = bf16[4,32,1152]{2,1,0:T(8,128)(2,1)} custom-call(s32[3]{0:T(128)S(1)} %pad_add_fusion.place, bf16[16,2,1152]{2,1,0:T(2,128)(2,1)S(1)} %all_to_all.32.slab), custom_call_target="tpu_custom_call" | custom-call | flops 73728 | bytes 442368 | tf_op jit(solution)/shard_map/onward/pallas_call | solution.py:515
  133.9 4.8 %all-to-all-start.5 = ((bf16[4,32,1152]{2,1,0:T(8,128)(2,1)}), bf16[4,32,1152]{2,1,0:T(8,128)(2,1)S(1)}, u32[]{:S(2)}, u32[]{:S(2)}) async-start(bf16[4,32,1152]{2,1,0:T(8,128)(2,1)} %onward.1), calls=%async_computation.5 | async-start | bytes 589824 | tf_op jit(solution)/shard_map/all_to_all | solution.py:684
  138.7 1.9 %embed_grad.1 = (bf16[96,2048]{1,0:T(8,128)(2,1)}, f32[96,256]{1,0:T(8,128)S(1)}) custom-call(bf16[96,2048]{1,0:T(8,128)(2,1)S(1)} %get-tuple-element.37.grad, bf16[5,96]{1,0:T(8,128)(2,1)S(1)} %copy-done.5), custom_call_target="tpu_custom_call" | custom-call | flops 1966080 | bytes 786432 | tf_op jit(solution)/shard_map/embed_grad/pallas_call | solution.py:411
  140.6 2.9 %all-to-all-done.5.wide = bf16[4,32,1152]{2,1,0:T(8,128)(2,1)S(1)} async-done(((bf16[4,32,1152]{2,1,0:T(8,128)(2,1)}), bf16[4,32,1152]{2,1,0:T(8,128)(2,1)S(1)}, u32[]{:S(2)}, u32[]{:S(2)}) %all-to-all-start.5) | async-done | bytes 294944 | tf_op jit(solution)/shard_map/all_to_all | solution.py:684
  143.5 2.3 %finish.1 = (bf16[96,2048]{1,0:T(8,128)(2,1)}, f32[96,768]{1,0:T(8,128)}, f32[5,96]{1,0:T(8,128)}) custom-call(s32[3]{0:T(128)S(1)} %pad_add_fusion.place, bf16[16,2,1152]{2,1,0:T(2,128)(2,1)S(1)} %all_to_all.32.slab, bf16[4,32,1152]{2,1,0:T(8,128)(2,1)S(1)} %all-to-all-done.5.wide, ...), custom_call_target="tpu_custom_call", output_to_operand_aliasing={{0}: (5, {})} | custom-call | flops 36864 | bytes 294912 | tf_op jit(solution)/shard_map/finish/pallas_call | solution.py:604
  (38 shorter events, 13.1 us)
Async XLA Ops:
  1.5 16.6 %collective-permute-start.1 = (bf16[96,2]{1,0:T(8,128)(2,1)S(1)}, bf16[96,2]{1,0:T(8,128)(2,1)S(1)}, u32[]{:S(2)}, u32[]{:S(2)}) collective-permute-start(bf16[96,2]{1,0:T(8,128)(2,1)S(1)} %get-tuple-element.42), channel_id=1, source_target_pairs={{8,0},{16,8},{24,16},{32,24},{40,32},{48,40},{56,48},{64,56},{72,6... | collective-permute-start | bytes 1160 | tf_op jit(solution)/shard_map/ppermute | solution.py:30
  13.1 7.8 %collective-permute-start = (bf16[96,2]{1,0:T(8,128)(2,1)S(1)}, bf16[96,2]{1,0:T(8,128)(2,1)S(1)}, u32[]{:S(2)}, u32[]{:S(2)}) collective-permute-start(bf16[96,2]{1,0:T(8,128)(2,1)S(1)} %get-tuple-element.43), channel_id=1, source_target_pairs={{0,8},{8,16},{16,24},{24,32},{32,40},{40,48},{48,56},{56,64},{64,7... | collective-permute-start | bytes 1160 | tf_op jit(solution)/shard_map/ppermute | solution.py:29
  15.1 1.0 copy-start
  16.1 0.7 copy-start.4
  21.7 25.6 %copy-start.6 = (bf16[96,768]{1,0:T(8,128)(2,1)S(1)}, bf16[96,768]{1,0:T(8,128)(2,1)}, u32[]{:S(2)}) copy-start(bf16[96,768]{1,0:T(8,128)(2,1)} %param.6) | copy-start | bytes 442372
  45.4 5.3 %collective-permute-start.2 = (bf16[384,2048]{1,0:T(8,128)(2,1)S(1)}, bf16[384,2048]{1,0:T(8,128)(2,1)S(1)}, u32[]{:S(2)}, u32[]{:S(2)}) collective-permute-start(bf16[384,2048]{1,0:T(8,128)(2,1)S(1)} %bitcast.32), channel_id=1, source_target_pairs={{0,1},{1,0},{2,3},{3,2},{4,5},{5,4},{6,7},{7,6},{8,9},{9,8},{10,11... | collective-permute-start | bytes 4718600 | tf_op jit(solution)/shard_map/ppermute | solution.py:24
  47.6 1.1 copy-start.2
  50.7 24.9 %copy-start.3 = (f32[96,2048]{1,0:T(8,128)S(1)}, f32[96,2048]{1,0:T(8,128)}, u32[]{:S(2)}) copy-start(f32[96,2048]{1,0:T(8,128)} %targets.3) | copy-start | bytes 2359300
  76.8 5.3 %collective-permute-start.3 = (bf16[384,2048]{1,0:T(8,128)(2,1)S(1)}, bf16[384,2048]{1,0:T(8,128)(2,1)S(1)}, u32[]{:S(2)}, u32[]{:S(2)}) collective-permute-start(bf16[384,2048]{1,0:T(8,128)(2,1)S(1)} %get-tuple-element.27), channel_id=1, source_target_pairs={{0,1},{1,0},{2,3},{3,2},{4,5},{5,4},{6,7},{7,6},{8,9},{9,8},{10,11... | collective-permute-start | bytes 4718600 | tf_op jit(solution)/shard_map/ppermute | solution.py:24
  81.1 30.7 %copy-start.1 = (bf16[96,2048]{1,0:T(8,128)(2,1)S(1)}, bf16[96,2048]{1,0:T(8,128)(2,1)}, u32[]{:S(2)}) copy-start(bf16[96,2048]{1,0:T(8,128)(2,1)} %cells.5) | copy-start | bytes 1179652
  81.1 30.7 %copy-start.5 = (bf16[5,96]{1,0:T(8,128)(2,1)S(1)}, bf16[5,96]{1,0:T(8,128)(2,1)}, u32[]{:S(2)}) copy-start(bf16[5,96]{1,0:T(8,128)(2,1)} %tap.9) | copy-start | bytes 2884
  84.0 14.7 %all-to-all-start.2 = ((f32[4,24,768]{2,1,0:T(8,128)}), f32[4,24,768]{2,1,0:T(8,128)S(1)}, u32[]{:S(2)}, u32[]{:S(2)}) async-start(f32[4,24,768]{2,1,0:T(8,128)} %bitcast.11), calls=%async_computation.2 | async-start | bytes 589824 | tf_op jit(solution)/shard_map/all_to_all | solution.py:676
  88.9 15.6 %collective-permute-start.4 = (bf16[96,2048]{1,0:T(8,128)(2,1)}, bf16[96,2048]{1,0:T(8,128)(2,1)S(1)}, u32[]{:S(2)}, u32[]{:S(2)}) collective-permute-start(bf16[96,2048]{1,0:T(8,128)(2,1)} %get-tuple-element.33), channel_id=1, source_target_pairs={{0,4},{2,6},{4,0},{6,2},{1,5},{3,7},{5,1},{7,3},{8,12},{10,14},{12... | collective-permute-start | bytes 1179656 | tf_op jit(solution)/shard_map/ppermute | solution.py:20
  91.7 20.2 %collective-permute-start.5 = (bf16[96,2048]{1,0:T(8,128)(2,1)}, bf16[96,2048]{1,0:T(8,128)(2,1)S(1)}, u32[]{:S(2)}, u32[]{:S(2)}) collective-permute-start(bf16[96,2048]{1,0:T(8,128)(2,1)} %get-tuple-element.34), channel_id=1, source_target_pairs={{0,2},{2,4},{4,6},{6,0},{1,3},{3,5},{5,7},{7,1},{8,10},{10,12},{12... | collective-permute-start | bytes 1179656 | tf_op jit(solution)/shard_map/ppermute | solution.py:20
  94.8 17.1 %collective-permute-start.6 = (bf16[96,2048]{1,0:T(8,128)(2,1)S(1)}, bf16[96,2048]{1,0:T(8,128)(2,1)S(1)}, u32[]{:S(2)}, u32[]{:S(2)}) collective-permute-start(bf16[96,2048]{1,0:T(8,128)(2,1)S(1)} %get-tuple-element.35), channel_id=1, source_target_pairs={{0,6},{2,0},{4,2},{6,4},{1,7},{3,1},{5,3},{7,5},{8,14},{10,8},{12,... | collective-permute-start | bytes 1179656 | tf_op jit(solution)/shard_map/ppermute | solution.py:20
  99.4 16.3 %all-to-all-start.3 = ((f32[16,1,1152]{2,1,0:T(1,128)}), f32[16,1,1152]{2,1,0:T(1,128)S(1)}, u32[]{:S(2)}, u32[]{:S(2)}) async-start(f32[16,1,1152]{2,1,0:T(1,128)} %sum_to_rows.1), calls=%async_computation.3 | async-start | bytes 147456 | tf_op jit(solution)/shard_map/all_to_all | solution.py:678
  133.9 9.6 %all-to-all-start.5 = ((bf16[4,32,1152]{2,1,0:T(8,128)(2,1)}), bf16[4,32,1152]{2,1,0:T(8,128)(2,1)S(1)}, u32[]{:S(2)}, u32[]{:S(2)}) async-start(bf16[4,32,1152]{2,1,0:T(8,128)(2,1)} %onward.1), calls=%async_computation.5 | async-start | bytes 589824 | tf_op jit(solution)/shard_map/all_to_all | solution.py:684

commit v9 on v8

--- a/solution.py
+++ b/solution.py
@@ -63,14 +63,16 @@
             shift = (reach - k) % whole.shape[1]
             moved = pltpu.roll(whole, shift, 1) if shift else whole
             conv = conv + taps[:, k : k + 1] * moved[:, LANES : LANES + count]
-        hidden[at, :] = (conv * jax.nn.sigmoid(conv)).astype(BF16)
-
-
-def forward(cells, tap):
+        value = (conv * jax.nn.sigmoid(conv)).astype(BF16)
+        for chip in range(hidden.shape[0]):
+            hidden[chip, at, :] = value
+
+
+def forward(cells, tap, chips):
     rows, count = cells.shape
     return pl.pallas_call(
         forward_kernel,
-        out_shape=jax.ShapeDtypeStruct((rows, count), BF16),
+        out_shape=jax.ShapeDtypeStruct((chips, rows, count), BF16),
         scratch_shapes=[
             pltpu.VMEM((16, count + 2 * LANES), F32),
             pltpu.VMEM((8, LANES), F32),
@@ -107,9 +109,11 @@
             moved = pltpu.roll(whole, shift, 1) if shift else whole
             conv = conv + taps[:, k : k + 1] * moved[:, LANES : 2 * LANES]
         tiles[side] = (conv * jax.nn.sigmoid(conv)).astype(BF16)
-        spot = hidden.at[:, pl.ds(at, LANES)]
-        writes.append(pltpu.make_async_copy(tiles.at[side], spot, sems.at[side]))
-        writes[side].start()
+        for chip in range(hidden.shape[0]):
+            spot = hidden.at[chip, :, pl.ds(at, LANES)]
+            sem = sems.at[2 * chip + side]
+            writes.append(pltpu.make_async_copy(tiles.at[side], spot, sem))
+            writes[-1].start()
     for write in writes:
         write.wait()
 
@@ -128,7 +132,7 @@
             pltpu.VMEM((8, LANES), F32),
             pltpu.VMEM((LANES, 8), F32),
             pltpu.VMEM((2, width, LANES), BF16),
-            pltpu.SemaphoreType.DMA((2,)),
+            pltpu.SemaphoreType.DMA((2 * hidden.shape[0],)),
         ],
         compiler_params=pltpu.CompilerParams(vmem_limit_bytes=4 * 2**20),
         cost_estimate=pl.CostEstimate(
@@ -646,11 +650,9 @@
 
     place = jnp.stack([y, c])
     left, right = outer_columns(embeddings, reach)
-    block = with_rim(embeddings, left, right, taps, forward(embeddings, taps))
-
-    mine = lax.all_to_all(
-        jnp.broadcast_to(block[None], (ny, width, count)), "y", 0, 0, tiled=True
-    ).reshape(ny * width, count)
+    blocks = with_rim(embeddings, left, right, taps, forward(embeddings, taps, ny))
+
+    mine = lax.all_to_all(blocks, "y", 0, 0, tiled=True).reshape(ny * width, count)
     theirs = other_core(mine)
     weight = head_weight.T
     near, counts = near_logits(place, weight, mine, targets)

time: 147 us -> 147 us (level)
  no operation moved by 1% of the time
where the time goes in v9:
time: 147 us; the launch traced here: 146 us
  blocking collectives  62.9 us (43%)
  starting transfers between devices  40.4 us (27%)
  Pallas kernels  19.6 us (13%)
  waiting for transfers between devices  17.9 us (12%)
  local copies, waits for them, and re-layouts  3.91 us (3%)
    all_to_all x1, blocking collectives, shards(): lax.all_to_all(blocks, 'y', 0, 0, tiled=True).reshape(ny * width, count)  23.7 us
    all_to_all x1, blocking collectives, share(): return lax.all_to_all(copies, axes, 0, 0, tiled=True)[:, 0]  23.4 us
    all_to_all x1, blocking collectives, shards(): slab = lax.all_to_all(message, 'z', 0, 0, tiled=True)  15.8 us
    ppermute x1, starting transfers between devices, outer_columns(): lax.ppermute(cells[:, :width], SEQ, [(i + 1, i) for i in range(count - 1)])  11.7 us
    ppermute x3, starting transfers between devices, along_y(): lax.ppermute(value, 'y', [(i, (i + shift) % count) for i in range(count)])  9.77 us
    ppermute x3, waiting for transfers between devices, along_y(): lax.ppermute(value, 'y', [(i, (i + shift) % count) for i in range(count)])  8.81 us
    pallas_call x5, Pallas kernels, kernel_call(): pl.pallas_call(body, out_shape=outs, in_specs=[pl.BlockSpec(memory_space=...  7.88 us
    all_to_all x1, starting transfers between devices, shards(): lax.all_to_all(local.reshape(nx, tracks // nx, features), 'x', 0, 0, tile...  4.9 us
  transfers between devices with their start and end apart: 10, of which 7 were waited for; matrix products, arithmetic and copies ran while one was open for 0% of the time, Pallas kernels for 7%

profile of v9, /device:TPU:6, one launch (start us, length us, event | category | flops | bytes accessed | tf_op | source)
XLA Modules:
  0.0 145.7 jit_solution(10736882143004818035)
XLA Ops:
  1.5 11.7 %collective-permute-start.1 = (bf16[96,2]{1,0:T(8,128)(2,1)S(1)}, bf16[96,2]{1,0:T(8,128)(2,1)S(1)}, u32[]{:S(2)}, u32[]{:S(2)}) collective-permute-start(bf16[96,2]{1,0:T(8,128)(2,1)S(1)} %get-tuple-element.42), channel_id=1, source_target_pairs={{8,0},{16,8},{24,16},{32,24},{40,32},{48,40},{56,48},{64,56},{72,6... | collective-permute-start | bytes 1160 | tf_op jit(solution)/shard_map/ppermute | solution.py:30
  13.1 1.9 %collective-permute-start = (bf16[96,2]{1,0:T(8,128)(2,1)S(1)}, bf16[96,2]{1,0:T(8,128)(2,1)S(1)}, u32[]{:S(2)}, u32[]{:S(2)}) collective-permute-start(bf16[96,2]{1,0:T(8,128)(2,1)S(1)} %get-tuple-element.43), channel_id=1, source_target_pairs={{0,8},{8,16},{16,24},{24,32},{32,40},{40,48},{48,56},{56,64},{64,7... | collective-permute-start | bytes 1160 | tf_op jit(solution)/shard_map/ppermute | solution.py:29
  18.0 2.9 %collective-permute-done.left = bf16[96,2]{1,0:T(8,128)(2,1)S(1)} collective-permute-done((bf16[96,2]{1,0:T(8,128)(2,1)S(1)}, bf16[96,2]{1,0:T(8,128)(2,1)S(1)}, u32[]{:S(2)}, u32[]{:S(2)}) %collective-permute-start) | collective-permute-done | bytes 416 | tf_op jit(solution)/shard_map/ppermute | solution.py:29
  21.6 23.7 %all_to_all.30 = bf16[4,96,2048]{2,1,0:T(8,128)(2,1)S(1)} all-to-all(bf16[4,96,2048]{2,1,0:T(8,128)(2,1)S(1)} %outer_columns.1), channel_id=1, replica_groups=mesh['x'=4,'z'=16,'y'=4,'c'=2] {'y'}, dimensions={0} | all-to-all | bytes 3145728 | tf_op jit(solution)/shard_map/all_to_all | solution.py:655
  45.3 1.9 %collective-permute-start.2 = (bf16[384,2048]{1,0:T(8,128)(2,1)S(1)}, bf16[384,2048]{1,0:T(8,128)(2,1)S(1)}, u32[]{:S(2)}, u32[]{:S(2)}) collective-permute-start(bf16[384,2048]{1,0:T(8,128)(2,1)S(1)} %bitcast.32), channel_id=1, source_target_pairs={{0,1},{1,0},{2,3},{3,2},{4,5},{5,4},{6,7},{7,6},{8,9},{9,8},{10,11... | collective-permute-start | bytes 4718600 | tf_op jit(solution)/shard_map/ppermute | solution.py:24
  52.0 23.4 %all_to_all.31 = f32[64,1,384]{2,1,0:T(1,128)S(1)} all-to-all(f32[64,1,384]{2,1,0:T(1,128)S(1)} %broadcast_in_dim.21), channel_id=1, replica_groups=mesh['x'=4,'z'=16,'y'=4,'c'=2] {'x','z'}, dimensions={0} | all-to-all | bytes 196608 | tf_op jit(solution)/shard_map/all_to_all | solution.py:37
  76.7 1.9 %collective-permute-start.3 = (bf16[384,2048]{1,0:T(8,128)(2,1)S(1)}, bf16[384,2048]{1,0:T(8,128)(2,1)S(1)}, u32[]{:S(2)}, u32[]{:S(2)}) collective-permute-start(bf16[384,2048]{1,0:T(8,128)(2,1)S(1)} %get-tuple-element.27), channel_id=1, source_target_pairs={{0,1},{1,0},{2,3},{3,2},{4,5},{5,4},{6,7},{7,6},{8,9},{9,8},{10,11... | collective-permute-start | bytes 4718600 | tf_op jit(solution)/shard_map/ppermute | solution.py:24
  78.7 2.4 %weight_part.1 = f32[96,768]{1,0:T(8,128)} custom-call(s32[2]{0:T(128)S(1)} %pad_add_fusion.1.place, bf16[96,2048]{1,0:T(8,128)(2,1)S(1)} %get-tuple-element.26.grad, bf16[384,2048]{1,0:T(8,128)(2,1)S(1)} %bitcast.34, bf16[384,2048]{1,0:T(8,128)(2,1)S(1)} %collective-permute-done.2.hidden.theirs), custom_call_target="tpu_custom_call" | custom-call | flops 301989888 | bytes 3833856 | tf_op jit(solution)/shard_map/weight_part/pallas_call | solution.py:179
  82.0 1.9 %core_sum.1 = (f32[96,2048]{1,0:T(8,128)S(1)}, bf16[96,2048]{1,0:T(8,128)(2,1)}, bf16[96,2048]{1,0:T(8,128)(2,1)}, bf16[96,2048]{1,0:T(8,128)(2,1)S(1)}) custom-call(s32[2]{0:T(128)S(1)} %pad_add_fusion.1.place, bf16[768,96]{1,0:T(8,128)(2,1)S(1)} %bitcast.38, bf16[96,2048]{1,0:T(8,128)(2,1)S(1)} %get-tuple-element.26.grad, ...), custom_call_target="tpu_custom_call" | custom-call | flops 150994944 | bytes 4079616 | tf_op jit(solution)/shard_map/core_sum/pallas_call | solution.py:179
  83.9 4.9 %all-to-all-start.2 = ((f32[4,24,768]{2,1,0:T(8,128)}), f32[4,24,768]{2,1,0:T(8,128)S(1)}, u32[]{:S(2)}, u32[]{:S(2)}) async-start(f32[4,24,768]{2,1,0:T(8,128)} %bitcast.11), calls=%async_computation.2 | async-start | bytes 589824 | tf_op jit(solution)/shard_map/all_to_all | solution.py:678
  88.9 2.7 %collective-permute-start.4 = (bf16[96,2048]{1,0:T(8,128)(2,1)}, bf16[96,2048]{1,0:T(8,128)(2,1)S(1)}, u32[]{:S(2)}, u32[]{:S(2)}) collective-permute-start(bf16[96,2048]{1,0:T(8,128)(2,1)} %get-tuple-element.33), channel_id=1, source_target_pairs={{0,4},{2,6},{4,0},{6,2},{1,5},{3,7},{5,1},{7,3},{8,12},{10,14},{12... | collective-permute-start | bytes 1179656 | tf_op jit(solution)/shard_map/ppermute | solution.py:20
  91.6 3.1 %collective-permute-start.5 = (bf16[96,2048]{1,0:T(8,128)(2,1)}, bf16[96,2048]{1,0:T(8,128)(2,1)S(1)}, u32[]{:S(2)}, u32[]{:S(2)}) collective-permute-start(bf16[96,2048]{1,0:T(8,128)(2,1)} %get-tuple-element.34), channel_id=1, source_target_pairs={{0,2},{2,4},{4,6},{6,0},{1,3},{3,5},{5,7},{7,1},{8,10},{10,12},{12... | collective-permute-start | bytes 1179656 | tf_op jit(solution)/shard_map/ppermute | solution.py:20
  94.7 3.9 %collective-permute-start.6 = (bf16[96,2048]{1,0:T(8,128)(2,1)S(1)}, bf16[96,2048]{1,0:T(8,128)(2,1)S(1)}, u32[]{:S(2)}, u32[]{:S(2)}) collective-permute-start(bf16[96,2048]{1,0:T(8,128)(2,1)S(1)} %get-tuple-element.35), channel_id=1, source_target_pairs={{0,6},{2,0},{4,2},{6,4},{1,7},{3,1},{5,3},{7,5},{8,14},{10,8},{12,... | collective-permute-start | bytes 1179656 | tf_op jit(solution)/shard_map/ppermute | solution.py:20
  99.3 3.5 %all-to-all-start.3 = ((f32[16,1,1152]{2,1,0:T(1,128)}), f32[16,1,1152]{2,1,0:T(1,128)S(1)}, u32[]{:S(2)}, u32[]{:S(2)}) async-start(f32[16,1,1152]{2,1,0:T(1,128)} %sum_to_rows.1), calls=%async_computation.3 | async-start | bytes 147456 | tf_op jit(solution)/shard_map/all_to_all | solution.py:680
  102.9 1.6 %collective-permute-done.4.one = bf16[96,2048]{1,0:T(8,128)(2,1)S(1)} collective-permute-done((bf16[96,2048]{1,0:T(8,128)(2,1)}, bf16[96,2048]{1,0:T(8,128)(2,1)S(1)}, u32[]{:S(2)}, u32[]{:S(2)}) %collective-permute-start.4) | collective-permute-done | bytes 393248 | tf_op jit(solution)/shard_map/ppermute | solution.py:20
  104.5 7.3 %collective-permute-done.5.two = bf16[96,2048]{1,0:T(8,128)(2,1)S(1)} collective-permute-done((bf16[96,2048]{1,0:T(8,128)(2,1)}, bf16[96,2048]{1,0:T(8,128)(2,1)S(1)}, u32[]{:S(2)}, u32[]{:S(2)}) %collective-permute-start.5) | collective-permute-done | bytes 393248 | tf_op jit(solution)/shard_map/ppermute | solution.py:20
  111.8 2.5 %conv_grad.1 = (bf16[96,2048]{1,0:T(8,128)(2,1)S(1)}, f32[16,96]{1,0:T(8,128)S(1)}) custom-call(f32[96,2048]{1,0:T(8,128)S(1)} %get-tuple-element.32.mine, bf16[96,2048]{1,0:T(8,128)(2,1)S(1)} %collective-permute-done.4.one, bf16[96,2048]{1,0:T(8,128)(2,1)S(1)} %collective-permute-done.5.two, bf16[96,2048]{1,0:T(8,128)(2,1)S(1)} %collective-permute-done.6.three, ...), custom_call_target="tpu_custom_call" | custom-call | flops 7864320 | bytes 2752512 | tf_op jit(solution)/shard_map/conv_grad/pallas_call | solution.py:364
  114.3 1.3 all-to-all-done.3.slices
  116.5 15.8 %all_to_all.32.slab = bf16[16,2,1152]{2,1,0:T(2,128)(2,1)S(1)} all-to-all(bf16[16,2,1152]{2,1,0:T(2,128)(2,1)S(1)} %message.1), channel_id=1, replica_groups=mesh['x'=4,'z'=16,'y'=4,'c'=2] {'z'}, dimensions={0} | all-to-all | bytes 147456 | tf_op jit(solution)/shard_map/all_to_all | solution.py:685
  132.3 1.6 %onward.1 = bf16[4,32,1152]{2,1,0:T(8,128)(2,1)} custom-call(s32[3]{0:T(128)S(1)} %pad_add_fusion.place, bf16[16,2,1152]{2,1,0:T(2,128)(2,1)S(1)} %all_to_all.32.slab), custom_call_target="tpu_custom_call" | custom-call | flops 73728 | bytes 442368 | tf_op jit(solution)/shard_map/onward/pallas_call | solution.py:519
  133.8 4.8 %all-to-all-start.5 = ((bf16[4,32,1152]{2,1,0:T(8,128)(2,1)}), bf16[4,32,1152]{2,1,0:T(8,128)(2,1)S(1)}, u32[]{:S(2)}, u32[]{:S(2)}) async-start(bf16[4,32,1152]{2,1,0:T(8,128)(2,1)} %onward.1), calls=%async_computation.5 | async-start | bytes 589824 | tf_op jit(solution)/shard_map/all_to_all | solution.py:686
  138.6 1.9 %embed_grad.1 = (bf16[96,2048]{1,0:T(8,128)(2,1)}, f32[96,256]{1,0:T(8,128)S(1)}) custom-call(bf16[96,2048]{1,0:T(8,128)(2,1)S(1)} %get-tuple-element.37.grad, bf16[5,96]{1,0:T(8,128)(2,1)S(1)} %copy-done.5), custom_call_target="tpu_custom_call" | custom-call | flops 1966080 | bytes 786432 | tf_op jit(solution)/shard_map/embed_grad/pallas_call | solution.py:415
  140.5 2.9 %all-to-all-done.5.wide = bf16[4,32,1152]{2,1,0:T(8,128)(2,1)S(1)} async-done(((bf16[4,32,1152]{2,1,0:T(8,128)(2,1)}), bf16[4,32,1152]{2,1,0:T(8,128)(2,1)S(1)}, u32[]{:S(2)}, u32[]{:S(2)}) %all-to-all-start.5) | async-done | bytes 294944 | tf_op jit(solution)/shard_map/all_to_all | solution.py:686
  143.4 2.3 %finish.1 = (bf16[96,2048]{1,0:T(8,128)(2,1)}, f32[96,768]{1,0:T(8,128)}, f32[5,96]{1,0:T(8,128)}) custom-call(s32[3]{0:T(128)S(1)} %pad_add_fusion.place, bf16[16,2,1152]{2,1,0:T(2,128)(2,1)S(1)} %all_to_all.32.slab, bf16[4,32,1152]{2,1,0:T(8,128)(2,1)S(1)} %all-to-all-done.5.wide, ...), custom_call_target="tpu_custom_call", output_to_operand_aliasing={{0}: (5, {})} | custom-call | flops 36864 | bytes 294912 | tf_op jit(solution)/shard_map/finish/pallas_call | solution.py:608
  (37 shorter events, 13.0 us)
Async XLA Ops:
  1.5 16.6 %collective-permute-start.1 = (bf16[96,2]{1,0:T(8,128)(2,1)S(1)}, bf16[96,2]{1,0:T(8,128)(2,1)S(1)}, u32[]{:S(2)}, u32[]{:S(2)}) collective-permute-start(bf16[96,2]{1,0:T(8,128)(2,1)S(1)} %get-tuple-element.42), channel_id=1, source_target_pairs={{8,0},{16,8},{24,16},{32,24},{40,32},{48,40},{56,48},{64,56},{72,6... | collective-permute-start | bytes 1160 | tf_op jit(solution)/shard_map/ppermute | solution.py:30
  13.1 7.8 %collective-permute-start = (bf16[96,2]{1,0:T(8,128)(2,1)S(1)}, bf16[96,2]{1,0:T(8,128)(2,1)S(1)}, u32[]{:S(2)}, u32[]{:S(2)}) collective-permute-start(bf16[96,2]{1,0:T(8,128)(2,1)S(1)} %get-tuple-element.43), channel_id=1, source_target_pairs={{0,8},{8,16},{16,24},{24,32},{32,40},{40,48},{48,56},{56,64},{64,7... | collective-permute-start | bytes 1160 | tf_op jit(solution)/shard_map/ppermute | solution.py:29
  15.1 1.0 copy-start
  16.1 0.7 copy-start.4
  21.6 25.6 %copy-start.6 = (bf16[96,768]{1,0:T(8,128)(2,1)S(1)}, bf16[96,768]{1,0:T(8,128)(2,1)}, u32[]{:S(2)}) copy-start(bf16[96,768]{1,0:T(8,128)(2,1)} %param.6) | copy-start | bytes 442372
  45.3 5.3 %collective-permute-start.2 = (bf16[384,2048]{1,0:T(8,128)(2,1)S(1)}, bf16[384,2048]{1,0:T(8,128)(2,1)S(1)}, u32[]{:S(2)}, u32[]{:S(2)}) collective-permute-start(bf16[384,2048]{1,0:T(8,128)(2,1)S(1)} %bitcast.32), channel_id=1, source_target_pairs={{0,1},{1,0},{2,3},{3,2},{4,5},{5,4},{6,7},{7,6},{8,9},{9,8},{10,11... | collective-permute-start | bytes 4718600 | tf_op jit(solution)/shard_map/ppermute | solution.py:24
  47.5 1.1 copy-start.2
  50.6 24.9 %copy-start.3 = (f32[96,2048]{1,0:T(8,128)S(1)}, f32[96,2048]{1,0:T(8,128)}, u32[]{:S(2)}) copy-start(f32[96,2048]{1,0:T(8,128)} %targets.3) | copy-start | bytes 2359300
  76.7 5.3 %collective-permute-start.3 = (bf16[384,2048]{1,0:T(8,128)(2,1)S(1)}, bf16[384,2048]{1,0:T(8,128)(2,1)S(1)}, u32[]{:S(2)}, u32[]{:S(2)}) collective-permute-start(bf16[384,2048]{1,0:T(8,128)(2,1)S(1)} %get-tuple-element.27), channel_id=1, source_target_pairs={{0,1},{1,0},{2,3},{3,2},{4,5},{5,4},{6,7},{7,6},{8,9},{9,8},{10,11... | collective-permute-start | bytes 4718600 | tf_op jit(solution)/shard_map/ppermute | solution.py:24
  81.1 30.7 %copy-start.1 = (bf16[96,2048]{1,0:T(8,128)(2,1)S(1)}, bf16[96,2048]{1,0:T(8,128)(2,1)}, u32[]{:S(2)}) copy-start(bf16[96,2048]{1,0:T(8,128)(2,1)} %cells.5) | copy-start | bytes 1179652
  81.1 30.7 %copy-start.5 = (bf16[5,96]{1,0:T(8,128)(2,1)S(1)}, bf16[5,96]{1,0:T(8,128)(2,1)}, u32[]{:S(2)}) copy-start(bf16[5,96]{1,0:T(8,128)(2,1)} %tap.9) | copy-start | bytes 2884
  83.9 14.7 %all-to-all-start.2 = ((f32[4,24,768]{2,1,0:T(8,128)}), f32[4,24,768]{2,1,0:T(8,128)S(1)}, u32[]{:S(2)}, u32[]{:S(2)}) async-start(f32[4,24,768]{2,1,0:T(8,128)} %bitcast.11), calls=%async_computation.2 | async-start | bytes 589824 | tf_op jit(solution)/shard_map/all_to_all | solution.py:678
  88.9 15.6 %collective-permute-start.4 = (bf16[96,2048]{1,0:T(8,128)(2,1)}, bf16[96,2048]{1,0:T(8,128)(2,1)S(1)}, u32[]{:S(2)}, u32[]{:S(2)}) collective-permute-start(bf16[96,2048]{1,0:T(8,128)(2,1)} %get-tuple-element.33), channel_id=1, source_target_pairs={{0,4},{2,6},{4,0},{6,2},{1,5},{3,7},{5,1},{7,3},{8,12},{10,14},{12... | collective-permute-start | bytes 1179656 | tf_op jit(solution)/shard_map/ppermute | solution.py:20
  91.6 20.2 %collective-permute-start.5 = (bf16[96,2048]{1,0:T(8,128)(2,1)}, bf16[96,2048]{1,0:T(8,128)(2,1)S(1)}, u32[]{:S(2)}, u32[]{:S(2)}) collective-permute-start(bf16[96,2048]{1,0:T(8,128)(2,1)} %get-tuple-element.34), channel_id=1, source_target_pairs={{0,2},{2,4},{4,6},{6,0},{1,3},{3,5},{5,7},{7,1},{8,10},{10,12},{12... | collective-permute-start | bytes 1179656 | tf_op jit(solution)/shard_map/ppermute | solution.py:20
  94.7 17.0 %collective-permute-start.6 = (bf16[96,2048]{1,0:T(8,128)(2,1)S(1)}, bf16[96,2048]{1,0:T(8,128)(2,1)S(1)}, u32[]{:S(2)}, u32[]{:S(2)}) collective-permute-start(bf16[96,2048]{1,0:T(8,128)(2,1)S(1)} %get-tuple-element.35), channel_id=1, source_target_pairs={{0,6},{2,0},{4,2},{6,4},{1,7},{3,1},{5,3},{7,5},{8,14},{10,8},{12,... | collective-permute-start | bytes 1179656 | tf_op jit(solution)/shard_map/ppermute | solution.py:20
  99.3 16.3 %all-to-all-start.3 = ((f32[16,1,1152]{2,1,0:T(1,128)}), f32[16,1,1152]{2,1,0:T(1,128)S(1)}, u32[]{:S(2)}, u32[]{:S(2)}) async-start(f32[16,1,1152]{2,1,0:T(1,128)} %sum_to_rows.1), calls=%async_computation.3 | async-start | bytes 147456 | tf_op jit(solution)/shard_map/all_to_all | solution.py:680
  133.8 9.6 %all-to-all-start.5 = ((bf16[4,32,1152]{2,1,0:T(8,128)(2,1)}), bf16[4,32,1152]{2,1,0:T(8,128)(2,1)S(1)}, u32[]{:S(2)}, u32[]{:S(2)}) async-start(bf16[4,32,1152]{2,1,0:T(8,128)(2,1)} %onward.1), calls=%async_computation.5 | async-start | bytes 589824 | tf_op jit(solution)/shard_map/all_to_all | solution.py:686

commit v10 on v9

--- a/solution.py
+++ b/solution.py
@@ -52,7 +52,7 @@
     line[:, :LANES] = jnp.zeros((rows, LANES), F32)
     line[:, LANES + count :] = jnp.zeros((rows, LANES), F32)
 
-    @pl.loop(0, cells.shape[0] // rows)
+    @pl.loop(0, cells.shape[0] // rows, unroll=2)
     def _(block):
         at = pl.ds(pl.multiple_of(block * rows, rows), rows)
         line[:, LANES : LANES + count] = cells[at, :].astype(F32)
@@ -326,7 +326,7 @@
     for copy in copies:
         copy.wait()
 
-    @pl.loop(0, cells.shape[0] // rows)
+    @pl.loop(0, cells.shape[0] // rows, unroll=2)
     def _(block):
         at = pl.ds(pl.multiple_of(block * rows, rows), rows)
         line[:, LANES - reach : LANES] = sides[0, at, :].astype(F32)

time: 147 us -> 147 us (level)
  transfers between devices with their start and end apart: 10 -> 10, of which waited for: 7 -> 7; matrix products, arithmetic and copies ran while one was open for 0% -> 0% of each run, Pallas kernels for 7% -> 6%
where the time goes in v10:
time: 147 us; the launch traced here: 146 us
  blocking collectives  62.7 us (43%)
  starting transfers between devices  40.4 us (27%)
  Pallas kernels  19.1 us (13%)
  waiting for transfers between devices  18.4 us (13%)
  local copies, waits for them, and re-layouts  3.91 us (3%)
    all_to_all x1, blocking collectives, shards(): lax.all_to_all(blocks, 'y', 0, 0, tiled=True).reshape(ny * width, count)  23.7 us
    all_to_all x1, blocking collectives, share(): return lax.all_to_all(copies, axes, 0, 0, tiled=True)[:, 0]  23.2 us
    all_to_all x1, blocking collectives, shards(): slab = lax.all_to_all(message, 'z', 0, 0, tiled=True)  15.8 us
    ppermute x1, starting transfers between devices, outer_columns(): lax.ppermute(cells[:, :width], SEQ, [(i + 1, i) for i in range(count - 1)])  11.7 us
    ppermute x3, starting transfers between devices, along_y(): lax.ppermute(value, 'y', [(i, (i + shift) % count) for i in range(count)])  9.77 us
    ppermute x3, waiting for transfers between devices, along_y(): lax.ppermute(value, 'y', [(i, (i + shift) % count) for i in range(count)])  8.81 us
    pallas_call x5, Pallas kernels, kernel_call(): pl.pallas_call(body, out_shape=outs, in_specs=[pl.BlockSpec(memory_space=...  7.88 us
    all_to_all x1, starting transfers between devices, shards(): lax.all_to_all(local.reshape(nx, tracks // nx, features), 'x', 0, 0, tile...  4.9 us
  transfers between devices with their start and end apart: 10, of which 7 were waited for; matrix products, arithmetic and copies ran while one was open for 0% of the time, Pallas kernels for 6%

profile of v10, /device:TPU:6, one launch (start us, length us, event | category | flops | bytes accessed | tf_op | source)
XLA Modules:
  0.0 145.5 jit_solution(4418126952759451113)
XLA Ops:
  1.5 11.7 %collective-permute-start.1 = (bf16[96,2]{1,0:T(8,128)(2,1)S(1)}, bf16[96,2]{1,0:T(8,128)(2,1)S(1)}, u32[]{:S(2)}, u32[]{:S(2)}) collective-permute-start(bf16[96,2]{1,0:T(8,128)(2,1)S(1)} %get-tuple-element.42), channel_id=1, source_target_pairs={{8,0},{16,8},{24,16},{32,24},{40,32},{48,40},{56,48},{64,56},{72,6... | collective-permute-start | bytes 1160 | tf_op jit(solution)/shard_map/ppermute | solution.py:30
  13.1 1.9 %collective-permute-start = (bf16[96,2]{1,0:T(8,128)(2,1)S(1)}, bf16[96,2]{1,0:T(8,128)(2,1)S(1)}, u32[]{:S(2)}, u32[]{:S(2)}) collective-permute-start(bf16[96,2]{1,0:T(8,128)(2,1)S(1)} %get-tuple-element.43), channel_id=1, source_target_pairs={{0,8},{8,16},{16,24},{24,32},{32,40},{40,48},{48,56},{56,64},{64,7... | collective-permute-start | bytes 1160 | tf_op jit(solution)/shard_map/ppermute | solution.py:29
  17.8 3.1 %collective-permute-done.left = bf16[96,2]{1,0:T(8,128)(2,1)S(1)} collective-permute-done((bf16[96,2]{1,0:T(8,128)(2,1)S(1)}, bf16[96,2]{1,0:T(8,128)(2,1)S(1)}, u32[]{:S(2)}, u32[]{:S(2)}) %collective-permute-start) | collective-permute-done | bytes 416 | tf_op jit(solution)/shard_map/ppermute | solution.py:29
  21.6 23.7 %all_to_all.30 = bf16[4,96,2048]{2,1,0:T(8,128)(2,1)S(1)} all-to-all(bf16[4,96,2048]{2,1,0:T(8,128)(2,1)S(1)} %outer_columns.1), channel_id=1, replica_groups=mesh['x'=4,'z'=16,'y'=4,'c'=2] {'y'}, dimensions={0} | all-to-all | bytes 3145728 | tf_op jit(solution)/shard_map/all_to_all | solution.py:655
  45.3 1.9 %collective-permute-start.2 = (bf16[384,2048]{1,0:T(8,128)(2,1)S(1)}, bf16[384,2048]{1,0:T(8,128)(2,1)S(1)}, u32[]{:S(2)}, u32[]{:S(2)}) collective-permute-start(bf16[384,2048]{1,0:T(8,128)(2,1)S(1)} %bitcast.32), channel_id=1, source_target_pairs={{0,1},{1,0},{2,3},{3,2},{4,5},{5,4},{6,7},{7,6},{8,9},{9,8},{10,11... | collective-permute-start | bytes 4718600 | tf_op jit(solution)/shard_map/ppermute | solution.py:24
  52.0 23.2 %all_to_all.31 = f32[64,1,384]{2,1,0:T(1,128)S(1)} all-to-all(f32[64,1,384]{2,1,0:T(1,128)S(1)} %broadcast_in_dim.21), channel_id=1, replica_groups=mesh['x'=4,'z'=16,'y'=4,'c'=2] {'x','z'}, dimensions={0} | all-to-all | bytes 196608 | tf_op jit(solution)/shard_map/all_to_all | solution.py:37
  76.5 1.9 %collective-permute-start.3 = (bf16[384,2048]{1,0:T(8,128)(2,1)S(1)}, bf16[384,2048]{1,0:T(8,128)(2,1)S(1)}, u32[]{:S(2)}, u32[]{:S(2)}) collective-permute-start(bf16[384,2048]{1,0:T(8,128)(2,1)S(1)} %get-tuple-element.27), channel_id=1, source_target_pairs={{0,1},{1,0},{2,3},{3,2},{4,5},{5,4},{6,7},{7,6},{8,9},{9,8},{10,11... | collective-permute-start | bytes 4718600 | tf_op jit(solution)/shard_map/ppermute | solution.py:24
  78.5 2.4 %weight_part.1 = f32[96,768]{1,0:T(8,128)} custom-call(s32[2]{0:T(128)S(1)} %pad_add_fusion.1.place, bf16[96,2048]{1,0:T(8,128)(2,1)S(1)} %get-tuple-element.26.grad, bf16[384,2048]{1,0:T(8,128)(2,1)S(1)} %bitcast.34, bf16[384,2048]{1,0:T(8,128)(2,1)S(1)} %collective-permute-done.2.hidden.theirs), custom_call_target="tpu_custom_call" | custom-call | flops 301989888 | bytes 3833856 | tf_op jit(solution)/shard_map/weight_part/pallas_call | solution.py:179
  81.8 1.9 %core_sum.1 = (f32[96,2048]{1,0:T(8,128)S(1)}, bf16[96,2048]{1,0:T(8,128)(2,1)}, bf16[96,2048]{1,0:T(8,128)(2,1)}, bf16[96,2048]{1,0:T(8,128)(2,1)S(1)}) custom-call(s32[2]{0:T(128)S(1)} %pad_add_fusion.1.place, bf16[768,96]{1,0:T(8,128)(2,1)S(1)} %bitcast.38, bf16[96,2048]{1,0:T(8,128)(2,1)S(1)} %get-tuple-element.26.grad, ...), custom_call_target="tpu_custom_call" | custom-call | flops 150994944 | bytes 4079616 | tf_op jit(solution)/shard_map/core_sum/pallas_call | solution.py:179
  83.7 4.9 %all-to-all-start.2 = ((f32[4,24,768]{2,1,0:T(8,128)}), f32[4,24,768]{2,1,0:T(8,128)S(1)}, u32[]{:S(2)}, u32[]{:S(2)}) async-start(f32[4,24,768]{2,1,0:T(8,128)} %bitcast.11), calls=%async_computation.2 | async-start | bytes 589824 | tf_op jit(solution)/shard_map/all_to_all | solution.py:678
  88.6 2.7 %collective-permute-start.4 = (bf16[96,2048]{1,0:T(8,128)(2,1)}, bf16[96,2048]{1,0:T(8,128)(2,1)S(1)}, u32[]{:S(2)}, u32[]{:S(2)}) collective-permute-start(bf16[96,2048]{1,0:T(8,128)(2,1)} %get-tuple-element.33), channel_id=1, source_target_pairs={{0,4},{2,6},{4,0},{6,2},{1,5},{3,7},{5,1},{7,3},{8,12},{10,14},{12... | collective-permute-start | bytes 1179656 | tf_op jit(solution)/shard_map/ppermute | solution.py:20
  91.4 3.1 %collective-permute-start.5 = (bf16[96,2048]{1,0:T(8,128)(2,1)}, bf16[96,2048]{1,0:T(8,128)(2,1)S(1)}, u32[]{:S(2)}, u32[]{:S(2)}) collective-permute-start(bf16[96,2048]{1,0:T(8,128)(2,1)} %get-tuple-element.34), channel_id=1, source_target_pairs={{0,2},{2,4},{4,6},{6,0},{1,3},{3,5},{5,7},{7,1},{8,10},{10,12},{12... | collective-permute-start | bytes 1179656 | tf_op jit(solution)/shard_map/ppermute | solution.py:20
  94.5 3.9 %collective-permute-start.6 = (bf16[96,2048]{1,0:T(8,128)(2,1)S(1)}, bf16[96,2048]{1,0:T(8,128)(2,1)S(1)}, u32[]{:S(2)}, u32[]{:S(2)}) collective-permute-start(bf16[96,2048]{1,0:T(8,128)(2,1)S(1)} %get-tuple-element.35), channel_id=1, source_target_pairs={{0,6},{2,0},{4,2},{6,4},{1,7},{3,1},{5,3},{7,5},{8,14},{10,8},{12,... | collective-permute-start | bytes 1179656 | tf_op jit(solution)/shard_map/ppermute | solution.py:20
  99.1 3.5 %all-to-all-start.3 = ((f32[16,1,1152]{2,1,0:T(1,128)}), f32[16,1,1152]{2,1,0:T(1,128)S(1)}, u32[]{:S(2)}, u32[]{:S(2)}) async-start(f32[16,1,1152]{2,1,0:T(1,128)} %sum_to_rows.1), calls=%async_computation.3 | async-start | bytes 147456 | tf_op jit(solution)/shard_map/all_to_all | solution.py:680
  102.7 1.6 %collective-permute-done.4.one = bf16[96,2048]{1,0:T(8,128)(2,1)S(1)} collective-permute-done((bf16[96,2048]{1,0:T(8,128)(2,1)}, bf16[96,2048]{1,0:T(8,128)(2,1)S(1)}, u32[]{:S(2)}, u32[]{:S(2)}) %collective-permute-start.4) | collective-permute-done | bytes 393248 | tf_op jit(solution)/shard_map/ppermute | solution.py:20
  104.3 7.3 %collective-permute-done.5.two = bf16[96,2048]{1,0:T(8,128)(2,1)S(1)} collective-permute-done((bf16[96,2048]{1,0:T(8,128)(2,1)}, bf16[96,2048]{1,0:T(8,128)(2,1)S(1)}, u32[]{:S(2)}, u32[]{:S(2)}) %collective-permute-start.5) | collective-permute-done | bytes 393248 | tf_op jit(solution)/shard_map/ppermute | solution.py:20
  111.6 2.2 %conv_grad.1 = (bf16[96,2048]{1,0:T(8,128)(2,1)S(1)}, f32[16,96]{1,0:T(8,128)S(1)}) custom-call(f32[96,2048]{1,0:T(8,128)S(1)} %get-tuple-element.32.mine, bf16[96,2048]{1,0:T(8,128)(2,1)S(1)} %collective-permute-done.4.one, bf16[96,2048]{1,0:T(8,128)(2,1)S(1)} %collective-permute-done.5.two, bf16[96,2048]{1,0:T(8,128)(2,1)S(1)} %collective-permute-done.6.three, ...), custom_call_target="tpu_custom_call" | custom-call | flops 7864320 | bytes 2752512 | tf_op jit(solution)/shard_map/conv_grad/pallas_call | solution.py:364
  113.8 1.7 %all-to-all-done.3.slices = f32[16,1,1152]{2,1,0:T(1,128)S(1)} async-done(((f32[16,1,1152]{2,1,0:T(1,128)}), f32[16,1,1152]{2,1,0:T(1,128)S(1)}, u32[]{:S(2)}, u32[]{:S(2)}) %all-to-all-start.3) | async-done | bytes 73760 | tf_op jit(solution)/shard_map/all_to_all | solution.py:680
  116.3 15.8 %all_to_all.32.slab = bf16[16,2,1152]{2,1,0:T(2,128)(2,1)S(1)} all-to-all(bf16[16,2,1152]{2,1,0:T(2,128)(2,1)S(1)} %message.1), channel_id=1, replica_groups=mesh['x'=4,'z'=16,'y'=4,'c'=2] {'z'}, dimensions={0} | all-to-all | bytes 147456 | tf_op jit(solution)/shard_map/all_to_all | solution.py:685
  132.0 1.6 %onward.1 = bf16[4,32,1152]{2,1,0:T(8,128)(2,1)} custom-call(s32[3]{0:T(128)S(1)} %pad_add_fusion.place, bf16[16,2,1152]{2,1,0:T(2,128)(2,1)S(1)} %all_to_all.32.slab), custom_call_target="tpu_custom_call" | custom-call | flops 73728 | bytes 442368 | tf_op jit(solution)/shard_map/onward/pallas_call | solution.py:519
  133.6 4.8 %all-to-all-start.5 = ((bf16[4,32,1152]{2,1,0:T(8,128)(2,1)}), bf16[4,32,1152]{2,1,0:T(8,128)(2,1)S(1)}, u32[]{:S(2)}, u32[]{:S(2)}) async-start(bf16[4,32,1152]{2,1,0:T(8,128)(2,1)} %onward.1), calls=%async_computation.5 | async-start | bytes 589824 | tf_op jit(solution)/shard_map/all_to_all | solution.py:686
  138.4 1.9 %embed_grad.1 = (bf16[96,2048]{1,0:T(8,128)(2,1)}, f32[96,256]{1,0:T(8,128)S(1)}) custom-call(bf16[96,2048]{1,0:T(8,128)(2,1)S(1)} %get-tuple-element.37.grad, bf16[5,96]{1,0:T(8,128)(2,1)S(1)} %copy-done.5), custom_call_target="tpu_custom_call" | custom-call | flops 1966080 | bytes 786432 | tf_op jit(solution)/shard_map/embed_grad/pallas_call | solution.py:415
  140.3 2.9 %all-to-all-done.5.wide = bf16[4,32,1152]{2,1,0:T(8,128)(2,1)S(1)} async-done(((bf16[4,32,1152]{2,1,0:T(8,128)(2,1)}), bf16[4,32,1152]{2,1,0:T(8,128)(2,1)S(1)}, u32[]{:S(2)}, u32[]{:S(2)}) %all-to-all-start.5) | async-done | bytes 294944 | tf_op jit(solution)/shard_map/all_to_all | solution.py:686
  143.2 2.3 %finish.1 = (bf16[96,2048]{1,0:T(8,128)(2,1)}, f32[96,768]{1,0:T(8,128)}, f32[5,96]{1,0:T(8,128)}) custom-call(s32[3]{0:T(128)S(1)} %pad_add_fusion.place, bf16[16,2,1152]{2,1,0:T(2,128)(2,1)S(1)} %all_to_all.32.slab, bf16[4,32,1152]{2,1,0:T(8,128)(2,1)S(1)} %all-to-all-done.5.wide, ...), custom_call_target="tpu_custom_call", output_to_operand_aliasing={{0}: (5, {})} | custom-call | flops 36864 | bytes 294912 | tf_op jit(solution)/shard_map/finish/pallas_call | solution.py:608
  (37 shorter events, 12.8 us)
Async XLA Ops:
  1.5 16.4 %collective-permute-start.1 = (bf16[96,2]{1,0:T(8,128)(2,1)S(1)}, bf16[96,2]{1,0:T(8,128)(2,1)S(1)}, u32[]{:S(2)}, u32[]{:S(2)}) collective-permute-start(bf16[96,2]{1,0:T(8,128)(2,1)S(1)} %get-tuple-element.42), channel_id=1, source_target_pairs={{8,0},{16,8},{24,16},{32,24},{40,32},{48,40},{56,48},{64,56},{72,6... | collective-permute-start | bytes 1160 | tf_op jit(solution)/shard_map/ppermute | solution.py:30
  13.1 7.8 %collective-permute-start = (bf16[96,2]{1,0:T(8,128)(2,1)S(1)}, bf16[96,2]{1,0:T(8,128)(2,1)S(1)}, u32[]{:S(2)}, u32[]{:S(2)}) collective-permute-start(bf16[96,2]{1,0:T(8,128)(2,1)S(1)} %get-tuple-element.43), channel_id=1, source_target_pairs={{0,8},{8,16},{16,24},{24,32},{32,40},{40,48},{48,56},{56,64},{64,7... | collective-permute-start | bytes 1160 | tf_op jit(solution)/shard_map/ppermute | solution.py:29
  15.1 1.0 copy-start
  16.1 0.7 copy-start.4
  21.6 25.6 %copy-start.6 = (bf16[96,768]{1,0:T(8,128)(2,1)S(1)}, bf16[96,768]{1,0:T(8,128)(2,1)}, u32[]{:S(2)}) copy-start(bf16[96,768]{1,0:T(8,128)(2,1)} %param.6) | copy-start | bytes 442372
  45.3 5.3 %collective-permute-start.2 = (bf16[384,2048]{1,0:T(8,128)(2,1)S(1)}, bf16[384,2048]{1,0:T(8,128)(2,1)S(1)}, u32[]{:S(2)}, u32[]{:S(2)}) collective-permute-start(bf16[384,2048]{1,0:T(8,128)(2,1)S(1)} %bitcast.32), channel_id=1, source_target_pairs={{0,1},{1,0},{2,3},{3,2},{4,5},{5,4},{6,7},{7,6},{8,9},{9,8},{10,11... | collective-permute-start | bytes 4718600 | tf_op jit(solution)/shard_map/ppermute | solution.py:24
  47.5 1.1 copy-start.2
  50.6 24.7 %copy-start.3 = (f32[96,2048]{1,0:T(8,128)S(1)}, f32[96,2048]{1,0:T(8,128)}, u32[]{:S(2)}) copy-start(f32[96,2048]{1,0:T(8,128)} %targets.3) | copy-start | bytes 2359300
  76.5 5.3 %collective-permute-start.3 = (bf16[384,2048]{1,0:T(8,128)(2,1)S(1)}, bf16[384,2048]{1,0:T(8,128)(2,1)S(1)}, u32[]{:S(2)}, u32[]{:S(2)}) collective-permute-start(bf16[384,2048]{1,0:T(8,128)(2,1)S(1)} %get-tuple-element.27), channel_id=1, source_target_pairs={{0,1},{1,0},{2,3},{3,2},{4,5},{5,4},{6,7},{7,6},{8,9},{9,8},{10,11... | collective-permute-start | bytes 4718600 | tf_op jit(solution)/shard_map/ppermute | solution.py:24
  80.9 30.7 %copy-start.1 = (bf16[96,2048]{1,0:T(8,128)(2,1)S(1)}, bf16[96,2048]{1,0:T(8,128)(2,1)}, u32[]{:S(2)}) copy-start(bf16[96,2048]{1,0:T(8,128)(2,1)} %cells.5) | copy-start | bytes 1179652
  80.9 30.7 %copy-start.5 = (bf16[5,96]{1,0:T(8,128)(2,1)S(1)}, bf16[5,96]{1,0:T(8,128)(2,1)}, u32[]{:S(2)}) copy-start(bf16[5,96]{1,0:T(8,128)(2,1)} %tap.9) | copy-start | bytes 2884
  83.7 14.7 %all-to-all-start.2 = ((f32[4,24,768]{2,1,0:T(8,128)}), f32[4,24,768]{2,1,0:T(8,128)S(1)}, u32[]{:S(2)}, u32[]{:S(2)}) async-start(f32[4,24,768]{2,1,0:T(8,128)} %bitcast.11), calls=%async_computation.2 | async-start | bytes 589824 | tf_op jit(solution)/shard_map/all_to_all | solution.py:678
  88.6 15.6 %collective-permute-start.4 = (bf16[96,2048]{1,0:T(8,128)(2,1)}, bf16[96,2048]{1,0:T(8,128)(2,1)S(1)}, u32[]{:S(2)}, u32[]{:S(2)}) collective-permute-start(bf16[96,2048]{1,0:T(8,128)(2,1)} %get-tuple-element.33), channel_id=1, source_target_pairs={{0,4},{2,6},{4,0},{6,2},{1,5},{3,7},{5,1},{7,3},{8,12},{10,14},{12... | collective-permute-start | bytes 1179656 | tf_op jit(solution)/shard_map/ppermute | solution.py:20
  91.4 20.2 %collective-permute-start.5 = (bf16[96,2048]{1,0:T(8,128)(2,1)}, bf16[96,2048]{1,0:T(8,128)(2,1)S(1)}, u32[]{:S(2)}, u32[]{:S(2)}) collective-permute-start(bf16[96,2048]{1,0:T(8,128)(2,1)} %get-tuple-element.34), channel_id=1, source_target_pairs={{0,2},{2,4},{4,6},{6,0},{1,3},{3,5},{5,7},{7,1},{8,10},{10,12},{12... | collective-permute-start | bytes 1179656 | tf_op jit(solution)/shard_map/ppermute | solution.py:20
  94.5 17.0 %collective-permute-start.6 = (bf16[96,2048]{1,0:T(8,128)(2,1)S(1)}, bf16[96,2048]{1,0:T(8,128)(2,1)S(1)}, u32[]{:S(2)}, u32[]{:S(2)}) collective-permute-start(bf16[96,2048]{1,0:T(8,128)(2,1)S(1)} %get-tuple-element.35), channel_id=1, source_target_pairs={{0,6},{2,0},{4,2},{6,4},{1,7},{3,1},{5,3},{7,5},{8,14},{10,8},{12,... | collective-permute-start | bytes 1179656 | tf_op jit(solution)/shard_map/ppermute | solution.py:20
  99.1 16.3 %all-to-all-start.3 = ((f32[16,1,1152]{2,1,0:T(1,128)}), f32[16,1,1152]{2,1,0:T(1,128)S(1)}, u32[]{:S(2)}, u32[]{:S(2)}) async-start(f32[16,1,1152]{2,1,0:T(1,128)} %sum_to_rows.1), calls=%async_computation.3 | async-start | bytes 147456 | tf_op jit(solution)/shard_map/all_to_all | solution.py:680
  133.6 9.6 %all-to-all-start.5 = ((bf16[4,32,1152]{2,1,0:T(8,128)(2,1)}), bf16[4,32,1152]{2,1,0:T(8,128)(2,1)S(1)}, u32[]{:S(2)}, u32[]{:S(2)}) async-start(bf16[4,32,1152]{2,1,0:T(8,128)(2,1)} %onward.1), calls=%async_computation.5 | async-start | bytes 589824 | tf_op jit(solution)/shard_map/all_to_all | solution.py:686
